TPU v7x, 32 devices: a whole 2x2x4 slice. The times are simulated.
32 devices in a mesh: seq: 2 (over y), blk: 4 (over z), uly: 4 (over x, core).
Axes of the slice: x: 2, y: 2, z: 4, core: 2. Of those that a mesh axis runs over, the one named last changes fastest.
Arguments:
- inputs: bfloat16 [8, 1024, 2048], P('seq', ('blk', 'uly')), may hold values from -6 to 6
- doc_lengths: int32 [8, 3], P('seq'), may hold values from 1 to 896, 1024 in all within a row
- ln1_gain: bfloat16 [2048], P(('seq', 'blk', 'uly')), may hold values from 0.099609375 to 1.8984375
- ln1_shift: bfloat16 [2048], P(('seq', 'blk', 'uly')), may hold values from -1.5 to 1.5
- w_query: bfloat16 [2048, 2048], P(('seq', 'blk', 'uly')), may hold values from -0.125 to 0.125
- b_query: bfloat16 [2048], P(('seq', 'blk', 'uly')), may hold values from -1.5 to 1.5
- w_key: bfloat16 [2048, 2048], P(('seq', 'blk', 'uly')), may hold values from -0.125 to 0.125
- w_value: bfloat16 [2048, 2048], P(('seq', 'blk', 'uly')), may hold values from -0.125 to 0.125
- b_value: bfloat16 [2048], P(('seq', 'blk', 'uly')), may hold values from -1.5 to 1.5
- w_out: bfloat16 [2048, 2048], P(('seq', 'blk', 'uly')), may hold values from -1.5 to 1.5
- b_out: bfloat16 [2048], P(('seq', 'blk', 'uly')), may hold values from -1.5 to 1.5
- ln2_gain: bfloat16 [2048], P(('seq', 'blk', 'uly')), may hold values from 0.099609375 to 1.8984375
- ln2_shift: bfloat16 [2048], P(('seq', 'blk', 'uly')), may hold values from -1.5 to 1.5
- w_fc: bfloat16 [2048, 8192], P(('seq', 'blk', 'uly')), may hold values from -0.125 to 0.125
- b_fc: bfloat16 [8192], P(('seq', 'blk', 'uly')), may hold values from -1.5 to 1.5
- w_proj: bfloat16 [8192, 2048], P(('seq', 'blk', 'uly')), may hold values from -0.0625 to 0.0625
- b_proj: bfloat16 [2048], P(('seq', 'blk', 'uly')), may hold values from -1.5 to 1.5
- cotangent: bfloat16 [8, 1024, 2048], P('seq', ('blk', 'uly')), may hold values from -6 to 6
Outputs:
- output: bfloat16 [8, 1024, 2048], P('seq', ('blk', 'uly'))
- grad_inputs: bfloat16 [8, 1024, 2048], P('seq', ('blk', 'uly'))
- grad_ln1_gain: float32 [2048], P(('seq', 'blk', 'uly'))
- grad_ln1_shift: float32 [2048], P(('seq', 'blk', 'uly'))
- grad_w_query: float32 [2048, 2048], P(('seq', 'blk', 'uly'))
- grad_b_query: float32 [2048], P(('seq', 'blk', 'uly'))
- grad_w_key: float32 [2048, 2048], P(('seq', 'blk', 'uly'))
- grad_w_value: float32 [2048, 2048], P(('seq', 'blk', 'uly'))
- grad_b_value: float32 [2048], P(('seq', 'blk', 'uly'))
- grad_w_out: float32 [2048, 2048], P(('seq', 'blk', 'uly'))
- grad_b_out: float32 [2048], P(('seq', 'blk', 'uly'))
- grad_ln2_gain: float32 [2048], P(('seq', 'blk', 'uly'))
- grad_ln2_shift: float32 [2048], P(('seq', 'blk', 'uly'))
- grad_w_fc: float32 [2048, 8192], P(('seq', 'blk', 'uly'))
- grad_b_fc: float32 [8192], P(('seq', 'blk', 'uly'))
- grad_w_proj: float32 [8192, 2048], P(('seq', 'blk', 'uly'))
- grad_b_proj: float32 [2048], P(('seq', 'blk', 'uly'))
Inputs may be any that keep to these rules, and one draw needn't show every extreme that they name: `doc_lengths`: each row holds the lengths of the 3 documents packed in order into one sequence; they sum to 1024, and the longest is exactly 896 positions long.
All inputs are finite; a program needn't handle non-finite values.
Results may differ from a plain program's by a relative error of at most 0.02.
Values may be sent and summed in bfloat16 or wider, within the bound.
A program may use at most 448 MiB of HBM per device.

v0:
```python
import math

import jax
import jax.numpy as jnp
from jax import lax
from jax.sharding import PartitionSpec as P

HD = 128


EPS = 1e-05
NEGATIVE = -1e30


def passed_along(block, axis, distance):
    devices = range(lax.axis_size(axis))
    route = [(i - distance, i) for i in devices if i - distance in devices]
    return lax.ppermute(block, axis, route)


def from_behind(value, axis, by):
    devices = lax.axis_size(axis)
    return lax.ppermute(value, axis, [(i, (i + by) % devices) for i in range(devices)])


def layer_norm(values, norm_gain, norm_shift):
    average = jnp.mean(values, axis=-1, keepdims=True)
    centred = values - average
    variance = jnp.mean(centred * centred, axis=-1, keepdims=True)
    return centred * lax.rsqrt(variance + EPS) * norm_gain + norm_shift


def gelu_tanh(values):
    return jax.nn.gelu(values, approximate=True)


def product(left_side, right_side):
    return jnp.dot(left_side, right_side, preferred_element_type=jnp.float32)


def transposed(left_side, right_side):
    return lax.dot_general(
        left_side, right_side, (((0,), (0,)), ((), ())), preferred_element_type=jnp.float32
    )


def against(left_side, right_side):
    return lax.dot_general(
        left_side, right_side, (((1,), (1,)), ((), ())), preferred_element_type=jnp.float32
    )


def on_device(
    inputs,
    doc_lengths,
    ln1_gain,
    ln1_shift,
    w_query,
    b_query,
    w_key,
    w_value,
    b_value,
    w_out,
    b_out,
    ln2_gain,
    ln2_shift,
    w_fc,
    b_fc,
    w_proj,
    b_proj,
    cotangent,
):
    groups, tok_seq, model_width = inputs.shape
    heads_all = model_width // HD
    ulysses = lax.axis_size("uly")
    blocks = lax.axis_size("blk")
    heads_here = heads_all // ulysses
    block_rows = tok_seq * ulysses
    cycle_index = lax.axis_index("blk")
    scale = 1.0 / math.sqrt(HD)
    row_count = groups * tok_seq
    mixing_set = (
        lax.all_gather(ln1_gain, ("seq", "blk", "uly"), axis=0, tiled=True),
        lax.all_gather(ln1_shift, ("seq", "blk", "uly"), axis=0, tiled=True),
        lax.all_gather(w_query, ("seq", "blk", "uly"), axis=0, tiled=True),
        lax.all_gather(b_query, ("seq", "blk", "uly"), axis=0, tiled=True),
        lax.all_gather(w_key, ("seq", "blk", "uly"), axis=0, tiled=True),
        lax.all_gather(w_value, ("seq", "blk", "uly"), axis=0, tiled=True),
        lax.all_gather(b_value, ("seq", "blk", "uly"), axis=0, tiled=True),
        lax.all_gather(w_out, ("seq", "blk", "uly"), axis=0, tiled=True),
        lax.all_gather(b_out, ("seq", "blk", "uly"), axis=0, tiled=True),
    )
    feed_set = (
        lax.all_gather(ln2_gain, ("seq", "blk", "uly"), axis=0, tiled=True),
        lax.all_gather(ln2_shift, ("seq", "blk", "uly"), axis=0, tiled=True),
        lax.all_gather(w_fc, ("seq", "blk", "uly"), axis=0, tiled=True),
        lax.all_gather(b_fc, ("seq", "blk", "uly"), axis=0, tiled=True),
        lax.all_gather(w_proj, ("seq", "blk", "uly"), axis=0, tiled=True),
        lax.all_gather(b_proj, ("seq", "blk", "uly"), axis=0, tiled=True),
    )
    token_rows = inputs.reshape(row_count, model_width).astype(jnp.float32)
    gain_one = mixing_set[0].astype(jnp.float32)
    shift_one = mixing_set[1].astype(jnp.float32)
    normed_value, norm_back_one = jax.vjp(layer_norm, token_rows, gain_one, shift_one)
    normed = normed_value.astype(jnp.bfloat16)
    queries = ((product(normed, mixing_set[2]) + mixing_set[3].astype(jnp.float32)) * scale).astype(
        jnp.bfloat16
    )
    key_rows = product(normed, mixing_set[4]).astype(jnp.bfloat16)
    value_rows = (product(normed, mixing_set[5]) + mixing_set[6].astype(jnp.float32)).astype(
        jnp.bfloat16
    )
    head_shape = (groups, tok_seq, heads_all, HD)
    head_query, head_key, head_value = (
        lax.all_to_all(queries.reshape(head_shape), "uly", split_axis=2, concat_axis=1, tiled=True),
        lax.all_to_all(
            key_rows.reshape(head_shape), "uly", split_axis=2, concat_axis=1, tiled=True
        ),
        lax.all_to_all(
            value_rows.reshape(head_shape), "uly", split_axis=2, concat_axis=1, tiled=True
        ),
    )
    bounds = jnp.cumsum(doc_lengths, axis=1)
    offsets = jnp.arange(block_rows, dtype=jnp.int32)

    def doc_index(positions):
        first = (positions[None, :] >= bounds[:, 0:1]).astype(jnp.int32)
        return first + (positions[None, :] >= bounds[:, 1:2]).astype(jnp.int32)

    query_pos = cycle_index * block_rows + offsets
    query_doc = doc_index(query_pos)

    def allowed_for(source):
        key_pos = source * block_rows + offsets
        causal = (key_pos[None, :] <= query_pos[:, None]) & (source >= 0)
        same_doc = doc_index(key_pos)[:, None, :] == query_doc[:, :, None]
        return (causal[None] & same_doc)[:, :, None, :]

    def block_scores(key_block, source):
        products = jnp.einsum(
            "gqhd,gkhd->gqhk", head_query, key_block, preferred_element_type=jnp.float32
        )
        return jnp.where(allowed_for(source), products, NEGATIVE)

    def merge_block(key_value, source, running, denominator, weighted):
        scores = block_scores(key_value[0], source)
        newtop = jnp.maximum(running, jnp.max(scores, axis=3))
        factor = jnp.exp(running - newtop)
        powered = jnp.exp(scores - newtop[..., None])
        denominator = denominator * factor + jnp.sum(powered, axis=3)
        weighted = weighted * factor[..., None] + jnp.einsum(
            "gqhk,gkhd->gqhd",
            powered.astype(jnp.bfloat16),
            key_value[1],
            preferred_element_type=jnp.float32,
        )
        return (newtop, denominator, weighted)

    key_value = jnp.stack((head_key, head_value))
    start_top = jnp.full((groups, block_rows, heads_here), NEGATIVE, jnp.float32)
    start_sum = jnp.zeros((groups, block_rows, heads_here), jnp.float32)
    start_acc = jnp.zeros((groups, block_rows, heads_here, HD), jnp.float32)
    first_state = merge_block(key_value, cycle_index, start_top, start_sum, start_acc)

    def cycle_turn(turn_index, state_in):
        moving = passed_along(state_in[0], "blk", 1)
        source = cycle_index - turn_index
        return (moving,) + merge_block(moving, source, state_in[1], state_in[2], state_in[3])

    state_out = lax.fori_loop(1, blocks, cycle_turn, (key_value,) + first_state)
    running, denominator, weighted = (state_out[1], state_out[2], state_out[3])
    attended = weighted / denominator[..., None]
    log_total = running + jnp.log(denominator)
    attended_tok = lax.all_to_all(
        attended.astype(jnp.bfloat16), "uly", split_axis=1, concat_axis=2, tiled=True
    )
    attended_low = attended_tok.reshape(row_count, model_width)
    hidden = token_rows + product(attended_low, mixing_set[7]) + mixing_set[8].astype(jnp.float32)
    gain_two = feed_set[0].astype(jnp.float32)
    shift_two = feed_set[1].astype(jnp.float32)
    normed_two_value, norm_back_two = jax.vjp(layer_norm, hidden, gain_two, shift_two)
    normed_two = normed_two_value.astype(jnp.bfloat16)
    inner = product(normed_two, feed_set[2]) + feed_set[3].astype(jnp.float32)
    gelu_value, gelu_back = jax.vjp(gelu_tanh, inner)
    active = gelu_value.astype(jnp.bfloat16)
    result = (hidden + product(active, feed_set[4]) + feed_set[5].astype(jnp.float32)).astype(
        jnp.bfloat16
    )
    back_feed = (
        lax.all_gather(w_fc, ("seq", "blk", "uly"), axis=0, tiled=True),
        lax.all_gather(w_proj, ("seq", "blk", "uly"), axis=0, tiled=True),
    )
    grad_out = cotangent.reshape(row_count, model_width)
    grad_b_proj = jnp.sum(grad_out.astype(jnp.float32), axis=0)
    grad_w_proj = lax.psum_scatter(
        transposed(active, grad_out), ("seq", "blk", "uly"), scatter_dimension=0, tiled=True
    )
    grad_active = against(grad_out, back_feed[1])
    grad_inner = gelu_back(grad_active)[0].astype(jnp.bfloat16)
    grad_b_fc = jnp.sum(grad_inner.astype(jnp.float32), axis=0)
    grad_w_fc = lax.psum_scatter(
        transposed(normed_two, grad_inner), ("seq", "blk", "uly"), scatter_dimension=0, tiled=True
    )
    grad_normed_two = against(grad_inner, back_feed[0])
    hidden_part, grad_ln2_gain, grad_ln2_shift = norm_back_two(grad_normed_two)
    grad_hidden = grad_out.astype(jnp.float32) + hidden_part
    back_mixing = (
        lax.all_gather(w_query, ("seq", "blk", "uly"), axis=0, tiled=True),
        lax.all_gather(w_key, ("seq", "blk", "uly"), axis=0, tiled=True),
        lax.all_gather(w_value, ("seq", "blk", "uly"), axis=0, tiled=True),
        lax.all_gather(w_out, ("seq", "blk", "uly"), axis=0, tiled=True),
    )
    grad_branch = grad_hidden.astype(jnp.bfloat16)
    grad_b_out = jnp.sum(grad_branch.astype(jnp.float32), axis=0)
    grad_w_out = transposed(attended_low, grad_branch)
    grad_attended = against(grad_branch, back_mixing[3]).astype(jnp.bfloat16)
    grad_heads = lax.all_to_all(
        grad_attended.reshape(head_shape), "uly", split_axis=2, concat_axis=1, tiled=True
    )
    row_dots = jnp.sum(grad_heads.astype(jnp.float32) * attended, axis=3)

    def back_block(key_pair, source):
        scores = block_scores(key_pair[0], source)
        chances = jnp.exp(scores - log_total[..., None])
        grad_value = jnp.einsum(
            "gqhk,gqhd->gkhd",
            chances.astype(jnp.bfloat16),
            grad_heads,
            preferred_element_type=jnp.float32,
        )
        grad_chances = jnp.einsum(
            "gqhd,gkhd->gqhk", grad_heads, key_pair[1], preferred_element_type=jnp.float32
        )
        grad_scores = (chances * (grad_chances - row_dots[..., None])).astype(jnp.bfloat16)
        grad_query = jnp.einsum(
            "gqhk,gkhd->gqhd", grad_scores, key_pair[0], preferred_element_type=jnp.float32
        )
        grad_key = jnp.einsum(
            "gqhk,gqhd->gkhd", grad_scores, head_query, preferred_element_type=jnp.float32
        )
        return (grad_query, jnp.stack((grad_key, grad_value)))

    def back_turn(turn_index, state_in):
        moving, moving_grads, query_grads = state_in
        source = cycle_index - turn_index
        grad_query, grad_pair = back_block(moving, source)
        moving_grads = from_behind(
            (moving_grads + grad_pair).astype(jnp.bfloat16), "blk", 1
        ).astype(jnp.float32)
        moving = passed_along(moving, "blk", 1)
        return (moving, moving_grads, query_grads + grad_query)

    start_pair = jnp.zeros((2, groups, block_rows, heads_here, HD), jnp.float32)
    state_back = lax.fori_loop(0, blocks, back_turn, (key_value, start_pair, start_acc))
    pair_grads = state_back[1].astype(jnp.bfloat16)
    query_back, key_back, value_back = (
        lax.all_to_all(
            state_back[2].astype(jnp.bfloat16), "uly", split_axis=1, concat_axis=2, tiled=True
        ),
        lax.all_to_all(pair_grads[0], "uly", split_axis=1, concat_axis=2, tiled=True),
        lax.all_to_all(pair_grads[1], "uly", split_axis=1, concat_axis=2, tiled=True),
    )
    query_back = query_back.reshape(row_count, model_width)
    key_back = key_back.reshape(row_count, model_width)
    value_back = value_back.reshape(row_count, model_width)
    grad_b_query = jnp.sum(query_back.astype(jnp.float32), axis=0) * scale
    grad_b_value = jnp.sum(value_back.astype(jnp.float32), axis=0)
    grad_w_query = transposed(normed, query_back) * scale
    grad_w_key = transposed(normed, key_back)
    grad_w_value = transposed(normed, value_back)
    grad_normed = (
        against(query_back, back_mixing[0]) * scale
        + against(key_back, back_mixing[1])
        + against(value_back, back_mixing[2])
    )
    token_part, grad_ln1_gain, grad_ln1_shift = norm_back_one(grad_normed)
    grad_inputs = (
        (grad_hidden + token_part).astype(jnp.bfloat16).reshape(groups, tok_seq, model_width)
    )
    summed = (
        lax.psum_scatter(grad_ln1_gain, ("seq", "blk", "uly"), scatter_dimension=0, tiled=True),
        lax.psum_scatter(grad_ln1_shift, ("seq", "blk", "uly"), scatter_dimension=0, tiled=True),
        lax.psum_scatter(grad_w_query, ("seq", "blk", "uly"), scatter_dimension=0, tiled=True),
        lax.psum_scatter(grad_b_query, ("seq", "blk", "uly"), scatter_dimension=0, tiled=True),
        lax.psum_scatter(grad_w_key, ("seq", "blk", "uly"), scatter_dimension=0, tiled=True),
        lax.psum_scatter(grad_w_value, ("seq", "blk", "uly"), scatter_dimension=0, tiled=True),
        lax.psum_scatter(grad_b_value, ("seq", "blk", "uly"), scatter_dimension=0, tiled=True),
        lax.psum_scatter(grad_w_out, ("seq", "blk", "uly"), scatter_dimension=0, tiled=True),
        lax.psum_scatter(grad_b_out, ("seq", "blk", "uly"), scatter_dimension=0, tiled=True),
        lax.psum_scatter(grad_ln2_gain, ("seq", "blk", "uly"), scatter_dimension=0, tiled=True),
        lax.psum_scatter(grad_ln2_shift, ("seq", "blk", "uly"), scatter_dimension=0, tiled=True),
        lax.psum_scatter(grad_b_fc, ("seq", "blk", "uly"), scatter_dimension=0, tiled=True),
        lax.psum_scatter(grad_b_proj, ("seq", "blk", "uly"), scatter_dimension=0, tiled=True),
    )
    return (
        result.reshape(groups, tok_seq, model_width),
        grad_inputs,
        summed[0],
        summed[1],
        summed[2],
        summed[3],
        summed[4],
        summed[5],
        summed[6],
        summed[7],
        summed[8],
        summed[9],
        summed[10],
        grad_w_fc,
        summed[11],
        grad_w_proj,
        summed[12],
    )


def solution(mesh):
    placed = (
        P("seq", ("blk", "uly"), None),
        P("seq", None),
        P(("seq", "blk", "uly")),
        P(("seq", "blk", "uly")),
        P(("seq", "blk", "uly"), None),
        P(("seq", "blk", "uly")),
        P(("seq", "blk", "uly"), None),
        P(("seq", "blk", "uly"), None),
        P(("seq", "blk", "uly")),
        P(("seq", "blk", "uly"), None),
        P(("seq", "blk", "uly")),
        P(("seq", "blk", "uly")),
        P(("seq", "blk", "uly")),
        P(("seq", "blk", "uly"), None),
        P(("seq", "blk", "uly")),
        P(("seq", "blk", "uly"), None),
        P(("seq", "blk", "uly")),
        P("seq", ("blk", "uly"), None),
    )
    return jax.shard_map(
        on_device,
        mesh=mesh,
        in_specs=placed,
        out_specs=(
            P("seq", ("blk", "uly"), None),
            P("seq", ("blk", "uly"), None),
            P(("seq", "blk", "uly")),
            P(("seq", "blk", "uly")),
            P(("seq", "blk", "uly"), None),
            P(("seq", "blk", "uly")),
            P(("seq", "blk", "uly"), None),
            P(("seq", "blk", "uly"), None),
            P(("seq", "blk", "uly")),
            P(("seq", "blk", "uly"), None),
            P(("seq", "blk", "uly")),
            P(("seq", "blk", "uly")),
            P(("seq", "blk", "uly")),
            P(("seq", "blk", "uly"), None),
            P(("seq", "blk", "uly")),
            P(("seq", "blk", "uly"), None),
            P(("seq", "blk", "uly")),
        ),
        check_vma=False,
    )
```

profile of v0, /device:TPU:8, one launch (start us, length us, event | category | flops | bytes accessed | tf_op | source)
XLA Modules:
  0.0 3700.6 jit_solution(2482686726236969654)
XLA Ops:
  13.3 41.7 %all-reduce.18 = (bf16[2048]{0:T(1024)(128)(2,1)S(1)}, bf16[2048]{0:T(1024)(128)(2,1)S(1)}, bf16[2048]{0:T(1024)(128)(2,1)S(1)}, bf16[2048]{0:T(1024)(128)(2,1)S...) all-reduce(bf16[2048]{0:T(1024)(128)(2,1)S(1)} %dynamic-update-slic, ...), channel_id=1, replica_groups=mesh['seq'=2,'blk'=4,'uly'=4] {'seq','blk','uly'}, use_global_device_ids=true, to_apply=%add.1 | all-reduce | flops 16384 | bytes 65536
  57.1 32.6 all-gather.10.cloned.1.call-done
  89.7 5.7 fusion.74
  100.5 69.5 %all-gather.8.cloned.1.call-done = bf16[2048,2048]{1,0:T(8,128)(2,1)} async-done(((bf16[64,2048]{1,0:T(8,128)(2,1)}), bf16[2048,2048]{1,0:T(8,128)(2,1)}) %all-gather.8.cloned.1.call-update) | async-done | bytes 8388624 | tf_op jit(solution)/shard_map/all_gather | solution.py:87
  180.8 69.6 %all-gather.12.cloned.1.call-done = bf16[2048,2048]{1,0:T(8,128)(2,1)} async-done(((bf16[64,2048]{1,0:T(8,128)(2,1)}), bf16[2048,2048]{1,0:T(8,128)(2,1)}) %all-gather.12.cloned.1.call-update) | async-done | bytes 8388624 | tf_op jit(solution)/shard_map/all_gather | solution.py:85
  250.4 5.8 fusion.73
  268.8 8.0 all-to-all-done.2
  285.1 339.6 %while.38 = (s32[]{:T(128)}, bf16[2,4,256,4,128]{4,2,3,1,0:T(8,128)(2,1)}, f32[4,256,4]{1,2,0:T(4,128)S(1)}, f32[4,256,4]{1,2,0:T(4,128)S(1)}, f32[4,256,4,128]{...) while((s32[]{:T(128)}, ...), condition=%wide.region_8.9_spmd.clone, body=%wide.region_5.8_spmd.clone.sunk | while | flops 546982400 | bytes 50747796 | solution.py:170
  288.5 72.8 %collective-permute-done = bf16[2,4,256,4,128]{4,2,3,1,0:T(8,128)(2,1)S(1)} collective-permute-done((bf16[2,4,256,4,128]{4,2,3,1,0:T(8,128)(2,1)}, bf16[2,4,256,4,128]{4,2,3,1,0:T(8,128)(2,1)S(1)}, u32[]{:S(2)}, u32[]{:S(2)}) %collective-permute-start) | collective-permute-done | bytes 2097184 | tf_op jit(solution)/shard_map/while/body/eval_jaxpr/ppermute | solution.py:18
  372.2 103.2 %collective-permute-done = bf16[2,4,256,4,128]{4,2,3,1,0:T(8,128)(2,1)S(1)} collective-permute-done((bf16[2,4,256,4,128]{4,2,3,1,0:T(8,128)(2,1)}, bf16[2,4,256,4,128]{4,2,3,1,0:T(8,128)(2,1)S(1)}, u32[]{:S(2)}, u32[]{:S(2)}) %collective-permute-start) | collective-permute-done | bytes 2097184 | tf_op jit(solution)/shard_map/while/body/eval_jaxpr/ppermute | solution.py:18
  487.4 130.1 %collective-permute-done = bf16[2,4,256,4,128]{4,2,3,1,0:T(8,128)(2,1)S(1)} collective-permute-done((bf16[2,4,256,4,128]{4,2,3,1,0:T(8,128)(2,1)}, bf16[2,4,256,4,128]{4,2,3,1,0:T(8,128)(2,1)S(1)}, u32[]{:S(2)}, u32[]{:S(2)}) %collective-permute-start) | collective-permute-done | bytes 2097184 | tf_op jit(solution)/shard_map/while/body/eval_jaxpr/ppermute | solution.py:18
  625.0 5.9 fusion.81
  634.5 50.0 %all-gather = bf16[32,1,256]{2,1,0:T(2,128)(2,1)S(1)} all-gather(bf16[1,1,256]{2,1,0:T(2,128)(2,1)S(1)} %reshape.607), channel_id=1, replica_groups=mesh['seq'=2,'blk'=4,'uly'=4] {'seq','blk','uly'}, dimensions={0}, use_global_device_ids=true | all-gather | bytes 16896 | tf_op jit(solution)/shard_map/all_gather | solution.py:97
  687.8 6.2 fusion.88
  695.8 18.8 fusion.89
  714.6 103.9 %all-gather.16.cloned.1.call-done = bf16[2048,8192]{1,0:T(8,128)(2,1)} async-done(((bf16[64,8192]{1,0:T(8,128)(2,1)}), bf16[2048,8192]{1,0:T(8,128)(2,1)}) %all-gather.16.cloned.1.call-update) | async-done | bytes 33554448 | tf_op jit(solution)/shard_map/all_gather | solution.py:96
  818.5 25.3 convert_reduce_fusion
  843.8 18.4 multiply_reduce_fusion
  865.9 6.1 fusion.72
  877.1 14.4 all-to-all-done.4
  893.1 7.1 multiply_reduce_fusion.3
  900.4 422.0 %while.39 = (s32[]{:T(128)}, bf16[2,4,256,4,128]{4,2,3,1,0:T(8,128)(2,1)}, f32[2,4,256,4,128]{4,2,3,1,0:T(8,128)}, f32[4,256,4,128]{3,1,2,0:T(8,128)}, s32[]{:T(...) while((s32[]{:T(128)}, ...), condition=%wide.region_15.16_spmd.clone, body=%wide.region_14.15_spmd.clone.sunk | while | flops 1357523456 | bytes 98507256 | solution.py:254
  922.5 41.1 %collective-permute-done.2 = bf16[2,4,256,4,128]{4,2,3,1,0:T(8,128)(2,1)} collective-permute-done((bf16[2,4,256,4,128]{4,2,3,1,0:T(8,128)(2,1)}, bf16[2,4,256,4,128]{4,2,3,1,0:T(8,128)(2,1)}, u32[]{:S(2)}, u32[]{:S(2)}) %collective-permute-start.2) | collective-permute-done | bytes 2097184 | tf_op jit(solution)/shard_map/while/body/eval_jaxpr/ppermute | solution.py:23
  967.7 39.8 %collective-permute-done.1 = bf16[2,4,256,4,128]{4,2,3,1,0:T(8,128)(2,1)} collective-permute-done((bf16[2,4,256,4,128]{4,2,3,1,0:T(8,128)(2,1)}, bf16[2,4,256,4,128]{4,2,3,1,0:T(8,128)(2,1)}, u32[]{:S(2)}, u32[]{:S(2)}) %collective-permute-start.1) | collective-permute-done | bytes 2097184 | tf_op jit(solution)/shard_map/while/body/eval_jaxpr/ppermute | solution.py:18
  1029.6 40.7 %collective-permute-done.2 = bf16[2,4,256,4,128]{4,2,3,1,0:T(8,128)(2,1)} collective-permute-done((bf16[2,4,256,4,128]{4,2,3,1,0:T(8,128)(2,1)}, bf16[2,4,256,4,128]{4,2,3,1,0:T(8,128)(2,1)}, u32[]{:S(2)}, u32[]{:S(2)}) %collective-permute-start.2) | collective-permute-done | bytes 2097184 | tf_op jit(solution)/shard_map/while/body/eval_jaxpr/ppermute | solution.py:23
  1074.4 38.9 %collective-permute-done.1 = bf16[2,4,256,4,128]{4,2,3,1,0:T(8,128)(2,1)} collective-permute-done((bf16[2,4,256,4,128]{4,2,3,1,0:T(8,128)(2,1)}, bf16[2,4,256,4,128]{4,2,3,1,0:T(8,128)(2,1)}, u32[]{:S(2)}, u32[]{:S(2)}) %collective-permute-start.1) | collective-permute-done | bytes 2097184 | tf_op jit(solution)/shard_map/while/body/eval_jaxpr/ppermute | solution.py:18
  1135.1 41.1 %collective-permute-done.2 = bf16[2,4,256,4,128]{4,2,3,1,0:T(8,128)(2,1)} collective-permute-done((bf16[2,4,256,4,128]{4,2,3,1,0:T(8,128)(2,1)}, bf16[2,4,256,4,128]{4,2,3,1,0:T(8,128)(2,1)}, u32[]{:S(2)}, u32[]{:S(2)}) %collective-permute-start.2) | collective-permute-done | bytes 2097184 | tf_op jit(solution)/shard_map/while/body/eval_jaxpr/ppermute | solution.py:23
  1180.2 37.9 %collective-permute-done.1 = bf16[2,4,256,4,128]{4,2,3,1,0:T(8,128)(2,1)} collective-permute-done((bf16[2,4,256,4,128]{4,2,3,1,0:T(8,128)(2,1)}, bf16[2,4,256,4,128]{4,2,3,1,0:T(8,128)(2,1)}, u32[]{:S(2)}, u32[]{:S(2)}) %collective-permute-start.1) | collective-permute-done | bytes 2097184 | tf_op jit(solution)/shard_map/while/body/eval_jaxpr/ppermute | solution.py:18
  1239.6 41.4 %collective-permute-done.2 = bf16[2,4,256,4,128]{4,2,3,1,0:T(8,128)(2,1)} collective-permute-done((bf16[2,4,256,4,128]{4,2,3,1,0:T(8,128)(2,1)}, bf16[2,4,256,4,128]{4,2,3,1,0:T(8,128)(2,1)}, u32[]{:S(2)}, u32[]{:S(2)}) %collective-permute-start.2) | collective-permute-done | bytes 2097184 | tf_op jit(solution)/shard_map/while/body/eval_jaxpr/ppermute | solution.py:23
  1285.1 37.0 %collective-permute-done.1 = bf16[2,4,256,4,128]{4,2,3,1,0:T(8,128)(2,1)} collective-permute-done((bf16[2,4,256,4,128]{4,2,3,1,0:T(8,128)(2,1)}, bf16[2,4,256,4,128]{4,2,3,1,0:T(8,128)(2,1)}, u32[]{:S(2)}, u32[]{:S(2)}) %collective-permute-start.1) | collective-permute-done | bytes 2097184 | tf_op jit(solution)/shard_map/while/body/eval_jaxpr/ppermute | solution.py:18
  1329.1 17.7 all_to_all.132
  1353.4 12.2 all-to-all-done.6
  1387.5 5.9 fusion.91
  1393.5 5.9 fusion.90
  1407.2 8.2 fusion.94
  1416.6 8.1 convolution_multiply_fusion
  1426.0 8.3 fusion.92
  1435.5 8.2 fusion.93
  1445.3 25.5 fusion.82
  1470.9 27.5 fusion.83
  1499.1 19.6 fusion.62
  1523.2 9.4 all-reduce.21.cloned.1.call-done
  1543.9 172.4 %reduce-scatter.13.cloned.1.call-done = f32[64,2048]{1,0:T(8,128)} async-done(((f32[2048,2048]{1,0:T(8,128)}), f32[64,2048]{1,0:T(8,128)}) %reduce-scatter.13.cloned.1.call-update) | async-done | bytes 524304 | tf_op jit(solution)/shard_map/reduce_scatter | solution.py:288
  1716.3 186.8 %reduce-scatter.7.cloned.1.call-done = f32[64,2048]{1,0:T(8,128)} async-done(((f32[2048,2048]{1,0:T(8,128)}), f32[64,2048]{1,0:T(8,128)}) %reduce-scatter.7.cloned.1.call-update) | async-done | bytes 524304 | tf_op jit(solution)/shard_map/reduce_scatter | solution.py:283
  1903.2 187.0 %reduce-scatter.9.cloned.1.call-done = f32[64,2048]{1,0:T(8,128)} async-done(((f32[2048,2048]{1,0:T(8,128)}), f32[64,2048]{1,0:T(8,128)}) %reduce-scatter.9.cloned.1.call-update) | async-done | bytes 524304 | tf_op jit(solution)/shard_map/reduce_scatter | solution.py:285
  2090.2 187.2 %reduce-scatter.11.cloned.1.call-done = f32[64,2048]{1,0:T(8,128)} async-done(((f32[2048,2048]{1,0:T(8,128)}), f32[64,2048]{1,0:T(8,128)}) %reduce-scatter.11.cloned.1.call-update) | async-done | bytes 524304 | tf_op jit(solution)/shard_map/reduce_scatter | solution.py:286
  2277.4 707.2 %reduce-scatter.15.cloned.1.call-done = f32[64,8192]{1,0:T(8,128)} async-done(((f32[2048,8192]{1,0:T(8,128)}), f32[64,8192]{1,0:T(8,128)}) %reduce-scatter.15.cloned.1.call-update) | async-done | bytes 2097168 | tf_op jit(solution)/shard_map/reduce_scatter | solution.py:201
  2984.6 709.0 %reduce-scatter.17.cloned.1.call-done = f32[256,2048]{1,0:T(8,128)} async-done(((f32[8192,2048]{1,0:T(8,128)}), f32[256,2048]{1,0:T(8,128)}) %reduce-scatter.17.cloned.1.call-update) | async-done | bytes 2097168 | tf_op jit(solution)/shard_map/reduce_scatter | solution.py:195
  (419 shorter events, 265.2 us)
Async XLA Ops:
  7.3 47.7 %copy-start.5 = (bf16[4,64,2048]{2,1,0:T(8,128)(2,1)S(1)}, bf16[4,64,2048]{2,1,0:T(8,128)(2,1)}, u32[]{:S(2)}) copy-start(bf16[4,64,2048]{2,1,0:T(8,128)(2,1)} %param.22) | copy-start | bytes 3145732
  7.3 82.4 %all-gather.10.cloned.1.call-start = ((), (), s32[]{:S(2)}) async-start(), calls=%async_computation.15 | async-start | bytes 8650752 | tf_op jit(solution)/shard_map/all_gather | solution.py:88
  8.0 162.0 %all-gather.8.cloned.1.call-start = ((), (), s32[]{:S(2)}) async-start(), calls=%async_computation.14 | async-start | bytes 8650752 | tf_op jit(solution)/shard_map/all_gather | solution.py:87
  8.8 241.6 %all-gather.12.cloned.1.call-start = ((), (), s32[]{:S(2)}) async-start(), calls=%async_computation.16 | async-start | bytes 8650752 | tf_op jit(solution)/shard_map/all_gather | solution.py:85
  9.5 678.3 %all-gather.14.cloned.1.call-start = ((), (), s32[]{:S(2)}) async-start(), calls=%async_computation.17 | async-start | bytes 8650752 | tf_op jit(solution)/shard_map/all_gather | solution.py:90
  10.1 46.4 %copy-start.57 = (s32[4,3]{1,0:T(4,128)S(1)}, s32[4,3]{1,0:T(4,128)}, u32[]{:S(2)}) copy-start(s32[4,3]{1,0:T(4,128)} %param.23) | copy-start | bytes 148
  10.1 685.6 %all-gather.18.cloned.1.call-start = ((), (), s32[]{:S(2)}) async-start(), calls=%async_computation.19 | async-start | bytes 34603008 | tf_op jit(solution)/shard_map/all_gather | solution.py:98
  10.7 807.8 %all-gather.16.cloned.1.call-start = ((), (), s32[]{:S(2)}) async-start(), calls=%async_computation.18 | async-start | bytes 34603008 | tf_op jit(solution)/shard_map/all_gather | solution.py:96
  55.2 40.2 %copy-start.45 = (f32[4,64]{1,0:T(4,128)}, f32[4,64]{1,0:T(4,128)S(1)}, u32[]{:S(2)}) copy-start(f32[4,64]{1,0:T(4,128)S(1)} %broadcast_multiply_fusion.1) | copy-start | bytes 3076
  55.3 40.1 %copy-start.47 = (f32[256]{0:T(256)}, f32[256]{0:T(256)S(1)}, u32[]{:S(2)}) copy-start(f32[256]{0:T(256)S(1)} %div.47) | copy-start | bytes 3076
  56.4 39.0 %copy-start.53 = (f32[256]{0:T(256)}, f32[256]{0:T(256)S(1)}, u32[]{:S(2)}) copy-start(f32[256]{0:T(256)S(1)} %add.294) | copy-start | bytes 3076
  56.4 39.0 %copy-start.49 = (f32[256]{0:T(256)}, f32[256]{0:T(256)S(1)}, u32[]{:S(2)}) copy-start(f32[256]{0:T(256)S(1)} %rsqrt.23) | copy-start | bytes 3076
  96.9 80.3 %all-to-all-start.1 = ((bf16[4,64,16,128]{3,1,0,2:T(8,128)(2,1)}), bf16[4,64,16,128]{3,1,0,2:T(8,128)(2,1)S(1)}, u32[]{:S(2)}, u32[]{:S(2)}) async-start(bf16[4,64,16,128]{3,1,0,2:T(8,128)(2,1)} %copy.118), calls=%async_computation.1 | async-start | bytes 2097152 | tf_op jit(solution)/shard_map/all_to_all | solution.py:119
  177.3 80.4 %all-to-all-start = ((bf16[4,64,16,128]{3,1,0,2:T(8,128)(2,1)}), bf16[4,64,16,128]{3,1,0,2:T(8,128)(2,1)S(1)}, u32[]{:S(2)}, u32[]{:S(2)}) async-start(bf16[4,64,16,128]{3,1,0,2:T(8,128)(2,1)} %copy.116), calls=%async_computation | async-start | bytes 2097152 | tf_op jit(solution)/shard_map/all_to_all | solution.py:116
  257.7 19.1 all-to-all-start.2
  285.1 76.1 %collective-permute-start = (bf16[2,4,256,4,128]{4,2,3,1,0:T(8,128)(2,1)}, bf16[2,4,256,4,128]{4,2,3,1,0:T(8,128)(2,1)S(1)}, u32[]{:S(2)}, u32[]{:S(2)}) collective-permute-start(bf16[2,4,256,4,128]{4,2,3,1,0:T(8,128)(2,1)} %get-tuple-element.915), channel_id=1, source_target_pairs={{0,4},{4,8},{8,12},{1,5},{5,9},{9,13},{2,6},{6,10},{10,14},{3,7},{... | collective-permute-start | bytes 6291464 | tf_op jit(solution)/shard_map/while/body/eval_jaxpr/ppermute | solution.py:18
  368.5 106.8 %collective-permute-start = (bf16[2,4,256,4,128]{4,2,3,1,0:T(8,128)(2,1)}, bf16[2,4,256,4,128]{4,2,3,1,0:T(8,128)(2,1)S(1)}, u32[]{:S(2)}, u32[]{:S(2)}) collective-permute-start(bf16[2,4,256,4,128]{4,2,3,1,0:T(8,128)(2,1)} %get-tuple-element.915), channel_id=1, source_target_pairs={{0,4},{4,8},{8,12},{1,5},{5,9},{9,13},{2,6},{6,10},{10,14},{3,7},{... | collective-permute-start | bytes 6291464 | tf_op jit(solution)/shard_map/while/body/eval_jaxpr/ppermute | solution.py:18
  482.6 134.9 %collective-permute-start = (bf16[2,4,256,4,128]{4,2,3,1,0:T(8,128)(2,1)}, bf16[2,4,256,4,128]{4,2,3,1,0:T(8,128)(2,1)S(1)}, u32[]{:S(2)}, u32[]{:S(2)}) collective-permute-start(bf16[2,4,256,4,128]{4,2,3,1,0:T(8,128)(2,1)} %get-tuple-element.915), channel_id=1, source_target_pairs={{0,4},{4,8},{8,12},{1,5},{5,9},{9,13},{2,6},{6,10},{10,14},{3,7},{... | collective-permute-start | bytes 6291464 | tf_op jit(solution)/shard_map/while/body/eval_jaxpr/ppermute | solution.py:18
  630.9 53.6 %all-to-all-start.3 = ((bf16[4,256,4,128]{3,2,0,1:T(4,128)(2,1)}), bf16[4,256,4,128]{3,2,0,1:T(4,128)(2,1)S(1)}, u32[]{:S(2)}, u32[]{:S(2)}) async-start(bf16[4,256,4,128]{3,2,0,1:T(4,128)(2,1)} %fusion.81), calls=%async_computation.3 | async-start | bytes 2097152 | tf_op jit(solution)/shard_map/all_to_all | solution.py:174
  684.5 133.9 %copy-start.35 = (f32[2048]{0:T(1024)}, f32[2048]{0:T(1024)S(1)}, u32[]{:S(2)}) copy-start(f32[2048]{0:T(1024)S(1)} %convert_element_type.236) | copy-start | bytes 24580
  684.6 177.6 %copy-start.33 = (f32[2048]{0:T(1024)}, f32[2048]{0:T(1024)S(1)}, u32[]{:S(2)}) copy-start(f32[2048]{0:T(1024)S(1)} %convert_element_type.235) | copy-start | bytes 24580
  694.0 168.2 %copy-start.39 = (f32[256]{0:T(256)}, f32[256]{0:T(256)S(1)}, u32[]{:S(2)}) copy-start(f32[256]{0:T(256)S(1)} %broadcast_multiply_fusion.2) | copy-start | bytes 3076
  695.7 166.5 %copy-start.43 = (f32[256]{0:T(256)}, f32[256]{0:T(256)S(1)}, u32[]{:S(2)}) copy-start(f32[256]{0:T(256)S(1)} %fusion.76) | copy-start | bytes 3076
  695.7 122.7 %copy-start.11 = (f32[256,2048]{1,0:T(8,128)S(1)}, f32[256,2048]{1,0:T(8,128)}, u32[]{:S(2)}) copy-start(f32[256,2048]{1,0:T(8,128)} %copy-done.10) | copy-start | bytes 6291460
  873.5 18.0 all-to-all-start.4
  914.4 49.2 %collective-permute-start.2 = (bf16[2,4,256,4,128]{4,2,3,1,0:T(8,128)(2,1)}, bf16[2,4,256,4,128]{4,2,3,1,0:T(8,128)(2,1)}, u32[]{:S(2)}, u32[]{:S(2)}) collective-permute-start(bf16[2,4,256,4,128]{4,2,3,1,0:T(8,128)(2,1)} %fusion.174), channel_id=1, source_target_pairs={{0,4},{4,8},{8,12},{12,0},{1,5},{5,9},{9,13},{13,1},{2,6},{6,10},{... | collective-permute-start | bytes 6291464 | tf_op jit(solution)/shard_map/while/body/eval_jaxpr/ppermute | solution.py:23
  916.8 90.6 %collective-permute-start.1 = (bf16[2,4,256,4,128]{4,2,3,1,0:T(8,128)(2,1)}, bf16[2,4,256,4,128]{4,2,3,1,0:T(8,128)(2,1)}, u32[]{:S(2)}, u32[]{:S(2)}) collective-permute-start(bf16[2,4,256,4,128]{4,2,3,1,0:T(8,128)(2,1)} %copy.197), channel_id=1, source_target_pairs={{0,4},{4,8},{8,12},{1,5},{5,9},{9,13},{2,6},{6,10},{10,14},{3,7},{... | collective-permute-start | bytes 6291464 | tf_op jit(solution)/shard_map/while/body/eval_jaxpr/ppermute | solution.py:18
  922.5 85.0 %copy-start.9 = (bf16[4,256,4,128]{3,1,2,0:T(8,128)(2,1)S(1)}, bf16[4,256,4,128]{3,1,2,0:T(8,128)(2,1)}, u32[]{:S(2)}) copy-start(bf16[4,256,4,128]{3,1,2,0:T(8,128)(2,1)} %copy-done.8) | copy-start | bytes 3145732 | tf_op jit(solution)/shard_map/while
  1021.4 48.9 %collective-permute-start.2 = (bf16[2,4,256,4,128]{4,2,3,1,0:T(8,128)(2,1)}, bf16[2,4,256,4,128]{4,2,3,1,0:T(8,128)(2,1)}, u32[]{:S(2)}, u32[]{:S(2)}) collective-permute-start(bf16[2,4,256,4,128]{4,2,3,1,0:T(8,128)(2,1)} %fusion.174), channel_id=1, source_target_pairs={{0,4},{4,8},{8,12},{12,0},{1,5},{5,9},{9,13},{13,1},{2,6},{6,10},{... | collective-permute-start | bytes 6291464 | tf_op jit(solution)/shard_map/while/body/eval_jaxpr/ppermute | solution.py:23
  1023.2 90.1 %collective-permute-start.1 = (bf16[2,4,256,4,128]{4,2,3,1,0:T(8,128)(2,1)}, bf16[2,4,256,4,128]{4,2,3,1,0:T(8,128)(2,1)}, u32[]{:S(2)}, u32[]{:S(2)}) collective-permute-start(bf16[2,4,256,4,128]{4,2,3,1,0:T(8,128)(2,1)} %copy.197), channel_id=1, source_target_pairs={{0,4},{4,8},{8,12},{1,5},{5,9},{9,13},{2,6},{6,10},{10,14},{3,7},{... | collective-permute-start | bytes 6291464 | tf_op jit(solution)/shard_map/while/body/eval_jaxpr/ppermute | solution.py:18
  1029.6 83.7 %copy-start.9 = (bf16[4,256,4,128]{3,1,2,0:T(8,128)(2,1)S(1)}, bf16[4,256,4,128]{3,1,2,0:T(8,128)(2,1)}, u32[]{:S(2)}) copy-start(bf16[4,256,4,128]{3,1,2,0:T(8,128)(2,1)} %copy-done.8) | copy-start | bytes 3145732 | tf_op jit(solution)/shard_map/while
  1127.2 48.9 %collective-permute-start.2 = (bf16[2,4,256,4,128]{4,2,3,1,0:T(8,128)(2,1)}, bf16[2,4,256,4,128]{4,2,3,1,0:T(8,128)(2,1)}, u32[]{:S(2)}, u32[]{:S(2)}) collective-permute-start(bf16[2,4,256,4,128]{4,2,3,1,0:T(8,128)(2,1)} %fusion.174), channel_id=1, source_target_pairs={{0,4},{4,8},{8,12},{12,0},{1,5},{5,9},{9,13},{13,1},{2,6},{6,10},{... | collective-permute-start | bytes 6291464 | tf_op jit(solution)/shard_map/while/body/eval_jaxpr/ppermute | solution.py:23
  1128.7 89.5 %collective-permute-start.1 = (bf16[2,4,256,4,128]{4,2,3,1,0:T(8,128)(2,1)}, bf16[2,4,256,4,128]{4,2,3,1,0:T(8,128)(2,1)}, u32[]{:S(2)}, u32[]{:S(2)}) collective-permute-start(bf16[2,4,256,4,128]{4,2,3,1,0:T(8,128)(2,1)} %copy.197), channel_id=1, source_target_pairs={{0,4},{4,8},{8,12},{1,5},{5,9},{9,13},{2,6},{6,10},{10,14},{3,7},{... | collective-permute-start | bytes 6291464 | tf_op jit(solution)/shard_map/while/body/eval_jaxpr/ppermute | solution.py:18
  1135.1 83.1 %copy-start.9 = (bf16[4,256,4,128]{3,1,2,0:T(8,128)(2,1)S(1)}, bf16[4,256,4,128]{3,1,2,0:T(8,128)(2,1)}, u32[]{:S(2)}) copy-start(bf16[4,256,4,128]{3,1,2,0:T(8,128)(2,1)} %copy-done.8) | copy-start | bytes 3145732 | tf_op jit(solution)/shard_map/while
  1232.1 48.9 %collective-permute-start.2 = (bf16[2,4,256,4,128]{4,2,3,1,0:T(8,128)(2,1)}, bf16[2,4,256,4,128]{4,2,3,1,0:T(8,128)(2,1)}, u32[]{:S(2)}, u32[]{:S(2)}) collective-permute-start(bf16[2,4,256,4,128]{4,2,3,1,0:T(8,128)(2,1)} %fusion.174), channel_id=1, source_target_pairs={{0,4},{4,8},{8,12},{12,0},{1,5},{5,9},{9,13},{13,1},{2,6},{6,10},{... | collective-permute-start | bytes 6291464 | tf_op jit(solution)/shard_map/while/body/eval_jaxpr/ppermute | solution.py:23
  1233.2 88.9 %collective-permute-start.1 = (bf16[2,4,256,4,128]{4,2,3,1,0:T(8,128)(2,1)}, bf16[2,4,256,4,128]{4,2,3,1,0:T(8,128)(2,1)}, u32[]{:S(2)}, u32[]{:S(2)}) collective-permute-start(bf16[2,4,256,4,128]{4,2,3,1,0:T(8,128)(2,1)} %copy.197), channel_id=1, source_target_pairs={{0,4},{4,8},{8,12},{1,5},{5,9},{9,13},{2,6},{6,10},{10,14},{3,7},{... | collective-permute-start | bytes 6291464 | tf_op jit(solution)/shard_map/while/body/eval_jaxpr/ppermute | solution.py:18
  1239.6 82.5 %copy-start.9 = (bf16[4,256,4,128]{3,1,2,0:T(8,128)(2,1)S(1)}, bf16[4,256,4,128]{3,1,2,0:T(8,128)(2,1)}, u32[]{:S(2)}) copy-start(bf16[4,256,4,128]{3,1,2,0:T(8,128)(2,1)} %copy-done.8) | copy-start | bytes 3145732 | tf_op jit(solution)/shard_map/while
  1329.1 22.0 copy-start.4
  1346.8 18.8 all-to-all-start.6
  1365.6 18.0 all-to-all-start.5
  1369.1 163.5 %all-reduce.21.cloned.1.call-start = ((), (), s32[]{:S(2)}) async-start(), calls=%async_computation.26 | async-start | bytes 196608
  1406.9 309.4 %reduce-scatter.13.cloned.1.call-start = ((), (), s32[]{:S(2)}) async-start(), calls=%async_computation.23 | async-start | bytes 17301504 | tf_op jit(solution)/shard_map/reduce_scatter | solution.py:288
  1415.4 487.8 %reduce-scatter.7.cloned.1.call-start = ((), (), s32[]{:S(2)}) async-start(), calls=%async_computation.20 | async-start | bytes 17301504 | tf_op jit(solution)/shard_map/reduce_scatter | solution.py:283
  1424.8 665.4 %reduce-scatter.9.cloned.1.call-start = ((), (), s32[]{:S(2)}) async-start(), calls=%async_computation.21 | async-start | bytes 17301504 | tf_op jit(solution)/shard_map/reduce_scatter | solution.py:285
  1434.3 843.1 %reduce-scatter.11.cloned.1.call-start = ((), (), s32[]{:S(2)}) async-start(), calls=%async_computation.22 | async-start | bytes 17301504 | tf_op jit(solution)/shard_map/reduce_scatter | solution.py:286
  1443.8 1540.8 %reduce-scatter.15.cloned.1.call-start = ((), (), s32[]{:S(2)}) async-start(), calls=%async_computation.24 | async-start | bytes 69206016 | tf_op jit(solution)/shard_map/reduce_scatter | solution.py:201
  1470.9 2222.7 %reduce-scatter.17.cloned.1.call-start = ((), (), s32[]{:S(2)}) async-start(), calls=%async_computation.25 | async-start | bytes 69206016 | tf_op jit(solution)/shard_map/reduce_scatter | solution.py:195
  1499.1 19.6 copy-start.52
  (65 other events, 266.4 us)
Sparse Core Ops, SparseCore 0:
  11.0 78.6 all-gather.9
  92.5 77.4 all-gather.7
  172.9 77.4 all-gather.11
  253.1 97.7 all-gather.13
  353.6 268.7 all-gather.17
  625.1 193.3 all-gather.15
  1407.1 125.4 all-reduce.20
  1535.5 180.7 reduce-scatter.12
  1719.3 183.8 reduce-scatter.6
  1906.0 184.1 reduce-scatter.8
  2093.2 184.1 reduce-scatter.10
  2280.3 704.2 reduce-scatter.14
  2987.7 705.9 reduce-scatter.16
where the time goes:
time: 3720 us; the launch traced here: 3700 us
  waiting for transfers between devices  3100 us (83%)
  matrix products  264 us (7%)
  blocking collectives  109 us (3%)
  local copies, waits for them, and re-layouts  93 us (2%)
  other arithmetic  61.7 us (2%)
  starting transfers between devices  54 us (1%)
    reduce_scatter x1, waiting for transfers between devices, on_device(): lax.psum_scatter(transposed(active, grad_out), ('seq', 'blk', 'uly'), sca...  709 us
    reduce_scatter x1, waiting for transfers between devices, on_device(): lax.psum_scatter(transposed(normed_two, grad_inner), ('seq', 'blk', 'uly'...  707 us
    ppermute x7, waiting for transfers between devices, passed_along(): return lax.ppermute(block, axis, route)  460 us
    reduce_scatter x1, waiting for transfers between devices, on_device(): lax.psum_scatter(grad_w_value, ('seq', 'blk', 'uly'), scatter_dimension=0...  187 us
    reduce_scatter x1, waiting for transfers between devices, on_device(): lax.psum_scatter(grad_w_key, ('seq', 'blk', 'uly'), scatter_dimension=0,...  187 us
    reduce_scatter x1, waiting for transfers between devices, on_device(): lax.psum_scatter(grad_w_query, ('seq', 'blk', 'uly'), scatter_dimension=0...  187 us
    reduce_scatter x1, waiting for transfers between devices, on_device(): lax.psum_scatter(grad_w_out, ('seq', 'blk', 'uly'), scatter_dimension=0,...  172 us
    ppermute x4, waiting for transfers between devices, from_behind(): lax.ppermute(value, axis, [(i, (i + by) % devices) for i in range(devices)])  164 us
  transfers between devices with their start and end apart: 31, of which 26 were waited for; matrix products, arithmetic and copies ran while one was open for 7% of the time, Pallas kernels for 0%

commit v1 on v0

v1 whole, which is shorter than its diff:
```python
import math

import jax
import jax.numpy as jnp
from jax import lax
from jax.sharding import PartitionSpec as P

HD = 128
EPS = 1e-05
NEGATIVE = -1e30
ALL = ("seq", "blk", "uly")
PLANE = ("seq", "uly")
BF = jnp.bfloat16
F32 = jnp.float32


def layer_norm(values, norm_gain, norm_shift):
    average = jnp.mean(values, axis=-1, keepdims=True)
    centred = values - average
    variance = jnp.mean(centred * centred, axis=-1, keepdims=True)
    return centred * lax.rsqrt(variance + EPS) * norm_gain + norm_shift


def gelu_tanh(values):
    return jax.nn.gelu(values, approximate=True)


def product(left_side, right_side):
    return jnp.dot(left_side, right_side, preferred_element_type=F32)


def transposed(left_side, right_side):
    return lax.dot_general(
        left_side, right_side, (((0,), (0,)), ((), ())), preferred_element_type=F32
    )


def against(left_side, right_side):
    return lax.dot_general(
        left_side, right_side, (((1,), (1,)), ((), ())), preferred_element_type=F32
    )


def gather_plane(rows):
    return lax.all_gather(rows, PLANE, axis=0, tiled=True)


def scatter_plane(rows):
    return lax.psum_scatter(rows.astype(BF), PLANE, scatter_dimension=0, tiled=True)


def on_device(
    inputs,
    doc_lengths,
    ln1_gain,
    ln1_shift,
    w_query,
    b_query,
    w_key,
    w_value,
    b_value,
    w_out,
    b_out,
    ln2_gain,
    ln2_shift,
    w_fc,
    b_fc,
    w_proj,
    b_proj,
    cotangent,
):
    seqs, tok, width = inputs.shape
    n_seq, n_blk, n_uly = (lax.axis_size(a) for a in ALL)
    plane = n_seq * n_uly
    devices = plane * n_blk
    here_seq, here_blk, here_uly = (lax.axis_index(a) for a in ALL)
    here = here_seq * n_uly + here_uly
    scale = 1.0 / math.sqrt(HD)
    rows = w_query.shape[0]
    hidden_rows = w_proj.shape[0]
    share = width // plane
    heads = share // HD
    ff_share = hidden_rows * n_blk
    sharing = max(1, n_blk // seqs)
    held = seqs * sharing // n_blk
    part = tok // sharing
    n_rows = n_blk * held * part

    high = doc_lengths // 16
    vectors = (ln1_gain, ln1_shift, b_query, b_value, b_out, ln2_gain, ln2_shift, b_proj)
    small = jnp.concatenate(
        vectors
        + (
            b_fc,
            high.reshape(-1).astype(BF),
            (doc_lengths - 16 * high).reshape(-1).astype(BF),
        )
    )
    small = lax.all_gather(small, ALL, axis=0, tiled=False)
    whole = [small[:, i * rows : (i + 1) * rows].reshape(-1).astype(F32) for i in range(8)]
    at = 8 * rows
    bias_fc = small[:, at : at + hidden_rows].reshape(n_seq, n_blk, n_uly, hidden_rows)
    bias_fc = lax.dynamic_slice(
        bias_fc, (here_seq, 0, here_uly, 0), (1, n_blk, 1, hidden_rows)
    ).reshape(ff_share).astype(F32)
    at += hidden_rows
    count = doc_lengths.size
    digits = small[:: n_blk * n_uly, at:].astype(F32).astype(jnp.int32)
    lengths = (16 * digits[:, :count] + digits[:, count:]).reshape(n_seq, *doc_lengths.shape)
    gain_one, shift_one, bias_q, bias_v, bias_out, gain_two, shift_two, bias_proj = whole
    mine = lambda v: lax.dynamic_slice(v, (here * share,), (share,))
    bias_q, bias_v = mine(bias_q), mine(bias_v)

    def to_planes(block):
        block = block.reshape(n_blk // sharing, held, sharing, part, width)
        block = block.transpose(0, 2, 1, 3, 4).reshape(n_blk, held * part, width)
        moved = lax.all_to_all(block, "blk", split_axis=0, concat_axis=0, tiled=True)
        return moved.reshape(n_rows, width)

    def from_planes(block):
        block = block.reshape(n_blk, held * part, width)
        moved = lax.all_to_all(block, "blk", split_axis=0, concat_axis=0, tiled=True)
        moved = moved.reshape(n_blk // sharing, sharing, held, part, width)
        return moved.transpose(0, 2, 1, 3, 4).reshape(seqs, tok, width)

    def columns_in(matrix, cols):
        moved = lax.all_to_all(matrix, PLANE, split_axis=1, concat_axis=0, tiled=True)
        moved = lax.all_gather(
            moved.reshape(plane * rows, cols), "blk", axis=0, tiled=True
        )
        moved = moved.reshape(n_blk, n_seq, n_uly * rows, cols)
        return moved.transpose(1, 0, 2, 3).reshape(width, cols)

    def columns_out(grad, cols):
        grad = grad.astype(BF).reshape(n_seq, n_blk, n_uly * rows, cols)
        grad = grad.transpose(1, 0, 2, 3).reshape(n_blk * plane * rows, cols)
        grad = lax.psum_scatter(grad, "blk", scatter_dimension=0, tiled=True)
        grad = grad.reshape(plane, rows, cols)
        return lax.all_to_all(grad, PLANE, split_axis=0, concat_axis=0, tiled=True)

    tokens = to_planes(inputs).astype(F32)
    qkv = jnp.stack([w.reshape(rows, plane, share) for w in (w_query, w_key, w_value)], axis=2)
    qkv = columns_in(qkv.reshape(rows, plane, 3 * share), 3 * share)
    out_part = lax.all_gather(w_out, "blk", axis=0, tiled=True)
    out_part = out_part.reshape(n_uly, n_blk // n_uly, rows, width)
    out_part = lax.all_to_all(out_part, "uly", split_axis=0, concat_axis=0, tiled=True)
    out_part = out_part.transpose(1, 0, 2, 3).reshape(share, width)
    fc = w_fc.reshape(rows, n_seq, n_blk, n_uly, hidden_rows).transpose(0, 1, 3, 2, 4)
    fc = columns_in(fc.reshape(rows, plane, ff_share), ff_share)
    proj = lax.all_gather(w_proj, "blk", axis=0, tiled=True)

    normed_value, norm_back_one = jax.vjp(layer_norm, tokens, gain_one, shift_one)
    normed = gather_plane(normed_value.astype(BF))
    grad_out = to_planes(cotangent)
    grad_all = gather_plane(grad_out)

    made = product(normed, qkv)
    queries = ((made[:, :share] + bias_q) * scale).astype(BF)
    keys = made[:, share : 2 * share].astype(BF)
    values = (made[:, 2 * share :] + bias_v).astype(BF)

    groups = [
        [g * sharing + i for i in range(sharing)] for g in range(n_blk // sharing)
    ]
    pairs = n_seq * held * heads // sharing
    length = n_blk * n_uly * tok

    def to_heads(matrix):
        matrix = matrix.reshape(n_seq, n_uly, n_blk, held, part, heads, HD)
        matrix = matrix.transpose(0, 3, 5, 2, 1, 4, 6)
        matrix = matrix.reshape(n_seq * held * heads, n_blk, n_uly, 1, part, HD)
        if sharing > 1:
            matrix = lax.all_to_all(
                matrix, "blk", split_axis=0, concat_axis=3, axis_index_groups=groups, tiled=True
            )
        return matrix.reshape(pairs, length, HD)

    def from_heads(matrix):
        matrix = matrix.reshape(pairs, n_blk, n_uly, sharing, part, HD)
        if sharing > 1:
            matrix = lax.all_to_all(
                matrix, "blk", split_axis=3, concat_axis=0, axis_index_groups=groups, tiled=True
            )
        matrix = matrix.reshape(n_seq, held, heads, n_blk, n_uly, part, HD)
        return matrix.transpose(0, 4, 3, 1, 5, 2, 6).reshape(plane * n_rows, share)

    hq, hk, hv = to_heads(queries), to_heads(keys), to_heads(values)
    turn = here_blk % sharing
    pair_at = turn * pairs + jnp.arange(pairs)
    seq_of = pair_at // (held * heads)
    held_of = (pair_at // heads) % held
    which = (here_blk // sharing) * held + held_of
    own_lengths = lengths[seq_of, which]
    first = own_lengths[:, 0:1]
    second = first + own_lengths[:, 1:2]
    position = jnp.arange(length, dtype=jnp.int32)[None]
    doc = (position >= first).astype(jnp.int32) + (position >= second).astype(jnp.int32)
    allowed = (doc[:, :, None] == doc[:, None, :]) & (
        position[:, None, :] <= position[:, :, None]
    )

    def head_forward(args):
        q, k, v, ok = args
        scores = jnp.where(ok, against(q, k), NEGATIVE)
        top = jnp.max(scores, axis=1, keepdims=True)
        powered = jnp.exp(scores - top)
        total = jnp.sum(powered, axis=1, keepdims=True)
        result = product(powered.astype(BF), v) / total
        return result, top + jnp.log(total)

    attended, log_total = lax.map(head_forward, (hq, hk, hv, allowed))
    attended_low = from_heads(attended.astype(BF))
    branch = scatter_plane(product(attended_low, out_part))
    hidden = tokens + branch.astype(F32) + bias_out
    normed_two_value, norm_back_two = jax.vjp(layer_norm, hidden, gain_two, shift_two)
    normed_two = gather_plane(normed_two_value.astype(BF))
    inner = product(normed_two, fc) + bias_fc
    gelu_value, gelu_back = jax.vjp(gelu_tanh, inner)
    active = gelu_value.astype(BF)
    fed = scatter_plane(product(active, proj))
    result = from_planes((hidden + fed.astype(F32) + bias_proj).astype(BF))

    grad_b_proj = jnp.sum(grad_out.astype(F32), axis=0)
    grad_inner = gelu_back(against(grad_all, proj))[0].astype(BF)
    grad_w_proj = lax.psum_scatter(
        transposed(active, grad_all).astype(BF), "blk", scatter_dimension=0, tiled=True
    ).astype(F32)
    grad_b_fc = jnp.sum(grad_inner.astype(F32), axis=0)
    grad_w_fc = columns_out(transposed(normed_two, grad_inner), ff_share)
    grad_w_fc = grad_w_fc.reshape(n_seq, n_uly, rows, n_blk, hidden_rows)
    grad_w_fc = grad_w_fc.transpose(2, 0, 3, 1, 4).reshape(rows, -1).astype(F32)
    grad_normed_two = scatter_plane(against(grad_inner, fc)).astype(F32)
    hidden_part, grad_ln2_gain, grad_ln2_shift = norm_back_two(grad_normed_two)
    grad_hidden = grad_out.astype(F32) + hidden_part
    grad_branch = grad_hidden.astype(BF)
    grad_b_out = jnp.sum(grad_branch.astype(F32), axis=0)
    branch_all = gather_plane(grad_branch)
    grad_w_out = transposed(attended_low, branch_all).astype(BF)
    grad_w_out = grad_w_out.reshape(n_blk // n_uly, n_uly, rows, width).transpose(1, 0, 2, 3)
    grad_w_out = lax.all_to_all(grad_w_out, "uly", split_axis=0, concat_axis=0, tiled=True)
    grad_w_out = lax.psum_scatter(
        grad_w_out.reshape(n_blk * rows, width), "blk", scatter_dimension=0, tiled=True
    ).astype(F32)
    grad_heads = to_heads(against(branch_all, out_part).astype(BF))

    def head_backward(args):
        q, k, v, ok, grad, kept, logs = args
        dots = jnp.sum(grad.astype(F32) * kept, axis=1, keepdims=True)
        scores = jnp.where(ok, against(q, k), NEGATIVE)
        chances = jnp.exp(scores - logs)
        grad_v = transposed(chances.astype(BF), grad)
        grad_scores = (chances * (against(grad, v) - dots)).astype(BF)
        grad_q = product(grad_scores, k)
        grad_k = transposed(grad_scores, q)
        return grad_q.astype(BF), grad_k.astype(BF), grad_v.astype(BF)

    backs = lax.map(head_backward, (hq, hk, hv, allowed, grad_heads, attended, log_total))
    query_back, key_back, value_back = (from_heads(b) for b in backs)
    grad_b_query = jnp.sum(query_back.astype(F32), axis=0) * scale
    grad_b_value = jnp.sum(value_back.astype(F32), axis=0)
    grad_normed = (
        against(query_back, qkv[:, :share]) * scale
        + against(key_back, qkv[:, share : 2 * share])
        + against(value_back, qkv[:, 2 * share :])
    )
    grad_qkv = jnp.concatenate(
        [
            transposed(normed, query_back) * scale,
            transposed(normed, key_back),
            transposed(normed, value_back),
        ],
        axis=1,
    )
    grad_qkv = columns_out(grad_qkv, 3 * share).reshape(plane, rows, 3, share)
    grad_qkv = grad_qkv.transpose(2, 1, 0, 3).reshape(3, rows, width).astype(F32)
    grad_normed = scatter_plane(grad_normed).astype(F32)
    token_part, grad_ln1_gain, grad_ln1_shift = norm_back_one(grad_normed)
    grad_inputs = from_planes((grad_hidden + token_part).astype(BF))

    def widened(vector):
        return lax.dynamic_update_slice(jnp.zeros((width,), F32), vector, (here * share,))

    parts = (
        grad_ln1_gain,
        grad_ln1_shift,
        widened(grad_b_query),
        widened(grad_b_value),
        grad_b_out,
        grad_ln2_gain,
        grad_ln2_shift,
        grad_b_proj,
    )
    wide_fc = lax.dynamic_update_slice(
        jnp.zeros((n_seq, n_blk, n_uly, hidden_rows), F32),
        grad_b_fc.reshape(1, n_blk, 1, hidden_rows),
        (here_seq, 0, here_uly, 0),
    ).reshape(devices, hidden_rows)
    sums = jnp.concatenate([p.reshape(devices, rows) for p in parts] + [wide_fc], axis=1)
    sums = lax.psum_scatter(
        sums.reshape(-1), ALL, scatter_dimension=0, tiled=True
    )
    each = [sums[i * rows : (i + 1) * rows] for i in range(8)]
    return (
        result,
        grad_inputs,
        each[0],
        each[1],
        grad_qkv[0],
        each[2],
        grad_qkv[1],
        grad_qkv[2],
        each[3],
        grad_w_out,
        each[4],
        each[5],
        each[6],
        grad_w_fc,
        sums[8 * rows :],
        grad_w_proj,
        each[7],
    )


def solution(mesh):
    tokens = P("seq", ("blk", "uly"), None)
    vector = P(ALL)
    matrix = P(ALL, None)
    return jax.shard_map(
        on_device,
        mesh=mesh,
        in_specs=(
            tokens, P("seq", None), vector, vector, matrix, vector, matrix, matrix, vector,
            matrix, vector, vector, vector, matrix, vector, matrix, vector, tokens,
        ),
        out_specs=(
            tokens, tokens, vector, vector, matrix, vector, matrix, matrix, vector,
            matrix, vector, vector, vector, matrix, vector, matrix, vector,
        ),
        check_vma=False,
    )
```

time: 3720 us -> 1380 us (0.37)
  waiting for transfers between devices: 3100 us -> 771 us
  blocking collectives: 109 us -> 175 us
    reduce_scatter x6 -> x8, waiting for transfers between devices: 2150 us -> 273 us  [the longest x4 176 us: scatter_plane(): lax.psum_scatter(rows.astype(BF), PLANE, scatter_dimension=0, tiled=True)]
    ppermute x11 -> x0, waiting for transfers between devices: 624 us -> none  [the longest x7 460 us: passed_along(): return lax.ppermute(block, axis, route)]
    unnamed x14 -> x18, waiting for transfers between devices: 13.1 us -> 122 us
    all_to_all x1 -> x4, blocking collectives: 17.7 us -> 110 us  [the longest x1 56.3 us: to_planes(): lax.all_to_all(block, 'blk', split_axis=0, concat_axis=0, tiled=True)]
    dot_general x34 -> x12, matrix products: 120 us -> 64.6 us  [product(): return jnp.dot(left_side, right_side, preferred_element_type=F32)]
    all_gather x1 -> x0, blocking collectives: 50 us -> none  [on_device(): lax.all_gather(b_fc, ('seq', 'blk', 'uly'), axis=0, tiled=True)]
    while x49 -> x16, local copies, waits for them, and re-layouts: 38.7 us -> 0.03 us
    dot_general x6 -> x18, matrix products: 58.6 us -> 92.4 us  [against(): lax.dot_general(left_side, right_side, (((1,), (1,)), ((), ())), preferre...]
  transfers between devices with their start and end apart: 31 -> 23, of which waited for: 26 -> 16; matrix products, arithmetic and copies ran while one was open for 7% -> 24% of each run, Pallas kernels for 0% -> 0%
where the time goes in v1:
time: 1380 us
  waiting for transfers between devices  771 us (56%)
  matrix products  232 us (17%)
  blocking collectives  175 us (13%)
  local copies, waits for them, and re-layouts  98 us (7%)
  other arithmetic  55.1 us (4%)
  starting transfers between devices  27.5 us (2%)
  between operations  15.2 us (1%)
    all_gather x4, waiting for transfers between devices, gather_plane(): return lax.all_gather(rows, PLANE, axis=0, tiled=True)  206 us
    reduce_scatter x4, waiting for transfers between devices, scatter_plane(): lax.psum_scatter(rows.astype(BF), PLANE, scatter_dimension=0, tiled=True)  176 us
    unnamed x18, waiting for transfers between devices  122 us
    dot_general x18, matrix products, against(): lax.dot_general(left_side, right_side, (((1,), (1,)), ((), ())), preferre...  92.4 us
    reduce_scatter x1, waiting for transfers between devices, on_device(): lax.psum_scatter(transposed(active, grad_all).astype(BF), 'blk', scatter_...  79.8 us
    dot_general x14, matrix products, transposed(): lax.dot_general(left_side, right_side, (((0,), (0,)), ((), ())), preferre...  75.5 us
    unnamed x1, blocking collectives  65.8 us
    all_gather x1, waiting for transfers between devices, on_device(): proj = lax.all_gather(w_proj, 'blk', axis=0, tiled=True)  65.4 us
  transfers between devices with their start and end apart: 23, of which 16 were waited for; matrix products, arithmetic and copies ran while one was open for 24% of the time, Pallas kernels for 0%

profile of v1, /device:TPU:8, one launch (start us, length us, event | category | flops | bytes accessed | tf_op | source)
XLA Modules:
  0.0 1375.3 jit_solution(14960765163011419145)
XLA Ops:
  15.1 16.2 %all_to_all.70 = bf16[64,8,768]{2,0,1:T(8,128)(2,1)} all-to-all(bf16[64,8,768]{2,0,1:T(8,128)(2,1)S(1)} %copy.100), channel_id=1, replica_groups=mesh['seq'=2,'blk'=4,'uly'=4] {'seq','uly'}, dimensions={1} | all-to-all | bytes 1572864 | tf_op jit(solution)/shard_map/all_to_all | solution.py:127
  31.3 5.3 all-to-all-start
  37.2 65.8 %all-reduce.1 = bf16[25344]{0:T(1024)(128)(2,1)S(1)} all-reduce(bf16[25344]{0:T(1024)(128)(2,1)S(1)} %dynamic-update-slice), channel_id=2, replica_groups=mesh['seq'=2,'blk'=4,'uly'=4] {'seq','blk','uly'}, use_global_device_ids=true, to_apply=%add.1 | all-reduce | flops 25344 | bytes 101376
  108.0 4.3 compare_and_fusion
  112.3 4.3 all-to-all-start.2
  120.5 54.8 %all-gather.10.cloned.1.call-done = bf16[2048,2048]{1,0:T(8,128)(2,1)} async-done(((bf16[256,2048]{1,0:T(8,128)(2,1)}), bf16[2048,2048]{1,0:T(8,128)(2,1)}) %all-gather.10.cloned.1.call-update) | async-done | bytes 8388624 | tf_op jit(solution)/shard_map/all_gather | solution.py:45
  175.3 10.2 fusion.127
  194.2 28.3 %while.26 = (s32[]{:T(128)}, f32[4,1024,128]{2,1,0:T(8,128)}, f32[4,1024,1]{1,2,0:T(1,128)S(1)}, pred[4,1024,1024]{2,1,0:T(32,128)(4,1)}, bf16[4,1024,128]{2,1,0...) while((s32[]{:T(128)}, f32[4,1024,128]{2,1,0:T(8,128)}, ...), condition=%wide.region_5.6_spmd, body=%wide.region_2.5_spmd.sunk | while | flops 545389568 | bytes 21276772 | solution.py:211
  226.1 7.2 convolution_convert_fusion.4
  237.7 18.5 %all_to_all.71 = bf16[64,8,1024]{2,0,1:T(8,128)(2,1)} all-to-all(bf16[64,8,1024]{2,0,1:T(8,128)(2,1)S(1)} %copy.108), channel_id=1, replica_groups=mesh['seq'=2,'blk'=4,'uly'=4] {'seq','uly'}, dimensions={1} | all-to-all | bytes 2097152 | tf_op jit(solution)/shard_map/all_to_all | solution.py:127
  256.4 48.4 %reduce-scatter.9.cloned.1.call-done = bf16[256,2048]{1,0:T(8,128)(2,1)} async-done(((bf16[2048,2048]{1,0:T(8,128)(2,1)}), bf16[256,2048]{1,0:T(8,128)(2,1)}) %reduce-scatter.9.cloned.1.call-update) | async-done | bytes 1048592 | tf_op jit(solution)/shard_map/reduce_scatter | solution.py:49
  310.9 56.3 %all_to_all.72 = bf16[4,64,2048]{2,1,0:T(8,128)(2,1)} all-to-all(bf16[4,64,2048]{2,1,0:T(8,128)(2,1)S(1)} %copy-done.20), channel_id=1, replica_groups=mesh['seq'=2,'blk'=4,'uly'=4] {'blk'}, dimensions={0} | all-to-all | bytes 2097152 | tf_op jit(solution)/shard_map/all_to_all | solution.py:117
  367.3 38.1 %all-gather.18.cloned.1.call-done = bf16[2048,1024]{1,0:T(8,128)(2,1)} async-done(((bf16[512,1024]{1,0:T(8,128)(2,1)}), bf16[2048,1024]{1,0:T(8,128)(2,1)}) %all-gather.18.cloned.1.call-update) | async-done | bytes 4194320 | tf_op jit(solution)/shard_map/all_gather | solution.py:128
  405.4 4.6 copy.109
  410.0 54.0 %all-gather.16.cloned.1.call-done = bf16[2048,2048]{1,0:T(8,128)(2,1)} async-done(((bf16[256,2048]{1,0:T(8,128)(2,1)}), bf16[2048,2048]{1,0:T(8,128)(2,1)}) %all-gather.16.cloned.1.call-update) | async-done | bytes 8388624 | tf_op jit(solution)/shard_map/all_gather | solution.py:45
  464.0 14.4 %fusion.128 = f32[2048,1024]{1,0:T(8,128)} fusion(bf16[2048,2048]{1,0:T(8,128)(2,1)} %all-gather.16.cloned.1.call-done, bf16[2048,1024]{1,0:T(8,128)(2,1)} %bitcast.342), kind=kOutput, calls=%fused_computation.207 | convolution fusion | flops 8589934592 | bytes 20971520 | tf_op jit(solution)/shard_map/dot_general | solution.py:29
  478.4 65.4 %all-gather.20.cloned.1.call-done = bf16[1024,2048]{1,0:T(8,128)(2,1)} async-done(((bf16[256,2048]{1,0:T(8,128)(2,1)}), bf16[1024,2048]{1,0:T(8,128)(2,1)}) %all-gather.20.cloned.1.call-update) | async-done | bytes 4194320 | tf_op jit(solution)/shard_map/all_gather | solution.py:150
  543.8 57.6 %all-gather.22.cloned.1.call-done = bf16[2048,2048]{1,0:T(8,128)(2,1)} async-done(((bf16[256,2048]{1,0:T(8,128)(2,1)}), bf16[2048,2048]{1,0:T(8,128)(2,1)}) %all-gather.22.cloned.1.call-update) | async-done | bytes 8388624 | tf_op jit(solution)/shard_map/all_gather | solution.py:45
  601.4 20.8 %convert_reduce_fusion = (f32[1024]{0:T(1024)}, bf16[2048,1024]{1,0:T(8,128)(2,1)S(1)}) fusion(f32[2048,1024]{1,0:T(8,128)} %fusion.128, f32[1024]{0:T(1024)S(1)} %bitcast.375, bf16[2048,2048]{1,0:T(8,128)(2,1)} %all-gather.22.cloned.1.call-done, bf16[1024,2048]{1,0:T(8,128)(2,1)} %all-gather.20.cloned.1.call-done), kind=kOutput, calls=%fused_computation.73 | convolution fusion | flops 8638168064 | bytes 25174016 | tf_op jit(solution)/shard_map/dot_general | solution.py:39
  624.2 11.1 convolution_convert_fusion.2
  635.3 15.6 %convolution_convert_fusion.3 = bf16[2048,2048]{1,0:T(8,128)(2,1)} fusion(bf16[1024,2048]{1,0:T(8,128)(2,1)} %all-gather.20.cloned.1.call-done, f32[2048,1024]{1,0:T(8,128)} %fusion.128, f32[1024]{0:T(1024)S(1)} %bitcast.376), kind=kOutput, calls=%fused_computation.76 | convolution fusion | flops 8615100416 | bytes 20975616 | tf_op jit(solution)/shard_map/dot_general | solution.py:29
  651.7 55.0 %reduce-scatter.13.cloned.1.call-done = bf16[256,2048]{1,0:T(8,128)(2,1)} async-done(((bf16[2048,2048]{1,0:T(8,128)(2,1)}), bf16[256,2048]{1,0:T(8,128)(2,1)}) %reduce-scatter.13.cloned.1.call-update) | async-done | bytes 1048592 | tf_op jit(solution)/shard_map/reduce_scatter | solution.py:49
  709.0 72.3 %reduce-scatter.11.cloned.1.call-done = bf16[256,2048]{1,0:T(8,128)(2,1)} async-done(((bf16[2048,2048]{1,0:T(8,128)(2,1)}), bf16[256,2048]{1,0:T(8,128)(2,1)}) %reduce-scatter.11.cloned.1.call-update) | async-done | bytes 1048592 | tf_op jit(solution)/shard_map/reduce_scatter | solution.py:49
  787.9 12.9 convolution_convert_fusion.6
  803.3 39.0 %all-gather.24.cloned.1.call-done = bf16[2048,2048]{1,0:T(8,128)(2,1)} async-done(((bf16[256,2048]{1,0:T(8,128)(2,1)}), bf16[2048,2048]{1,0:T(8,128)(2,1)}) %all-gather.24.cloned.1.call-update) | async-done | bytes 8388624 | tf_op jit(solution)/shard_map/all_gather | solution.py:45
  842.3 7.0 convolution_convert_fusion.8
  854.0 49.0 %while.27 = (s32[]{:T(128)}, bf16[4,1024,128]{2,1,0:T(8,128)(2,1)}, bf16[4,1024,128]{2,1,0:T(8,128)(2,1)}, bf16[4,1024,128]{2,1,0:T(8,128)(2,1)}, pred[4,1024,10...) while((s32[]{:T(128)}, bf16[4,1024,128]{2,1,0:T(8,128)(2,1)}, ...), condition=%wide.region_15.16_spmd, body=%wide.region_13.15_spmd.sunk | while | flops 1351351296 | bytes 45381820 | solution.py:257
  909.3 8.1 fusion.96
  917.4 8.1 fusion.99
  925.6 15.7 %add_convert_fusion = bf16[2048,2048]{1,0:T(8,128)(2,1)} fusion(f32[2048,2048]{1,0:T(8,128)} %fusion.96, f32[2048,2048]{1,0:T(8,128)} %fusion.99, bf16[2048,768]{1,0:T(8,128)(2,1)} %bitcast.323, bf16[256,8,2,128]{3,2,1,0:T(2,128)(2,1)S(1)} %bitcast.333), kind=kOutput, calls=%fused_computation.62 | convolution fusion | flops 2164260864 | bytes 44040192 | tf_op jit(solution)/shard_map/dot_general | solution.py:39
  941.3 12.8 copy.130
  954.1 8.3 fusion.71
  964.7 6.5 convolution_convert_fusion.9
  971.2 6.1 convolution_convert_fusion.10
  979.1 4.7 copy.119
  983.9 16.8 %convolution_convert_fusion.5 = bf16[1024,2048]{1,0:T(8,128)(2,1)} fusion(bf16[2048,2048]{1,0:T(8,128)(2,1)} %all-gather.22.cloned.1.call-done, f32[2048,1024]{1,0:T(8,128)} %fusion.128, f32[1024]{0:T(1024)S(1)} %bitcast.377), kind=kOutput, calls=%fused_computation.79 | convolution fusion | flops 8613003264 | bytes 20975616 | tf_op jit(solution)/shard_map/dot_general | solution.py:33
  1000.8 4.4 all-to-all-start.9
  1005.2 6.8 convolution_convert_fusion.7
  1012.0 11.6 all-to-all-done.9
  1023.6 18.8 %all_to_all.73 = bf16[4,1,64,2048]{3,2,1,0:T(8,128)(2,1)} all-to-all(bf16[4,1,64,2048]{3,2,1,0:T(8,128)(2,1)} %bitcast.339), channel_id=1, replica_groups=mesh['seq'=2,'blk'=4,'uly'=4] {'uly'}, dimensions={0} | all-to-all | bytes 2097152 | tf_op jit(solution)/shard_map/all_to_all | solution.py:240
  1042.4 5.1 all-to-all-start.4
  1052.4 46.7 %all-to-all-done.4 = bf16[4,64,2048]{2,1,0:T(8,128)(2,1)} async-done(((bf16[4,64,2048]{2,1,0:T(8,128)(2,1)}), bf16[4,64,2048]{2,1,0:T(8,128)(2,1)}, u32[]{:S(2)}, u32[]{:S(2)}) %all-to-all-start.4) | async-done | bytes 1048608 | tf_op jit(solution)/shard_map/all_to_all | solution.py:122
  1099.1 7.1 reduce-scatter.17.cloned.1.call-done
  1106.2 4.2 all-to-all-start.7
  1114.0 9.0 all-to-all-done.7
  1126.9 79.8 %reduce-scatter.23.cloned.1.call-done = bf16[256,2048]{1,0:T(8,128)(2,1)} async-done(((bf16[1024,2048]{1,0:T(8,128)(2,1)}), bf16[256,2048]{1,0:T(8,128)(2,1)}) %reduce-scatter.23.cloned.1.call-update) | async-done | bytes 1048592 | tf_op jit(solution)/shard_map/reduce_scatter | solution.py:225
  1222.9 10.2 reduce-scatter.19.cloned.1.call-done
  1243.6 119.5 %all-reduce.5.cloned.1.call-done = f32[24576]{0:T(1024)} async-done(((f32[24576]{0:T(1024)}), f32[24576]{0:T(1024)}) %all-reduce.5.cloned.1.call-update) | async-done | bytes 98320
  (321 shorter events, 189.9 us)
Async XLA Ops:
  7.2 105.1 %all-gather.14.cloned.1.call-start = ((), (), s32[]{:S(2)}) async-start(), calls=%async_computation.20 | async-start | bytes 1310720 | tf_op jit(solution)/shard_map/all_gather | solution.py:144
  7.9 108.7 %all-gather.12.cloned.1.call-start = ((), (), s32[]{:S(2)}) async-start(), calls=%async_computation.19 | async-start | bytes 3932160 | tf_op jit(solution)/shard_map/all_gather | solution.py:128
  13.9 22.8 %copy-start.32 = (s32[4,3]{1,0:T(4,128)S(1)}, s32[4,3]{1,0:T(4,128)}, u32[]{:S(2)}) copy-start(s32[4,3]{1,0:T(4,128)} %param.23) | copy-start | bytes 148
  13.9 22.9 %copy-start.33 = (bf16[64]{0:T(256)(128)(2,1)S(1)}, bf16[64]{0:T(256)(128)(2,1)}, u32[]{:S(2)}) copy-start(bf16[64]{0:T(256)(128)(2,1)} %param.24) | copy-start | bytes 388
  13.9 22.9 %copy-start.34 = (bf16[64]{0:T(256)(128)(2,1)S(1)}, bf16[64]{0:T(256)(128)(2,1)}, u32[]{:S(2)}) copy-start(bf16[64]{0:T(256)(128)(2,1)} %param.25) | copy-start | bytes 388
  13.9 22.9 %copy-start.35 = (bf16[64]{0:T(256)(128)(2,1)S(1)}, bf16[64]{0:T(256)(128)(2,1)}, u32[]{:S(2)}) copy-start(bf16[64]{0:T(256)(128)(2,1)} %param.27) | copy-start | bytes 388
  13.9 22.9 %copy-start.36 = (bf16[64]{0:T(256)(128)(2,1)S(1)}, bf16[64]{0:T(256)(128)(2,1)}, u32[]{:S(2)}) copy-start(bf16[64]{0:T(256)(128)(2,1)} %param.30) | copy-start | bytes 388
  13.9 22.9 %copy-start.37 = (bf16[64]{0:T(256)(128)(2,1)S(1)}, bf16[64]{0:T(256)(128)(2,1)}, u32[]{:S(2)}) copy-start(bf16[64]{0:T(256)(128)(2,1)} %param.32) | copy-start | bytes 388
  13.9 22.9 %copy-start.38 = (bf16[64]{0:T(256)(128)(2,1)S(1)}, bf16[64]{0:T(256)(128)(2,1)}, u32[]{:S(2)}) copy-start(bf16[64]{0:T(256)(128)(2,1)} %param.33) | copy-start | bytes 388
  13.9 22.9 %copy-start.39 = (bf16[64]{0:T(256)(128)(2,1)S(1)}, bf16[64]{0:T(256)(128)(2,1)}, u32[]{:S(2)}) copy-start(bf16[64]{0:T(256)(128)(2,1)} %param.34) | copy-start | bytes 388
  14.0 22.9 %copy-start.40 = (bf16[64]{0:T(256)(128)(2,1)S(1)}, bf16[64]{0:T(256)(128)(2,1)}, u32[]{:S(2)}) copy-start(bf16[64]{0:T(256)(128)(2,1)} %param.38) | copy-start | bytes 388
  14.0 22.9 %copy-start.41 = (bf16[256]{0:T(256)(128)(2,1)S(1)}, bf16[256]{0:T(256)(128)(2,1)}, u32[]{:S(2)}) copy-start(bf16[256]{0:T(256)(128)(2,1)} %param.36) | copy-start | bytes 1540
  31.3 72.7 %all-to-all-start = ((bf16[4,64,2048]{2,1,0:T(8,128)(2,1)}), bf16[4,64,2048]{2,1,0:T(8,128)(2,1)S(1)}, u32[]{:S(2)}, u32[]{:S(2)}) async-start(bf16[4,64,2048]{2,1,0:T(8,128)(2,1)} %param.22), calls=%async_computation | async-start | bytes 2097152 | tf_op jit(solution)/shard_map/all_to_all | solution.py:117
  36.6 138.7 %all-gather.10.cloned.1.call-start = ((), (), s32[]{:S(2)}) async-start(), calls=%async_computation.18 | async-start | bytes 9437184 | tf_op jit(solution)/shard_map/all_gather | solution.py:45
  103.9 8.4 copy-start.22
  104.8 7.5 copy-start.27
  112.3 113.8 %all-to-all-start.2 = ((bf16[4,1,64,2048]{3,2,1,0:T(8,128)(2,1)}), bf16[4,1,64,2048]{3,2,1,0:T(8,128)(2,1)}, u32[]{:S(2)}, u32[]{:S(2)}) async-start(bf16[4,1,64,2048]{3,2,1,0:T(8,128)(2,1)} %bitcast.363), calls=%async_computation.2 | async-start | bytes 2097152 | tf_op jit(solution)/shard_map/all_to_all | solution.py:146
  116.6 188.2 %reduce-scatter.9.cloned.1.call-start = ((), (), s32[]{:S(2)}) async-start(), calls=%async_computation.21 | async-start | bytes 9437184 | tf_op jit(solution)/shard_map/reduce_scatter | solution.py:49
  222.5 10.8 copy-start.8
  226.1 7.2 copy-start.4
  233.3 172.1 %all-gather.18.cloned.1.call-start = ((), (), s32[]{:S(2)}) async-start(), calls=%async_computation.23 | async-start | bytes 5242880 | tf_op jit(solution)/shard_map/all_gather | solution.py:128
  256.2 207.8 %all-gather.16.cloned.1.call-start = ((), (), s32[]{:S(2)}) async-start(), calls=%async_computation.22 | async-start | bytes 9437184 | tf_op jit(solution)/shard_map/all_gather | solution.py:45
  310.1 233.7 %all-gather.20.cloned.1.call-start = ((), (), s32[]{:S(2)}) async-start(), calls=%async_computation.24 | async-start | bytes 5242880 | tf_op jit(solution)/shard_map/all_gather | solution.py:150
  310.9 290.6 %all-gather.22.cloned.1.call-start = ((), (), s32[]{:S(2)}) async-start(), calls=%async_computation.26 | async-start | bytes 9437184 | tf_op jit(solution)/shard_map/all_gather | solution.py:45
  367.2 339.5 %reduce-scatter.13.cloned.1.call-start = ((), (), s32[]{:S(2)}) async-start(), calls=%async_computation.27 | async-start | bytes 9437184 | tf_op jit(solution)/shard_map/reduce_scatter | solution.py:49
  601.4 22.8 %copy-start.15 = (bf16[4,2,256,1024]{3,2,0,1:T(8,128)(2,1)S(1)}, bf16[4,2,256,1024]{3,2,0,1:T(8,128)(2,1)}, u32[]{:S(2)}) copy-start(bf16[4,2,256,1024]{3,2,0,1:T(8,128)(2,1)} %copy.109) | copy-start | bytes 12582916
  635.3 146.1 %reduce-scatter.11.cloned.1.call-start = ((), (), s32[]{:S(2)}) async-start(), calls=%async_computation.25 | async-start | bytes 9437184 | tf_op jit(solution)/shard_map/reduce_scatter | solution.py:49
  650.9 191.4 %all-gather.24.cloned.1.call-start = ((), (), s32[]{:S(2)}) async-start(), calls=%async_computation.28 | async-start | bytes 9437184 | tf_op jit(solution)/shard_map/all_gather | solution.py:45
  709.0 77.3 %copy-start.1 = (bf16[4,64,2048]{2,1,0:T(8,128)(2,1)S(1)}, bf16[4,64,2048]{2,1,0:T(8,128)(2,1)}, u32[]{:S(2)}) copy-start(bf16[4,64,2048]{2,1,0:T(8,128)(2,1)} %all_to_all.72) | copy-start | bytes 3145732
  787.8 213.0 %reduce-scatter.21.cloned.1.call-start = ((), (), s32[]{:S(2)}) async-start(), calls=%async_computation.32 | async-start | bytes 5242880 | tf_op jit(solution)/shard_map/reduce_scatter | solution.py:137
  803.2 244.9 %reduce-scatter.15.cloned.1.call-start = ((), (), s32[]{:S(2)}) async-start(), calls=%async_computation.29 | async-start | bytes 9437184 | tf_op jit(solution)/shard_map/reduce_scatter | solution.py:49
  905.5 11.9 copy-start.14
  909.3 8.1 copy-start.12
  941.2 165.0 %reduce-scatter.17.cloned.1.call-start = ((), (), s32[]{:S(2)}) async-start(), calls=%async_computation.30 | async-start | bytes 3932160 | tf_op jit(solution)/shard_map/reduce_scatter | solution.py:137
  964.7 6.5 copy-start.13
  983.9 222.9 %reduce-scatter.23.cloned.1.call-start = ((), (), s32[]{:S(2)}) async-start(), calls=%async_computation.33 | async-start | bytes 5242880 | tf_op jit(solution)/shard_map/reduce_scatter | solution.py:225
  1000.8 22.8 %all-to-all-start.9 = ((bf16[8,64,1024]{2,1,0:T(8,128)(2,1)}), bf16[8,64,1024]{2,1,0:T(8,128)(2,1)}, u32[]{:S(2)}, u32[]{:S(2)}) async-start(bf16[8,64,1024]{2,1,0:T(8,128)(2,1)} %bitcast.364), calls=%async_computation.16 | async-start | bytes 2097152 | tf_op jit(solution)/shard_map/all_to_all | solution.py:139
  1012.0 36.1 %copy-start.23 = (f32[2048]{0:T(1024)S(1)}, f32[2048]{0:T(1024)}, u32[]{:S(2)}) copy-start(f32[2048]{0:T(1024)} %copy-done.22) | copy-start | bytes 24580
  1012.0 36.1 %copy-start.26 = (f32[256]{0:T(256)S(1)}, f32[256]{0:T(256)}, u32[]{:S(2)}) copy-start(f32[256]{0:T(256)} %copy-done.25) | copy-start | bytes 3076
  1012.0 38.1 %copy-start.30 = (f32[256]{0:T(256)S(1)}, f32[256]{0:T(256)}, u32[]{:S(2)}) copy-start(f32[256]{0:T(256)} %copy-done.29) | copy-start | bytes 3076
  1012.0 38.1 %copy-start.28 = (f32[256]{0:T(256)S(1)}, f32[256]{0:T(256)}, u32[]{:S(2)}) copy-start(f32[256]{0:T(256)} %copy-done.27) | copy-start | bytes 3076
  1042.4 56.8 %all-to-all-start.4 = ((bf16[4,64,2048]{2,1,0:T(8,128)(2,1)}), bf16[4,64,2048]{2,1,0:T(8,128)(2,1)}, u32[]{:S(2)}, u32[]{:S(2)}) async-start(bf16[4,64,2048]{2,1,0:T(8,128)(2,1)} %bitcast.356), calls=%async_computation.6 | async-start | bytes 2097152 | tf_op jit(solution)/shard_map/all_to_all | solution.py:122
  1047.5 185.6 %reduce-scatter.19.cloned.1.call-start = ((), (), s32[]{:S(2)}) async-start(), calls=%async_computation.31 | async-start | bytes 1310720 | tf_op jit(solution)/shard_map/reduce_scatter | solution.py:241
  1048.1 62.3 %copy-start.11 = (bf16[256,2048]{1,0:T(8,128)(2,1)S(1)}, bf16[256,2048]{1,0:T(8,128)(2,1)}, u32[]{:S(2)}) copy-start(bf16[256,2048]{1,0:T(8,128)(2,1)} %reduce-scatter.15.cloned.1.call-done) | copy-start | bytes 3145732
  1106.2 16.8 %all-to-all-start.7 = ((bf16[8,64,768]{2,1,0:T(8,128)(2,1)}), bf16[8,64,768]{2,1,0:T(8,128)(2,1)}, u32[]{:S(2)}, u32[]{:S(2)}) async-start(bf16[8,64,768]{2,1,0:T(8,128)(2,1)} %bitcast.367), calls=%async_computation.12 | async-start | bytes 1572864 | tf_op jit(solution)/shard_map/all_to_all | solution.py:139
  1110.5 16.4 %copy-start.31 = (f32[1024]{0:T(1024)S(1)}, f32[1024]{0:T(1024)}, u32[]{:S(2)}) copy-start(f32[1024]{0:T(1024)} %get-tuple-element.192) | copy-start | bytes 12292
  1123.1 242.0 %all-to-all-start.6 = ((bf16[4,64,2048]{2,1,0:T(8,128)(2,1)}), bf16[4,64,2048]{2,1,0:T(8,128)(2,1)S(1)}, u32[]{:S(2)}, u32[]{:S(2)}) async-start(bf16[4,64,2048]{2,1,0:T(8,128)(2,1)} %bitcast.357), calls=%async_computation.10 | async-start | bytes 2097152 | tf_op jit(solution)/shard_map/all_to_all | solution.py:122
  1126.6 236.5 %all-reduce.5.cloned.1.call-start = ((), (), s32[]{:S(2)}) async-start(), calls=%async_computation.34 | async-start | bytes 196608
  (24 other events, 84.1 us)
Sparse Core Ops, SparseCore 0:
  9.6 29.0 all-gather.13
  40.2 69.9 all-gather.11
  112.8 62.4 all-gather.9
  233.5 71.2 reduce-scatter.8
  306.3 99.0 all-gather.17
  407.9 56.0 all-gather.15
  465.7 78.1 all-gather.19
  545.9 55.5 all-gather.21
  635.4 71.2 reduce-scatter.12
  710.0 71.2 reduce-scatter.10
  787.9 54.3 all-gather.23
  844.5 76.7 reduce-scatter.20
  941.4 74.6 reduce-scatter.14
  1018.3 87.8 reduce-scatter.16
  1108.5 98.2 reduce-scatter.22
  1208.9 24.1 reduce-scatter.18
  1240.0 123.0 all-reduce.4

commit v2 on v1

v2 whole, which is shorter than its diff:
```python
import functools
import math

import jax
import jax.numpy as jnp
from jax import lax
from jax.experimental import pallas as pl
from jax.experimental.pallas import tpu as pltpu
from jax.sharding import PartitionSpec as P

HD = 128
EPS = 1e-05
NEGATIVE = -1e30
ALL = ("seq", "blk", "uly")
PLANE = ("seq", "uly")
BF = jnp.bfloat16
F32 = jnp.float32
MESH = pl.DeviceIdType.MESH
ANY = pl.BlockSpec(memory_space=pl.ANY)
VMEM = pl.BlockSpec(memory_space=pltpu.VMEM)
MIB = 2**20
CHUNK = 16
TILE = 512


def gelu_tanh(values):
    return jax.nn.gelu(values, approximate=True)


def product(left_side, right_side):
    return jnp.dot(left_side, right_side, preferred_element_type=F32)


def transposed(left_side, right_side):
    return lax.dot_general(
        left_side, right_side, (((0,), (0,)), ((), ())), preferred_element_type=F32
    )


def against(left_side, right_side):
    return lax.dot_general(
        left_side, right_side, (((1,), (1,)), ((), ())), preferred_element_type=F32
    )


def meet(peers):
    barrier = pltpu.get_barrier_semaphore()
    for peer in peers:
        pl.semaphore_signal(barrier, inc=1, device_id=peer, device_id_type=MESH)
    pl.semaphore_wait(barrier, len(peers))


def sender(send, recv):
    def copy(i, source, target, device):
        made = pltpu.make_async_remote_copy(
            src_ref=source,
            dst_ref=target,
            send_sem=send.at[i],
            recv_sem=recv.at[i],
            device_id=device,
            device_id_type=MESH,
        )
        made.start()
        return made

    return copy


def place():
    s, b, u = (lax.axis_index(a) for a in ALL)
    a, c = u // 2, u % 2
    beside = (s, b, 2 * (1 - a) + c)
    across = (1 - s, b, u)
    twin = (s, b, 2 * a + 1 - c)

    def blocks(core):
        own = 4 * s + 2 * a + core
        on_x = 4 * s + 2 * (1 - a) + core
        on_y = 4 * (1 - s) + 2 * a + core
        diagonal = 4 * (1 - s) + 2 * (1 - a) + core
        return diagonal, on_x, on_y, own

    return (s, b, u), (beside, across, twin), blocks(c), blocks(1 - c)


def spread(own, out, send, recv, local):
    _, (beside, across, twin), (diag, on_x, on_y, me), _ = place()
    half = own.shape[0] // 2
    parts = (pl.ds(0, half), pl.ds(half, half))
    copy = sender(send, recv)
    x0 = copy(0, own.at[parts[0]], out.at[me, parts[0]], beside)
    y1 = copy(1, own.at[parts[1]], out.at[me, parts[1]], across)
    x1 = copy(2, own.at[parts[1]], out.at[me, parts[1]], beside)
    y0 = copy(3, own.at[parts[0]], out.at[me, parts[0]], across)
    started = [x0, y1, x1, y0, copy(4, own, out.at[me], twin)]
    kept = pltpu.make_async_copy(own, out.at[me], local)
    kept.start()

    def pass_on(i, block, part, device):
        made = copy(i, out.at[block, parts[part]], out.at[block, parts[part]], device)
        started.append(made)
        return made

    x0.wait_recv()
    d0 = pass_on(5, on_x, 0, across)
    pass_on(6, on_x, 0, twin)
    y1.wait_recv()
    d1 = pass_on(7, on_y, 1, beside)
    pass_on(8, on_y, 1, twin)
    x1.wait_recv()
    pass_on(9, on_x, 1, twin)
    y0.wait_recv()
    pass_on(10, on_y, 0, twin)
    d0.wait_recv()
    pass_on(11, diag, 0, twin)
    d1.wait_recv()
    pass_on(12, diag, 1, twin)
    for i in (4, 6, 8, 9, 10, 11, 12):
        started[i].wait_recv()
    for made in started:
        made.wait_send()
    kept.wait()


SPREAD = 13


def collect(multiply, total, to_twin, from_twin, mine, in_x, in_y, send, recv):
    _, (beside, across, twin), here, other = place()
    rows, width = total.shape
    half = rows // 2
    parts = (pl.ds(0, half), pl.ds(half, half))
    copy = sender(send, recv)
    tiles = width // TILE

    def each_tile(body):
        def step(t, carry):
            body(pl.ds(pl.multiple_of(t * TILE, TILE), TILE))
            return carry

        lax.fori_loop(0, tiles, step, 0)

    to_twins = []
    for k in range(4):

        def first(cols, k=k):
            to_twin[k, :, cols] = multiply(other[k], cols).astype(BF)

        each_tile(first)
        to_twins.append(copy(k, to_twin.at[k], from_twin.at[k], twin))
    started = []
    for k in range(4):
        to_twins[k].wait_recv()
        if k < 3:

            def second(cols, k=k):
                term = multiply(here[k], cols) + from_twin[k, :, cols].astype(F32)
                mine[k, :, cols] = term.astype(BF)

            each_tile(second)
        else:

            def third(cols):
                total[:, cols] = multiply(here[3], cols) + from_twin[3, :, cols].astype(F32)

            each_tile(third)
        if k == 0:
            dx = copy(4, mine.at[0, parts[0]], in_x.at[0], beside)
            dy = copy(5, mine.at[0, parts[1]], in_y.at[0], across)
        elif k == 1:
            started.append(copy(6, mine.at[1, parts[0]], in_x.at[1], beside))
        elif k == 2:
            started.append(copy(7, mine.at[2, parts[1]], in_y.at[1], across))

    def add(k, part, arrived):
        def step(t, carry):
            at = pl.ds(pl.multiple_of(t * CHUNK, CHUNK), CHUNK)
            to = pl.ds(pl.multiple_of(part * half + t * CHUNK, CHUNK), CHUNK)
            mine[k, to] = (mine[k, to].astype(F32) + arrived[0, at].astype(F32)).astype(BF)
            return carry

        lax.fori_loop(0, half // CHUNK, step, 0)

    dy.wait_recv()
    add(1, 1, in_y)
    started.append(copy(8, mine.at[1, parts[1]], in_x.at[2], beside))
    dx.wait_recv()
    add(2, 0, in_x)
    started.append(copy(9, mine.at[2, parts[0]], in_y.at[2], across))
    for made in started:
        made.wait_recv()

    def finish(t, carry):
        at = pl.ds(pl.multiple_of(t * CHUNK, CHUNK), CHUNK)
        low = pl.ds(pl.multiple_of(half + t * CHUNK, CHUNK), CHUNK)
        total[at] += in_x[1, at].astype(F32) + in_y[2, at].astype(F32)
        total[low] += in_x[2, at].astype(F32) + in_y[1, at].astype(F32)
        return carry

    lax.fori_loop(0, half // CHUNK, finish, 0)
    for made in to_twins + started + [dx, dy]:
        made.wait_send()


COLLECT = 10


def collect_scratch(rows, width):
    return [
        pltpu.VMEM((rows, width), F32),
        pltpu.VMEM((4, rows, width), BF),
        pltpu.VMEM((4, rows, width), BF),
        pltpu.VMEM((3, rows, width), BF),
        pltpu.VMEM((3, rows // 2, width), BF),
        pltpu.VMEM((3, rows // 2, width), BF),
        pltpu.SemaphoreType.DMA((COLLECT,)),
        pltpu.SemaphoreType.DMA((COLLECT,)),
    ]


def reorder(values, outer, inner, lanes):
    return jnp.concatenate(
        [
            values[:, (o * inner + i) * lanes : (o * inner + i + 1) * lanes]
            for i in range(inner)
            for o in range(outer)
        ],
        axis=1,
    )


def norm_parts(values):
    average = jnp.mean(values, axis=-1, keepdims=True)
    centred = values - average
    variance = jnp.mean(centred * centred, axis=-1, keepdims=True)
    spread_back = lax.rsqrt(variance + EPS)
    return centred * spread_back, spread_back


def norm_back(grad, values, gain):
    unit, spread_back = norm_parts(values)
    scaled = grad * gain
    back = spread_back * (
        scaled
        - jnp.mean(scaled, axis=-1, keepdims=True)
        - unit * jnp.mean(scaled * unit, axis=-1, keepdims=True)
    )
    return back, grad * unit


def each_chunk(rows, body):
    def step(t, carry):
        body(pl.ds(pl.multiple_of(t * CHUNK, CHUNK), CHUNK))
        return carry

    lax.fori_loop(0, rows // CHUNK, step, 0)


def row_sum(values):
    return jnp.sum(values, axis=0, keepdims=True)


def return_rows(block, out, n_blk, send, recv, local):
    (s, b, u), _, _, _ = place()
    count = block.shape[0] // n_blk
    copy = sender(send, recv)
    started = []
    for j in range(1, n_blk):
        to = (b + j) % n_blk
        rows = pl.ds(pl.multiple_of(to * count, count), count)
        started.append(copy(j - 1, block.at[rows], out.at[b], (s, to, u)))
    rows = pl.ds(pl.multiple_of(b * count, count), count)
    kept = pltpu.make_async_copy(block.at[rows], out.at[b], local)
    kept.start()
    for made in started:
        made.wait()
    kept.wait()


def blk_peers(n_blk):
    (s, b, u), _, _, _ = place()
    return [(s, (b + j) % n_blk, u) for j in range(1, n_blk)]


def entry_kernel(
    n_blk, x_ref, qkv_ref, fc_ref, small_ref, tok, qkv, fc, small,
    blk_send, blk_recv, plane_send, plane_recv, local,
):
    (s, b, u), _, (_, _, _, me), _ = place()
    plane = qkv_ref.shape[0]
    n_uly = plane // 2
    others = [(me + j) % plane for j in range(1, plane)]
    friends = [(p // n_uly, b, p % n_uly) for p in others]
    column = blk_peers(n_blk)
    meet(friends + column)
    by_blk = sender(blk_send, blk_recv)
    by_plane = sender(plane_send, plane_recv)
    kept = [
        pltpu.make_async_copy(small_ref, small.at[me, b], local.at[0]),
        pltpu.make_async_copy(x_ref.at[b], tok.at[b], local.at[1]),
        pltpu.make_async_copy(qkv_ref.at[me], qkv.at[me], local.at[2]),
        pltpu.make_async_copy(fc_ref.at[me], fc.at[me], local.at[3]),
    ]
    for made in kept:
        made.start()
    vectors, started = [], []
    for j, peer in enumerate(column):
        vectors.append(by_blk(j, small_ref, small.at[me, b], peer))
    for j, peer in enumerate(column):
        started.append(by_blk(n_blk - 1 + j, x_ref.at[peer[1]], tok.at[b], peer))
    for j, (p, peer) in enumerate(zip(others, friends)):
        started.append(by_plane(3 * j, qkv_ref.at[p], qkv.at[me], peer))
        started.append(by_plane(3 * j + 1, fc_ref.at[p], fc.at[me], peer))
    kept[0].wait()
    for made in vectors:
        made.wait()
    for j, peer in enumerate(friends):
        started.append(by_plane(3 * j + 2, small.at[me], small.at[me], peer))
    for made in kept[1:] + started:
        made.wait()


def enter(x, qkv, fc, small, n_blk):
    plane = qkv.shape[0]
    return pl.pallas_call(
        functools.partial(entry_kernel, n_blk),
        name="enter",
        out_shape=(
            jax.ShapeDtypeStruct(x.shape, x.dtype),
            jax.ShapeDtypeStruct(qkv.shape, qkv.dtype),
            jax.ShapeDtypeStruct(fc.shape, fc.dtype),
            jax.ShapeDtypeStruct((plane, n_blk) + small.shape, small.dtype),
        ),
        in_specs=[ANY] * 4,
        out_specs=(ANY,) * 4,
        scratch_shapes=[
            pltpu.SemaphoreType.DMA((2 * (n_blk - 1),)),
            pltpu.SemaphoreType.DMA((2 * (n_blk - 1),)),
            pltpu.SemaphoreType.DMA((3 * (plane - 1),)),
            pltpu.SemaphoreType.DMA((3 * (plane - 1),)),
            pltpu.SemaphoreType.DMA((4,)),
        ],
        compiler_params=pltpu.CompilerParams(collective_id=0, has_side_effects=True),
        cost_estimate=pl.CostEstimate(flops=0, bytes_accessed=60 * MIB, transcendentals=0),
    )(x, qkv, fc, small)


def norm_kernel(order, tok, gain, shift, out, own, send, recv, local):
    _, near, _, _ = place()

    def chunk(at):
        unit, _ = norm_parts(tok[at].astype(F32))
        own[at] = reorder(unit * gain[...] + shift[...], *order).astype(BF)

    each_chunk(own.shape[0], chunk)
    meet(near)
    spread(own, out, send, recv, local)


def norm_gather(tok, gain, shift, plane, order):
    rows, width = tok.shape
    return pl.pallas_call(
        functools.partial(norm_kernel, order),
        name="norm_gather",
        out_shape=jax.ShapeDtypeStruct((plane, rows, width), BF),
        in_specs=[VMEM] * 3,
        out_specs=ANY,
        scratch_shapes=[
            pltpu.VMEM((rows, width), BF),
            pltpu.SemaphoreType.DMA((SPREAD,)),
            pltpu.SemaphoreType.DMA((SPREAD,)),
            pltpu.SemaphoreType.DMA,
        ],
        compiler_params=pltpu.CompilerParams(
            collective_id=1, has_side_effects=True, vmem_limit_bytes=16 * MIB
        ),
        cost_estimate=pl.CostEstimate(flops=0, bytes_accessed=100 * MIB, transcendentals=0),
    )(tok, gain, shift)


def cot_kernel(n_blk, x_ref, tok, out, send, recv, local, g_send, g_recv):
    (s, b, u), near, _, _ = place()
    column = blk_peers(n_blk)
    meet(list(near) + column)
    copy = sender(g_send, g_recv)
    count = x_ref.shape[1]
    own_rows = pl.ds(pl.multiple_of(b * count, count), count)
    started = [
        copy(j, x_ref.at[peer[1]], tok.at[own_rows], peer) for j, peer in enumerate(column)
    ]
    kept = pltpu.make_async_copy(x_ref.at[b], tok.at[own_rows], local)
    kept.start()
    kept.wait()
    for made in started:
        made.wait()
    spread(tok, out, send, recv, local)


def cot_gather(x, plane):
    n_blk, count, width = x.shape
    rows = n_blk * count
    return pl.pallas_call(
        functools.partial(cot_kernel, n_blk),
        name="cot_gather",
        out_shape=(
            jax.ShapeDtypeStruct((rows, width), BF),
            jax.ShapeDtypeStruct((plane, rows, width), BF),
        ),
        in_specs=[ANY],
        out_specs=(ANY, ANY),
        scratch_shapes=[
            pltpu.SemaphoreType.DMA((SPREAD,)),
            pltpu.SemaphoreType.DMA((SPREAD,)),
            pltpu.SemaphoreType.DMA,
            pltpu.SemaphoreType.DMA((n_blk - 1,)),
            pltpu.SemaphoreType.DMA((n_blk - 1,)),
        ],
        compiler_params=pltpu.CompilerParams(collective_id=2, has_side_effects=True),
        cost_estimate=pl.CostEstimate(flops=0, bytes_accessed=120 * MIB, transcendentals=0),
    )(x)


def rows_of(ref, block, rows):
    return ref[pl.ds(pl.multiple_of(block * rows, rows), rows), :]


def hidden_kernel(
    order, act, weight, tok, bias, gain, shift, hidden, out,
    total, to_twin, from_twin, mine, in_x, in_y, c_send, c_recv, own, send, recv, local,
):
    _, near, _, _ = place()
    rows = total.shape[0]
    meet(near)

    def multiply(block, cols):
        return product(rows_of(act, block, rows), weight[:, cols])

    collect(multiply, total, to_twin, from_twin, mine, in_x, in_y, c_send, c_recv)

    def chunk(at):
        values = total[at] + tok[at].astype(F32) + bias[...]
        hidden[at] = values
        unit, _ = norm_parts(values)
        own[at] = reorder(unit * gain[...] + shift[...], *order).astype(BF)

    each_chunk(rows, chunk)
    spread(own, out, send, recv, local)


def hidden_gather(act, weight, tok, bias, gain, shift, plane, order):
    rows, width = tok.shape
    return pl.pallas_call(
        functools.partial(hidden_kernel, order),
        name="hidden_gather",
        out_shape=(
            jax.ShapeDtypeStruct((rows, width), F32),
            jax.ShapeDtypeStruct((plane, rows, width), BF),
        ),
        in_specs=[VMEM] * 6,
        out_specs=(VMEM, ANY),
        scratch_shapes=collect_scratch(rows, width)
        + [
            pltpu.VMEM((rows, width), BF),
            pltpu.SemaphoreType.DMA((SPREAD,)),
            pltpu.SemaphoreType.DMA((SPREAD,)),
            pltpu.SemaphoreType.DMA,
        ],
        compiler_params=pltpu.CompilerParams(
            collective_id=3, has_side_effects=True, vmem_limit_bytes=40 * MIB
        ),
        cost_estimate=pl.CostEstimate(flops=0, bytes_accessed=250 * MIB, transcendentals=0),
    )(act, weight, tok, bias, gain, shift)


def branch_kernel(
    order, act, weight, hid, cot, gain, grad_hidden, sums, out,
    total, to_twin, from_twin, mine, in_x, in_y, c_send, c_recv, own, send, recv, local,
):
    _, near, _, _ = place()
    rows = total.shape[0]
    meet(near)

    def multiply(block, cols):
        return against(rows_of(act, block, rows), weight[cols, :])

    collect(multiply, total, to_twin, from_twin, mine, in_x, in_y, c_send, c_recv)
    sums[...] = jnp.zeros_like(sums)
    inner, outer, lanes = order[1], order[0], order[2]

    def chunk(at):
        grad = reorder(total[at], inner, outer, lanes)
        back, by_gain = norm_back(grad, hid[at], gain[...])
        passed = cot[at].astype(F32)
        back = back + passed
        grad_hidden[at] = back
        low = back.astype(BF)
        own[at] = low
        sums[0:1] += row_sum(by_gain)
        sums[1:2] += row_sum(grad)
        sums[2:3] += row_sum(low.astype(F32))
        sums[3:4] += row_sum(passed)

    each_chunk(rows, chunk)
    spread(own, out, send, recv, local)


def branch_gather(act, weight, hid, cot, gain, plane, order):
    rows, width = cot.shape
    return pl.pallas_call(
        functools.partial(branch_kernel, order),
        name="branch_gather",
        out_shape=(
            jax.ShapeDtypeStruct((rows, width), F32),
            jax.ShapeDtypeStruct((8, width), F32),
            jax.ShapeDtypeStruct((plane, rows, width), BF),
        ),
        in_specs=[VMEM] * 5,
        out_specs=(VMEM, VMEM, ANY),
        scratch_shapes=collect_scratch(rows, width)
        + [
            pltpu.VMEM((rows, width), BF),
            pltpu.SemaphoreType.DMA((SPREAD,)),
            pltpu.SemaphoreType.DMA((SPREAD,)),
            pltpu.SemaphoreType.DMA,
        ],
        compiler_params=pltpu.CompilerParams(
            collective_id=4, has_side_effects=True, vmem_limit_bytes=48 * MIB
        ),
        cost_estimate=pl.CostEstimate(flops=0, bytes_accessed=250 * MIB, transcendentals=0),
    )(act, weight, hid, cot, gain)


def result_kernel(
    n_blk, act, weight, hid, bias, out,
    total, to_twin, from_twin, mine, in_x, in_y, c_send, c_recv, own, send, recv, local,
):
    _, near, _, _ = place()
    rows = total.shape[0]
    meet(list(near) + blk_peers(n_blk))

    def multiply(block, cols):
        return product(rows_of(act, block, rows), weight[:, cols])

    collect(multiply, total, to_twin, from_twin, mine, in_x, in_y, c_send, c_recv)

    def chunk(at):
        own[at] = (total[at] + hid[at] + bias[...]).astype(BF)

    each_chunk(rows, chunk)
    return_rows(own, out, n_blk, send, recv, local)


def result_return(act, weight, hid, bias, n_blk):
    rows, width = hid.shape
    return pl.pallas_call(
        functools.partial(result_kernel, n_blk),
        name="result_return",
        out_shape=jax.ShapeDtypeStruct((n_blk, rows // n_blk, width), BF),
        in_specs=[VMEM] * 4,
        out_specs=ANY,
        scratch_shapes=collect_scratch(rows, width)
        + [
            pltpu.VMEM((rows, width), BF),
            pltpu.SemaphoreType.DMA((n_blk - 1,)),
            pltpu.SemaphoreType.DMA((n_blk - 1,)),
            pltpu.SemaphoreType.DMA,
        ],
        compiler_params=pltpu.CompilerParams(
            collective_id=5, has_side_effects=True, vmem_limit_bytes=40 * MIB
        ),
        cost_estimate=pl.CostEstimate(flops=0, bytes_accessed=180 * MIB, transcendentals=0),
    )(act, weight, hid, bias)


def inputs_kernel(
    n_blk, order, act, weight, tok, grad_hidden, gain, sums, out,
    total, to_twin, from_twin, mine, in_x, in_y, c_send, c_recv, own, send, recv, local,
):
    _, near, _, _ = place()
    rows = total.shape[0]
    meet(list(near) + blk_peers(n_blk))

    def multiply(block, cols):
        return against(rows_of(act, block, rows), weight[cols, :])

    collect(multiply, total, to_twin, from_twin, mine, in_x, in_y, c_send, c_recv)
    sums[...] = jnp.zeros_like(sums)
    inner, outer, lanes = order[1], order[0], order[2]

    def chunk(at):
        grad = reorder(total[at], inner, outer, lanes)
        back, by_gain = norm_back(grad, tok[at].astype(F32), gain[...])
        own[at] = (grad_hidden[at] + back).astype(BF)
        sums[0:1] += row_sum(by_gain)
        sums[1:2] += row_sum(grad)

    each_chunk(rows, chunk)
    return_rows(own, out, n_blk, send, recv, local)


def inputs_return(act, weight, tok, grad_hidden, gain, n_blk, order):
    rows, width = tok.shape
    return pl.pallas_call(
        functools.partial(inputs_kernel, n_blk, order),
        name="inputs_return",
        out_shape=(
            jax.ShapeDtypeStruct((8, width), F32),
            jax.ShapeDtypeStruct((n_blk, rows // n_blk, width), BF),
        ),
        in_specs=[VMEM] * 5,
        out_specs=(VMEM, ANY),
        scratch_shapes=collect_scratch(rows, width)
        + [
            pltpu.VMEM((rows, width), BF),
            pltpu.SemaphoreType.DMA((n_blk - 1,)),
            pltpu.SemaphoreType.DMA((n_blk - 1,)),
            pltpu.SemaphoreType.DMA,
        ],
        compiler_params=pltpu.CompilerParams(
            collective_id=6, has_side_effects=True, vmem_limit_bytes=40 * MIB
        ),
        cost_estimate=pl.CostEstimate(flops=0, bytes_accessed=180 * MIB, transcendentals=0),
    )(act, weight, tok, grad_hidden, gain)


def end_kernel(
    n_blk, qkv_ref, fc_ref, small_ref, qkv, fc, small, gathered, partial, arrived,
    blk_send, blk_recv, plane_send, plane_recv, local,
):
    (s, b, u), _, (_, _, _, me), _ = place()
    plane = qkv_ref.shape[0]
    n_uly = plane // 2
    others = [(me + j) % plane for j in range(1, plane)]
    friends = [(p // n_uly, b, p % n_uly) for p in others]
    column = blk_peers(n_blk)
    meet(friends + column)
    by_blk = sender(blk_send, blk_recv)
    by_plane = sender(plane_send, plane_recv)
    kept = [
        pltpu.make_async_copy(small_ref.at[me], gathered.at[me], local.at[0]),
        pltpu.make_async_copy(qkv_ref.at[me], qkv.at[me], local.at[1]),
        pltpu.make_async_copy(fc_ref.at[me], fc.at[me], local.at[2]),
    ]
    for made in kept:
        made.start()
    vectors, started = [], []
    for j, (p, peer) in enumerate(zip(others, friends)):
        vectors.append(by_plane(3 * j, small_ref.at[p], gathered.at[me], peer))
    for j, (p, peer) in enumerate(zip(others, friends)):
        started.append(by_plane(3 * j + 1, qkv_ref.at[p], qkv.at[me], peer))
        started.append(by_plane(3 * j + 2, fc_ref.at[p], fc.at[me], peer))
    kept[0].wait()
    for made in vectors:
        made.wait()
    partial[...] = jnp.sum(gathered[...], axis=0)
    own = pltpu.make_async_copy(partial.at[b], arrived.at[b], local.at[3])
    own.start()
    sent = [
        by_blk(j, partial.at[peer[1]], arrived.at[b], peer) for j, peer in enumerate(column)
    ]
    own.wait()
    for made in sent:
        made.wait()
    small[...] = jnp.sum(arrived[...], axis=0)
    for made in kept[1:] + started:
        made.wait()


def finish(qkv, fc, small):
    plane, n_blk = small.shape[:2]
    tail = small.shape[2:]
    return pl.pallas_call(
        functools.partial(end_kernel, n_blk),
        name="finish",
        out_shape=(
            jax.ShapeDtypeStruct(qkv.shape, qkv.dtype),
            jax.ShapeDtypeStruct(fc.shape, fc.dtype),
            jax.ShapeDtypeStruct(tail, small.dtype),
        ),
        in_specs=[ANY, ANY, ANY],
        out_specs=(ANY, ANY, VMEM),
        scratch_shapes=[
            pltpu.VMEM((plane, n_blk) + tail, F32),
            pltpu.VMEM((n_blk,) + tail, F32),
            pltpu.VMEM((n_blk,) + tail, F32),
            pltpu.SemaphoreType.DMA((n_blk - 1,)),
            pltpu.SemaphoreType.DMA((n_blk - 1,)),
            pltpu.SemaphoreType.DMA((3 * (plane - 1),)),
            pltpu.SemaphoreType.DMA((3 * (plane - 1),)),
            pltpu.SemaphoreType.DMA((4,)),
        ],
        compiler_params=pltpu.CompilerParams(
            collective_id=7, has_side_effects=True, vmem_limit_bytes=16 * MIB
        ),
        cost_estimate=pl.CostEstimate(flops=0, bytes_accessed=60 * MIB, transcendentals=0),
    )(qkv, fc, small)


def on_device(
    inputs,
    doc_lengths,
    ln1_gain,
    ln1_shift,
    w_query,
    b_query,
    w_key,
    w_value,
    b_value,
    w_out,
    b_out,
    ln2_gain,
    ln2_shift,
    w_fc,
    b_fc,
    w_proj,
    b_proj,
    cotangent,
):
    seqs, tok, width = inputs.shape
    n_seq, n_blk, n_uly = (lax.axis_size(a) for a in ALL)
    plane = n_seq * n_uly
    here_seq, here_blk, here_uly = (lax.axis_index(a) for a in ALL)
    here = here_seq * n_uly + here_uly
    scale = 1.0 / math.sqrt(HD)
    rows = w_query.shape[0]
    hidden_rows = w_proj.shape[0]
    share = width // plane
    heads = share // HD
    ff_share = hidden_rows * n_blk
    sharing = max(1, n_blk // seqs)
    held = seqs * sharing // n_blk
    part = tok // sharing
    n_rows = n_blk * held * part
    order = (n_seq, n_blk, n_uly * rows)

    def by_plane(block):
        block = block.reshape(n_blk // sharing, held, sharing, part, width)
        return block.transpose(0, 2, 1, 3, 4).reshape(n_blk, held * part, width)

    def from_plane(block):
        block = block.reshape(n_blk // sharing, sharing, held, part, width)
        return block.transpose(0, 2, 1, 3, 4).reshape(seqs, tok, width)

    vectors = (ln1_gain, ln1_shift, b_query, b_value, b_out, ln2_gain, ln2_shift, b_proj)
    small = jnp.concatenate(
        [v.astype(F32) for v in vectors + (b_fc, doc_lengths.reshape(-1))]
    )
    lanes = -(-small.size // 1024) * 8
    small = jnp.pad(small, (0, lanes * 128 - small.size)).reshape(lanes, 128)
    qkv = jnp.stack([w.reshape(rows, plane, share) for w in (w_query, w_key, w_value)], axis=2)
    qkv = qkv.transpose(1, 0, 2, 3).reshape(plane, rows, 3 * share)
    fc = w_fc.reshape(rows, n_seq, n_blk, n_uly, hidden_rows).transpose(1, 3, 0, 2, 4)
    fc = fc.reshape(plane, rows, ff_share)
    tokens, qkv, fc, small = enter(by_plane(inputs), qkv, fc, small, n_blk)
    tokens = tokens.reshape(n_rows, width)

    def over_blk(matrix):
        return lax.all_gather(matrix, "blk", axis=0, tiled=True)

    qkv = over_blk(qkv.reshape(plane * rows, 3 * share))
    out_part = over_blk(w_out).reshape(n_uly, n_blk // n_uly, rows, width)
    out_part = lax.all_to_all(out_part, "uly", split_axis=0, concat_axis=0, tiled=True)
    out_part = out_part.transpose(1, 0, 2, 3).reshape(share, width)
    fc = over_blk(fc.reshape(plane * rows, ff_share))
    proj = over_blk(w_proj)

    small = small.reshape(n_seq, n_uly, n_blk, lanes * 128)
    flat = small.transpose(0, 2, 1, 3).reshape(n_seq * n_blk * n_uly, lanes * 128)
    whole = [flat[:, i * rows : (i + 1) * rows].reshape(1, width) for i in range(8)]
    at = 8 * rows
    bias_fc = lax.dynamic_slice(
        small, (here_seq, here_uly, 0, at), (1, 1, n_blk, hidden_rows)
    ).reshape(1, ff_share)
    at += hidden_rows
    lengths = small[:, 0, 0, at : at + doc_lengths.size].astype(jnp.int32)
    lengths = lengths.reshape(n_seq, *doc_lengths.shape)
    gain_one, shift_one, bias_q, bias_v, bias_out, gain_two, shift_two, bias_proj = whole
    mine = lambda v: lax.dynamic_slice(v, (0, here * share), (1, share))
    bias_q, bias_v = mine(bias_q), mine(bias_v)

    normed = norm_gather(tokens, gain_one, shift_one, plane, order)
    normed = normed.reshape(plane * n_rows, width)
    grad_out, grad_all = cot_gather(by_plane(cotangent), plane)
    grad_all = grad_all.reshape(plane * n_rows, width)

    made = product(normed, qkv)
    queries = ((made[:, :share] + bias_q) * scale).astype(BF)
    keys = made[:, share : 2 * share].astype(BF)
    values = (made[:, 2 * share :] + bias_v).astype(BF)

    groups = [
        [g * sharing + i for i in range(sharing)] for g in range(n_blk // sharing)
    ]
    pairs = n_seq * held * heads // sharing
    length = n_blk * n_uly * tok

    def to_heads(matrix):
        matrix = matrix.reshape(n_seq, n_uly, n_blk, held, part, heads, HD)
        matrix = matrix.transpose(0, 3, 5, 2, 1, 4, 6)
        matrix = matrix.reshape(n_seq * held * heads, n_blk, n_uly, 1, part, HD)
        if sharing > 1:
            matrix = lax.all_to_all(
                matrix, "blk", split_axis=0, concat_axis=3, axis_index_groups=groups, tiled=True
            )
        return matrix.reshape(pairs, length, HD)

    def from_heads(matrix):
        matrix = matrix.reshape(pairs, n_blk, n_uly, sharing, part, HD)
        if sharing > 1:
            matrix = lax.all_to_all(
                matrix, "blk", split_axis=3, concat_axis=0, axis_index_groups=groups, tiled=True
            )
        matrix = matrix.reshape(n_seq, held, heads, n_blk, n_uly, part, HD)
        return matrix.transpose(0, 4, 3, 1, 5, 2, 6).reshape(plane * n_rows, share)

    hq, hk, hv = to_heads(queries), to_heads(keys), to_heads(values)
    turn = here_blk % sharing
    pair_at = turn * pairs + jnp.arange(pairs)
    seq_of = pair_at // (held * heads)
    held_of = (pair_at // heads) % held
    which = (here_blk // sharing) * held + held_of
    own_lengths = lengths[seq_of, which]
    first = own_lengths[:, 0:1]
    second = first + own_lengths[:, 1:2]
    position = jnp.arange(length, dtype=jnp.int32)[None]
    doc = (position >= first).astype(jnp.int32) + (position >= second).astype(jnp.int32)
    allowed = (doc[:, :, None] == doc[:, None, :]) & (
        position[:, None, :] <= position[:, :, None]
    )

    def head_forward(args):
        q, k, v, ok = args
        scores = jnp.where(ok, against(q, k), NEGATIVE)
        top = jnp.max(scores, axis=1, keepdims=True)
        powered = jnp.exp(scores - top)
        total = jnp.sum(powered, axis=1, keepdims=True)
        result = product(powered.astype(BF), v) / total
        return result, top + jnp.log(total)

    attended, log_total = lax.map(head_forward, (hq, hk, hv, allowed))
    attended_low = from_heads(attended.astype(BF))
    hidden, normed_two = hidden_gather(
        attended_low, out_part, tokens, bias_out, gain_two, shift_two, plane, order
    )
    normed_two = normed_two.reshape(plane * n_rows, width)
    inner = product(normed_two, fc) + bias_fc
    gelu_value, gelu_back = jax.vjp(gelu_tanh, inner)
    active = gelu_value.astype(BF)
    grad_w_proj = lax.psum_scatter(
        transposed(active, grad_all).astype(BF), "blk", scatter_dimension=0, tiled=True
    ).astype(F32)
    grad_inner = gelu_back(against(grad_all, proj))[0].astype(BF)
    grad_b_fc = jnp.sum(grad_inner.astype(F32), axis=0)
    grad_fc = lax.psum_scatter(
        transposed(normed_two, grad_inner).astype(BF), "blk", scatter_dimension=0, tiled=True
    )
    grad_hidden, sums_two, branch_all = branch_gather(
        grad_inner, fc, hidden, grad_out, gain_two, plane, order
    )
    branch_all = branch_all.reshape(plane * n_rows, width)
    result = result_return(active, proj, hidden, bias_proj, n_blk)
    grad_w_out = transposed(attended_low, branch_all).astype(BF)
    grad_w_out = grad_w_out.reshape(n_blk // n_uly, n_uly, rows, width).transpose(1, 0, 2, 3)
    grad_w_out = lax.all_to_all(grad_w_out, "uly", split_axis=0, concat_axis=0, tiled=True)
    grad_w_out = lax.psum_scatter(
        grad_w_out.reshape(n_blk * rows, width), "blk", scatter_dimension=0, tiled=True
    ).astype(F32)
    grad_heads = to_heads(against(branch_all, out_part).astype(BF))

    def head_backward(args):
        q, k, v, ok, grad, kept, logs = args
        dots = jnp.sum(grad.astype(F32) * kept, axis=1, keepdims=True)
        scores = jnp.where(ok, against(q, k), NEGATIVE)
        chances = jnp.exp(scores - logs)
        grad_v = transposed(chances.astype(BF), grad)
        grad_scores = (chances * (against(grad, v) - dots)).astype(BF)
        grad_q = product(grad_scores, k) * scale
        grad_k = transposed(grad_scores, q)
        return grad_q.astype(BF), grad_k.astype(BF), grad_v.astype(BF)

    backs = lax.map(head_backward, (hq, hk, hv, allowed, grad_heads, attended, log_total))
    backs = jnp.concatenate([from_heads(b) for b in backs], axis=1)
    grad_bias = jnp.sum(backs.astype(F32), axis=0)
    grad_qkv = lax.psum_scatter(
        transposed(normed, backs).astype(BF), "blk", scatter_dimension=0, tiled=True
    )
    sums_one, grad_inputs = inputs_return(
        backs, qkv, tokens, grad_hidden, gain_one, n_blk, order
    )

    def widened(vector):
        return lax.dynamic_update_slice(jnp.zeros((width,), F32), vector, (here * share,))

    parts = (
        sums_one[0],
        sums_one[1],
        widened(grad_bias[:share]),
        widened(grad_bias[2 * share :]),
        sums_two[2],
        sums_two[0],
        sums_two[1],
        sums_two[3],
    )
    wide_fc = lax.dynamic_update_slice(
        jnp.zeros((n_seq, n_blk, n_uly, hidden_rows), F32),
        grad_b_fc.reshape(1, n_blk, 1, hidden_rows),
        (here_seq, 0, here_uly, 0),
    )
    sums = jnp.concatenate(
        [p.reshape(n_seq, n_blk, n_uly, rows) for p in parts] + [wide_fc], axis=3
    )
    used = sums.shape[3]
    end_lanes = -(-used // 1024) * 8
    sums = jnp.pad(sums, ((0, 0),) * 3 + ((0, end_lanes * 128 - used),))
    sums = sums.transpose(0, 2, 1, 3).reshape(plane, n_blk, end_lanes, 128)
    grad_qkv, grad_fc, sums = finish(
        grad_qkv.reshape(plane, rows, 3 * share), grad_fc.reshape(plane, rows, ff_share), sums
    )
    sums = sums.reshape(-1)
    each = [sums[i * rows : (i + 1) * rows] for i in range(8)]
    grad_qkv = grad_qkv.reshape(plane, rows, 3, share).transpose(2, 1, 0, 3)
    grad_qkv = grad_qkv.reshape(3, rows, width).astype(F32)
    grad_fc = grad_fc.reshape(n_seq, n_uly, rows, n_blk, hidden_rows)
    grad_fc = grad_fc.transpose(2, 0, 3, 1, 4).reshape(rows, -1).astype(F32)
    return (
        from_plane(result),
        from_plane(grad_inputs),
        each[0],
        each[1],
        grad_qkv[0],
        each[2],
        grad_qkv[1],
        grad_qkv[2],
        each[3],
        grad_w_out,
        each[4],
        each[5],
        each[6],
        grad_fc,
        sums[8 * rows : used],
        grad_w_proj,
        each[7],
    )


def solution(mesh):
    tokens = P("seq", ("blk", "uly"), None)
    vector = P(ALL)
    matrix = P(ALL, None)
    return jax.shard_map(
        on_device,
        mesh=mesh,
        in_specs=(
            tokens, P("seq", None), vector, vector, matrix, vector, matrix, matrix, vector,
            matrix, vector, vector, vector, matrix, vector, matrix, vector, tokens,
        ),
        out_specs=(
            tokens, tokens, vector, vector, matrix, vector, matrix, matrix, vector,
            matrix, vector, vector, vector, matrix, vector, matrix, vector,
        ),
        check_vma=False,
    )
```

time: 1380 us -> 891 us (0.65)
  waiting for transfers between devices: 771 us -> 13.7 us
  Pallas kernels: 0 us -> 575 us
  blocking collectives: 175 us -> 0 us
  matrix products: 232 us -> 147 us
  other arithmetic: 55.1 us -> 25.7 us
  starting transfers between devices: 27.5 us -> 8.25 us
    pallas_call x0 -> x8, Pallas kernels: none -> 575 us  [the longest x1 104 us: inputs_return(): pl.pallas_call(functools.partial(inputs_kernel, n_blk, order), name='inpu...]
    all_gather x8 -> x4, waiting for transfers between devices: 309 us -> 0.03 us  [over_blk(): return lax.all_gather(matrix, 'blk', axis=0, tiled=True)]
    reduce_scatter x6 -> x2, waiting for transfers between devices: 183 us -> 0.01 us  [the longest x1 0.01 us: on_device(): lax.psum_scatter(transposed(normed, backs).astype(BF), 'blk', scatter_dim...]
    unnamed x18 -> x8, waiting for transfers between devices: 122 us -> 1.97 us
    all_to_all x4 -> x0, blocking collectives: 110 us -> none  [the longest x1 56.3 us: to_planes(): lax.all_to_all(block, 'blk', split_axis=0, concat_axis=0, tiled=True)]
    reduce_scatter x1, waiting for transfers between devices: 79.8 us -> 0.01 us  [on_device(): lax.psum_scatter(transposed(active, grad_all).astype(BF), 'blk', scatter_...]
    unnamed x1 -> x0, blocking collectives: 65.8 us -> none
    all_to_all x5 -> x1, waiting for transfers between devices: 67.3 us -> 11.7 us  [on_device(): lax.all_to_all(grad_w_out, 'uly', split_axis=0, concat_axis=0, tiled=True)]
  transfers between devices with their start and end apart: 23 -> 10, of which waited for: 16 -> 1; matrix products, arithmetic and copies ran while one was open for 24% -> 18% of each run, Pallas kernels for 0% -> 55%
where the time goes in v2:
time: 891 us; the launch traced here: 881 us
  Pallas kernels  575 us (65%)
  matrix products  147 us (16%)
  local copies, waits for them, and re-layouts  95.7 us (11%)
  other arithmetic  25.7 us (3%)
  between operations  15.4 us (2%)
  waiting for transfers between devices  13.7 us (2%)
    pallas_call x1, Pallas kernels, inputs_return(): pl.pallas_call(functools.partial(inputs_kernel, n_blk, order), name='inpu...  104 us
    pallas_call x1, Pallas kernels, result_return(): pl.pallas_call(functools.partial(result_kernel, n_blk), name='result_retu...  96.9 us
    pallas_call x1, Pallas kernels, branch_gather(): pl.pallas_call(functools.partial(branch_kernel, order), name='branch_gath...  94.1 us
    pallas_call x1, Pallas kernels, cot_gather(): pl.pallas_call(functools.partial(cot_kernel, n_blk), name='cot_gather', o...  87.9 us
    pallas_call x1, Pallas kernels, hidden_gather(): pl.pallas_call(functools.partial(hidden_kernel, order), name='hidden_gath...  83.9 us
    dot_general x12, matrix products, transposed(): lax.dot_general(left_side, right_side, (((0,), (0,)), ((), ())), preferre...  56.2 us
    dot_general x14, matrix products, against(): lax.dot_general(left_side, right_side, (((1,), (1,)), ((), ())), preferre...  48.4 us
    pallas_call x1, Pallas kernels, norm_gather(): pl.pallas_call(functools.partial(norm_kernel, order), name='norm_gather',...  42.6 us
  transfers between devices with their start and end apart: 10, of which 1 were waited for; matrix products, arithmetic and copies ran while one was open for 18% of the time, Pallas kernels for 55%

profile of v2, /device:TPU:8, one launch (start us, length us, event | category | flops | bytes accessed | tf_op | source)
XLA Modules:
  0.0 880.8 jit_solution(7175993409505428766)
XLA Ops:
  19.5 42.0 %enter.1 = (bf16[4,64,2048]{2,1,0:T(8,128)(2,1)}, bf16[8,64,768]{2,1,0:T(8,128)(2,1)}, bf16[8,64,1024]{2,1,0:T(8,128)(2,1)}, f32[8,4,8,128]{3,2,1,0:T(8,128)}) custom-call(bf16[4,64,2048]{2,1,0:T(8,128)(2,1)} %x_ref.2, bf16[8,64,768]{2,1,0:T(8,128)(2,1)} %reshape.344.qkv_ref, bf16[8,64,1024]{2,1,0:T(8,128)(2,1)} %reshape.346.fc_ref, ...), custom_call_target="tpu_custom_call" | custom-call | bytes 62914560 | tf_op jit(solution)/shard_map/enter/pallas_call | solution.py:325
  66.5 87.9 %cot_gather.1 = (bf16[256,2048]{1,0:T(8,128)(2,1)}, bf16[8,256,2048]{2,1,0:T(8,128)(2,1)}) custom-call(bf16[4,64,2048]{2,1,0:T(8,128)(2,1)} %x_ref.3), custom_call_target="tpu_custom_call" | custom-call | bytes 125829120 | tf_op jit(solution)/shard_map/cot_gather/pallas_call | solution.py:402
  154.5 4.3 compare_and_fusion
  158.8 42.6 %norm_gather.1 = bf16[8,256,2048]{2,1,0:T(8,128)(2,1)S(1)} custom-call(bf16[256,2048]{1,0:T(8,128)(2,1)S(1)} %bitcast.250, f32[1,2048]{1,0:T(1,128)S(1)} %reshape.351.gain, f32[1,2048]{1,0:T(1,128)S(1)} %reshape.352.shift), custom_call_target="tpu_custom_call" | custom-call | bytes 104857600 | tf_op jit(solution)/shard_map/norm_gather/pallas_call | solution.py:362
  201.4 3.2 copy-done.4
  204.7 3.7 all-to-all-start
  208.4 10.0 %fusion.83 = f32[2048,768]{1,0:T(8,128)S(1)} fusion(bf16[2048,2048]{1,0:T(8,128)(2,1)} %bitcast.253, bf16[2048,768]{1,0:T(8,128)(2,1)} %all-gather.5.cloned.1.call-done.weight), kind=kOutput, calls=%fused_computation.126 | convolution fusion | flops 6442450944 | bytes 17825792 | tf_op jit(solution)/shard_map/dot_general | solution.py:31
  220.3 2.1 reshape.356
  222.4 2.5 copy.117
  226.0 2.5 copy.118
  231.1 32.5 %while.26 = (s32[]{:T(128)}, f32[4,1024,128]{2,1,0:T(8,128)}, f32[4,1024,1]{1,2,0:T(1,128)S(1)}, pred[4,1024,1024]{2,1,0:T(32,128)(4,1)}, bf16[4,1024,128]{2,1,0...) while((s32[]{:T(128)}, f32[4,1024,128]{2,1,0:T(8,128)}, ...), condition=%wide.region_3.4_spmd, body=%wide.region_0.3_spmd.sunk | while | flops 545389568 | bytes 21276772 | solution.py:840
  236.3 2.9 fusion.126
  244.5 2.9 fusion.126
  252.6 2.9 fusion.126
  260.7 2.9 fusion.126
  271.1 83.9 %hidden_gather.1 = (f32[256,2048]{1,0:T(8,128)S(1)}, bf16[8,256,2048]{2,1,0:T(8,128)(2,1)S(1)}) custom-call(bf16[2048,256]{1,0:T(8,128)(2,1)S(1)} %bitcast.257, bf16[256,2048]{1,0:T(8,128)(2,1)S(1)} %bitcast.255, bf16[256,2048]{1,0:T(8,128)(2,1)S(1)} %bitcast.251, f32[1,2048]{1,0:T(1,128)S(1)} %reshape.362.bias, f32[1,2048]{1,0:T(1,128)S(1)} %reshape.363.gain, ...), custom_call_target="tpu_custom_call" | custom-call | bytes 262144000 | tf_op jit(solution)/shard_map/hidden_gather/pallas_call | solution.py:452
  355.1 3.3 copy-done.23
  358.3 15.2 %fusion.84 = f32[2048,1024]{1,0:T(8,128)} fusion(bf16[2048,2048]{1,0:T(8,128)(2,1)} %bitcast.261, bf16[2048,1024]{1,0:T(8,128)(2,1)} %all-gather.9.cloned.1.call-done.weight), kind=kOutput, calls=%fused_computation.127 | convolution fusion | flops 8589934592 | bytes 20971520 | tf_op jit(solution)/shard_map/dot_general | solution.py:31
  373.5 21.0 %convert_reduce_fusion = (f32[1024]{0:T(1024)S(1)}, bf16[2048,1024]{1,0:T(8,128)(2,1)}, bf16[2048,1024]{1,0:T(8,128)(2,1)}) fusion(f32[2048,1024]{1,0:T(8,128)} %fusion.84, f32[1024]{0:T(1024)S(1)} %bitcast.306, bf16[2048,2048]{1,0:T(8,128)(2,1)} %bitcast.308, bf16[1024,2048]{1,0:T(8,128)(2,1)} %all-gather.11.cloned.1.call-done.weight), kind=kOutput, calls=%fused_computation.73 | convolution fusion | flops 8642362368 | bytes 29368320 | tf_op jit(solution)/shard_map/dot_general | solution.py:41
  394.5 94.1 %branch_gather.1 = (f32[256,2048]{1,0:T(8,128)S(1)}, f32[8,2048]{1,0:T(8,128)S(1)}, bf16[8,256,2048]{2,1,0:T(8,128)(2,1)}) custom-call(bf16[2048,1024]{1,0:T(8,128)(2,1)} %get-tuple-element.224.act, bf16[2048,1024]{1,0:T(8,128)(2,1)} %all-gather.9.cloned.1.call-done.weight, f32[256,2048]{1,0:T(8,128)S(1)} %get-tuple-element.136.hid, ...), custom_call_target="tpu_custom_call" | custom-call | bytes 262144000 | tf_op jit(solution)/shard_map/branch_gather/pallas_call | solution.py:509
  488.7 6.6 convolution_convert_fusion.5
  495.4 3.3 convolution_convert_fusion.4
  501.4 40.4 %while.27 = (s32[]{:T(128)}, bf16[4,1024,128]{2,1,0:T(8,128)(2,1)}, bf16[4,1024,128]{2,1,0:T(8,128)(2,1)}, bf16[4,1024,128]{2,1,0:T(8,128)(2,1)}, pred[4,1024,10...) while((s32[]{:T(128)}, bf16[4,1024,128]{2,1,0:T(8,128)(2,1)}, ...), condition=%wide.region_6.7_spmd, body=%wide.region_4.6_spmd.sunk | while | flops 1351482368 | bytes 41187488 | solution.py:881
  503.8 2.7 multiply_convert_fusion.3
  509.4 2.1 fusion.141
  513.8 2.7 multiply_convert_fusion.3
  519.4 2.1 fusion.141
  523.9 2.7 multiply_convert_fusion.3
  529.5 2.1 fusion.141
  533.9 2.7 multiply_convert_fusion.3
  539.6 2.1 fusion.141
  541.8 3.4 copy.123
  545.2 3.3 copy.124
  548.5 2.1 copy.125
  550.5 4.2 all-to-all-start.1
  557.6 11.7 %all-to-all-done.1 = bf16[4,1,64,2048]{3,2,1,0:T(8,128)(2,1)} async-done(((bf16[4,1,64,2048]{3,2,1,0:T(8,128)(2,1)}), bf16[4,1,64,2048]{3,2,1,0:T(8,128)(2,1)}, u32[]{:S(2)}, u32[]{:S(2)}) %all-to-all-start.1) | async-done | bytes 1048608 | tf_op jit(solution)/shard_map/all_to_all | solution.py:864
  570.7 10.4 %convolution_convert_fusion.3 = bf16[2048,768]{1,0:T(8,128)(2,1)} fusion(bf16[2048,2048]{1,0:T(8,128)(2,1)} %bitcast.254, bf16[2048,768]{1,0:T(8,128)(2,1)S(1)} %bitcast_dynamic-update-slice_fusion.act), kind=kOutput, calls=%fused_computation.79 | convolution fusion | flops 6444023808 | bytes 14680064 | tf_op jit(solution)/shard_map/dot_general | solution.py:35
  581.2 14.0 %convolution_convert_fusion.2 = bf16[2048,1024]{1,0:T(8,128)(2,1)} fusion(bf16[2048,2048]{1,0:T(8,128)(2,1)} %bitcast.262, bf16[2048,1024]{1,0:T(8,128)(2,1)} %get-tuple-element.224.act), kind=kOutput, calls=%fused_computation.78 | convolution fusion | flops 8592031744 | bytes 16777216 | tf_op jit(solution)/shard_map/dot_general | solution.py:35
  595.3 14.3 %convolution_convert_fusion.1 = bf16[1024,2048]{1,0:T(8,128)(2,1)} fusion(bf16[2048,1024]{1,0:T(8,128)(2,1)} %get-tuple-element.227.act, bf16[2048,2048]{1,0:T(8,128)(2,1)} %bitcast.309), kind=kOutput, calls=%fused_computation.77 | convolution fusion | flops 8592031744 | bytes 16777216 | tf_op jit(solution)/shard_map/dot_general | solution.py:35
  612.0 2.3 copy-done.11
  614.2 2.2 copy-done.12
  616.4 96.9 %result_return.1 = bf16[4,64,2048]{2,1,0:T(8,128)(2,1)S(1)} custom-call(bf16[2048,1024]{1,0:T(8,128)(2,1)S(1)} %copy-done.12, bf16[1024,2048]{1,0:T(8,128)(2,1)S(1)} %copy-done.11, f32[256,2048]{1,0:T(8,128)S(1)} %copy-done.3, f32[1,2048]{1,0:T(1,128)S(1)} %reshape.367.bias), custom_call_target="tpu_custom_call" | custom-call | bytes 188743680 | tf_op jit(solution)/shard_map/result_return/pallas_call | solution.py:555
  713.4 103.8 %inputs_return.1 = (f32[8,2048]{1,0:T(8,128)S(1)}, bf16[4,64,2048]{2,1,0:T(8,128)(2,1)S(1)}) custom-call(bf16[2048,768]{1,0:T(8,128)(2,1)S(1)} %bitcast_dynamic-update-slice_fusion.act, bf16[2048,768]{1,0:T(8,128)(2,1)S(1)} %copy-done.13, bf16[256,2048]{1,0:T(8,128)(2,1)S(1)} %bitcast.252, f32[256,2048]{1,0:T(8,128)S(1)} %copy-done.15, f32[1,2048]{1,0:T(1,128)S(1)} %copy-done.22), custom_call_target="tpu_custom_call" | custom-call | bytes 188743680 | tf_op jit(solution)/shard_map/inputs_return/pallas_call | solution.py:603
  824.3 23.5 %finish.1 = (bf16[8,64,768]{2,1,0:T(8,128)(2,1)S(1)}, bf16[8,64,1024]{2,1,0:T(8,128)(2,1)S(1)}, f32[8,128]{1,0:T(8,128)S(1)}) custom-call(bf16[8,64,768]{2,1,0:T(8,128)(2,1)S(1)} %bitcast.259, bf16[8,64,1024]{2,1,0:T(8,128)(2,1)S(1)} %bitcast.258, f32[8,4,8,128]{3,2,1,0:T(8,128)S(1)} %reshape.379.small_ref), custom_call_target="tpu_custom_call" | custom-call | bytes 62914560 | tf_op jit(solution)/shard_map/finish/pallas_call | solution.py:672
  849.6 4.5 fusion.80
  859.9 4.3 copy.138
  864.2 3.4 reshape.382
  868.8 2.8 convert_element_type.187
  (255 shorter events, 99.1 us)
Async XLA Ops:
  7.2 197.5 %all-gather.7.cloned.1.call-start = ((), (), s32[]{:S(2)}) async-start(), calls=%async_computation.7 | async-start | bytes 1310720 | tf_op jit(solution)/shard_map/all_gather | solution.py:758
  7.9 200.5 %all-gather.5.cloned.1.call-start = ((), (), s32[]{:S(2)}) async-start(), calls=%async_computation.6 | async-start | bytes 3932160 | tf_op jit(solution)/shard_map/all_gather | solution.py:758
  8.0 8.0 copy-start.30
  14.1 4.6 copy-start.33
  14.2 4.6 copy-start.34
  14.2 4.6 copy-start.35
  14.2 4.6 copy-start.36
  14.2 4.6 copy-start.37
  14.2 4.6 copy-start.38
  14.2 4.6 copy-start.39
  14.2 4.6 copy-start.40
  14.2 4.6 copy-start.41
  14.2 4.6 copy-start.42
  61.6 296.7 %all-gather.9.cloned.1.call-start = ((), (), s32[]{:S(2)}) async-start(), calls=%async_computation.8 | async-start | bytes 5242880 | tf_op jit(solution)/shard_map/all_gather | solution.py:758
  62.3 311.2 %all-gather.11.cloned.1.call-start = ((), (), s32[]{:S(2)}) async-start(), calls=%async_computation.9 | async-start | bytes 5242880 | tf_op jit(solution)/shard_map/all_gather | solution.py:758
  62.9 95.9 %copy-start = (bf16[4,64,2048]{2,1,0:T(8,128)(2,1)S(1)}, bf16[4,64,2048]{2,1,0:T(8,128)(2,1)}, u32[]{:S(2)}) copy-start(bf16[4,64,2048]{2,1,0:T(8,128)(2,1)} %get-tuple-element.131) | copy-start | bytes 3145732
  66.0 135.4 %copy-start.21 = (f32[1,2048]{1,0:T(1,128)}, f32[1,2048]{1,0:T(1,128)S(1)}, u32[]{:S(2)}) copy-start(f32[1,2048]{1,0:T(1,128)S(1)} %reshape.351.gain) | copy-start | bytes 24580
  201.4 3.3 copy-start.4
  204.7 63.0 %all-to-all-start = ((bf16[4,1,64,2048]{3,2,1,0:T(8,128)(2,1)}), bf16[4,1,64,2048]{3,2,1,0:T(8,128)(2,1)S(1)}, u32[]{:S(2)}, u32[]{:S(2)}) async-start(bf16[4,1,64,2048]{3,2,1,0:T(8,128)(2,1)} %bitcast.288), calls=%async_computation | async-start | bytes 2097152 | tf_op jit(solution)/shard_map/all_to_all | solution.py:762
  266.4 2.2 copy-start.26
  355.1 3.3 copy-start.23
  358.3 36.2 %copy-start.2 = (f32[256,2048]{1,0:T(8,128)}, f32[256,2048]{1,0:T(8,128)S(1)}, u32[]{:S(2)}) copy-start(f32[256,2048]{1,0:T(8,128)S(1)} %get-tuple-element.136.hid) | copy-start | bytes 6291460
  373.5 21.0 %copy-start.16 = (bf16[256,2048]{1,0:T(8,128)(2,1)S(1)}, bf16[256,2048]{1,0:T(8,128)(2,1)}, u32[]{:S(2)}) copy-start(bf16[256,2048]{1,0:T(8,128)(2,1)} %get-tuple-element.139.cot) | copy-start | bytes 3145732
  394.5 94.2 %copy-start.9 = (bf16[4,1,64,2048]{3,2,1,0:T(8,128)(2,1)S(1)}, bf16[4,1,64,2048]{3,2,1,0:T(8,128)(2,1)}, u32[]{:S(2)}) copy-start(bf16[4,1,64,2048]{3,2,1,0:T(8,128)(2,1)} %copy-done.7) | copy-start | bytes 3145732
  488.7 6.6 copy-start.14
  488.7 6.6 copy-start.25
  488.7 6.7 copy-start.27
  498.7 2.6 copy-start.28
  498.7 2.6 copy-start.29
  501.4 2.4 copy-start.24
  511.4 2.3 copy-start.24
  521.5 2.3 copy-start.24
  531.6 2.3 copy-start.24
  541.8 6.6 copy-start.31
  550.5 18.8 %all-to-all-start.1 = ((bf16[4,1,64,2048]{3,2,1,0:T(8,128)(2,1)}), bf16[4,1,64,2048]{3,2,1,0:T(8,128)(2,1)}, u32[]{:S(2)}, u32[]{:S(2)}) async-start(bf16[4,1,64,2048]{3,2,1,0:T(8,128)(2,1)} %bitcast.54), calls=%async_computation.3 | async-start | bytes 2097152 | tf_op jit(solution)/shard_map/all_to_all | solution.py:864
  554.8 265.4 %reduce-scatter.9.cloned.1.call-start = ((), (), s32[]{:S(2)}) async-start(), calls=%async_computation.12 | async-start | bytes 1310720 | tf_op jit(solution)/shard_map/reduce_scatter | solution.py:865
  569.3 252.6 %reduce-scatter.5.cloned.1.call-start = ((), (), s32[]{:S(2)}) async-start(), calls=%async_computation.10 | async-start | bytes 3932160 | tf_op jit(solution)/shard_map/reduce_scatter | solution.py:884
  581.2 240.8 %reduce-scatter.7.cloned.1.call-start = ((), (), s32[]{:S(2)}) async-start(), calls=%async_computation.11 | async-start | bytes 5242880 | tf_op jit(solution)/shard_map/reduce_scatter | solution.py:854
  595.2 273.5 %reduce-scatter.11.cloned.1.call-start = ((), (), s32[]{:S(2)}) async-start(), calls=%async_computation.13 | async-start | bytes 5242880 | tf_op jit(solution)/shard_map/reduce_scatter | solution.py:849
  612.0 2.3 copy-start.11
  614.2 2.2 copy-start.12
  616.4 96.9 %copy-start.1 = (bf16[4,64,2048]{2,1,0:T(8,128)(2,1)S(1)}, bf16[4,64,2048]{2,1,0:T(8,128)(2,1)}, u32[]{:S(2)}) copy-start(bf16[4,64,2048]{2,1,0:T(8,128)(2,1)} %get-tuple-element.131) | copy-start | bytes 3145732
  616.4 96.9 %copy-start.13 = (bf16[2048,768]{1,0:T(8,128)(2,1)S(1)}, bf16[2048,768]{1,0:T(8,128)(2,1)}, u32[]{:S(2)}) copy-start(bf16[2048,768]{1,0:T(8,128)(2,1)} %all-gather.5.cloned.1.call-done.weight) | copy-start | bytes 9437188
  616.4 97.0 %copy-start.15 = (f32[256,2048]{1,0:T(8,128)S(1)}, f32[256,2048]{1,0:T(8,128)}, u32[]{:S(2)}) copy-start(f32[256,2048]{1,0:T(8,128)} %copy-done.14) | copy-start | bytes 6291460
  616.4 97.0 %copy-start.22 = (f32[1,2048]{1,0:T(1,128)S(1)}, f32[1,2048]{1,0:T(1,128)}, u32[]{:S(2)}) copy-start(f32[1,2048]{1,0:T(1,128)} %copy-done.21) | copy-start | bytes 24580
  713.3 103.9 %copy-start.5 = (bf16[4,64,2048]{2,1,0:T(8,128)(2,1)}, bf16[4,64,2048]{2,1,0:T(8,128)(2,1)S(1)}, u32[]{:S(2)}) copy-start(bf16[4,64,2048]{2,1,0:T(8,128)(2,1)S(1)} %result_return.1) | copy-start | bytes 3145732
  864.2 7.4 copy-start.6
  864.2 8.4 copy-start.18
  (8 other events, 9.1 us)
Sparse Core Ops, SparseCore 0:
  9.6 44.8 all-gather.6
  61.7 79.6 all-gather.4
  143.0 79.9 all-gather.8
  224.5 79.2 all-gather.10
  569.4 22.4 reduce-scatter.8
  594.2 60.4 reduce-scatter.4
  657.1 96.6 reduce-scatter.6
  756.1 96.6 reduce-scatter.10

commit v3 on v2

--- a/solution.py
+++ b/solution.py
@@ -101,16 +101,19 @@
         started.append(made)
         return made
 
+    yield
     x0.wait_recv()
     d0 = pass_on(5, on_x, 0, across)
     pass_on(6, on_x, 0, twin)
     y1.wait_recv()
     d1 = pass_on(7, on_y, 1, beside)
     pass_on(8, on_y, 1, twin)
+    yield
     x1.wait_recv()
     pass_on(9, on_x, 1, twin)
     y0.wait_recv()
     pass_on(10, on_y, 0, twin)
+    yield
     d0.wait_recv()
     pass_on(11, diag, 0, twin)
     d1.wait_recv()
@@ -122,6 +125,11 @@
     kept.wait()
 
 
+def run(steps):
+    for _ in steps:
+        pass
+
+
 SPREAD = 13
 
 
@@ -141,36 +149,40 @@
         lax.fori_loop(0, tiles, step, 0)
 
     to_twins = []
-    for k in range(4):
-
-        def first(cols, k=k):
+
+    def for_twin(k):
+        def term(cols):
             to_twin[k, :, cols] = multiply(other[k], cols).astype(BF)
 
-        each_tile(first)
+        each_tile(term)
         to_twins.append(copy(k, to_twin.at[k], from_twin.at[k], twin))
+
+    def for_here(k):
+        to_twins[k].wait_recv()
+
+        def term(cols):
+            both = multiply(here[k], cols) + from_twin[k, :, cols].astype(F32)
+            if k < 3:
+                mine[k, :, cols] = both.astype(BF)
+            else:
+                total[:, cols] = both
+
+        each_tile(term)
+
     started = []
-    for k in range(4):
-        to_twins[k].wait_recv()
-        if k < 3:
-
-            def second(cols, k=k):
-                term = multiply(here[k], cols) + from_twin[k, :, cols].astype(F32)
-                mine[k, :, cols] = term.astype(BF)
-
-            each_tile(second)
-        else:
-
-            def third(cols):
-                total[:, cols] = multiply(here[3], cols) + from_twin[3, :, cols].astype(F32)
-
-            each_tile(third)
-        if k == 0:
-            dx = copy(4, mine.at[0, parts[0]], in_x.at[0], beside)
-            dy = copy(5, mine.at[0, parts[1]], in_y.at[0], across)
-        elif k == 1:
-            started.append(copy(6, mine.at[1, parts[0]], in_x.at[1], beside))
-        elif k == 2:
-            started.append(copy(7, mine.at[2, parts[1]], in_y.at[1], across))
+    for_twin(0)
+    for_twin(1)
+    for_here(0)
+    dx = copy(4, mine.at[0, parts[0]], in_x.at[0], beside)
+    dy = copy(5, mine.at[0, parts[1]], in_y.at[0], across)
+    for_twin(2)
+    for_here(1)
+    started.append(copy(6, mine.at[1, parts[0]], in_x.at[1], beside))
+    for_twin(3)
+    for_here(2)
+    started.append(copy(7, mine.at[2, parts[1]], in_y.at[1], across))
+    for_here(3)
+    yield
 
     def add(k, part, arrived):
         def step(t, carry):
@@ -187,6 +199,7 @@
     dx.wait_recv()
     add(2, 0, in_x)
     started.append(copy(9, mine.at[2, parts[0]], in_y.at[2], across))
+    yield
     for made in started:
         made.wait_recv()
 
@@ -354,7 +367,7 @@
 
     each_chunk(own.shape[0], chunk)
     meet(near)
-    spread(own, out, send, recv, local)
+    run(spread(own, out, send, recv, local))
 
 
 def norm_gather(tok, gain, shift, plane, order):
@@ -378,46 +391,192 @@
     )(tok, gain, shift)
 
 
-def cot_kernel(n_blk, x_ref, tok, out, send, recv, local, g_send, g_recv):
-    (s, b, u), near, _, _ = place()
-    column = blk_peers(n_blk)
-    meet(list(near) + column)
-    copy = sender(g_send, g_recv)
-    count = x_ref.shape[1]
-    own_rows = pl.ds(pl.multiple_of(b * count, count), count)
-    started = [
-        copy(j, x_ref.at[peer[1]], tok.at[own_rows], peer) for j, peer in enumerate(column)
-    ]
-    kept = pltpu.make_async_copy(x_ref.at[b], tok.at[own_rows], local)
-    kept.start()
-    kept.wait()
-    for made in started:
-        made.wait()
-    spread(tok, out, send, recv, local)
-
-
-def cot_gather(x, plane):
-    n_blk, count, width = x.shape
-    rows = n_blk * count
+BLOCK = 256
+
+
+def document_start(bounds, s, position):
+    first, second = bounds[2 * s], bounds[2 * s + 1]
+    return jnp.where(position >= second, second, jnp.where(position >= first, first, 0))
+
+
+def chunks_of(layout):
+    n_seq, n_uly, n_blk, part, _ = layout
+    for s in range(n_seq):
+        for b in range(n_blk):
+            for u in range(n_uly):
+                yield ((s * n_uly + u) * n_blk + b) * part, s, (b * n_uly + u) * part
+
+
+def attend_kernel(
+    layout, bounds, qkv, cot, low, natural, attended, logs, out, send, recv, local,
+):
+    _, near, _, _ = place()
+    _, _, _, part, heads = layout
+    meet(near)
+    moving = spread(cot, out, send, recv, local)
+    next(moving)
+    share = heads * HD
+    pairs, length = natural.shape[1:3]
+    for row, s, position in chunks_of(layout):
+        for kind in range(3):
+            for h in range(heads):
+                lane = kind * share + h * HD
+                natural[kind, s * heads + h, position : position + part] = qkv[
+                    row : row + part, lane : lane + HD
+                ]
+
+    def pair(p, carry):
+        for start in range(0, length, BLOCK):
+            stop = start + BLOCK
+            scores = against(natural[0, p, start:stop], natural[1, p, :stop])
+            row = start + lax.broadcasted_iota(jnp.int32, (BLOCK, 1), 0)
+            key = lax.broadcasted_iota(jnp.int32, (BLOCK, stop), 1)
+            allowed = (key >= document_start(bounds, p // heads, row)) & (key <= row)
+            scores = jnp.where(allowed, scores, NEGATIVE)
+            top = jnp.max(scores, axis=1, keepdims=True)
+            powered = jnp.exp(scores - top)
+            total = jnp.sum(powered, axis=1, keepdims=True)
+            made = product(powered.astype(BF), natural[2, p, :stop])
+            attended[p, start:stop] = made / total
+            log_total = jnp.broadcast_to(top + jnp.log(total), (BLOCK, HD))
+            logs[p, :, start:stop] = log_total.T[:8]
+        return carry
+
+    cut = (pairs + 1) // 2
+    lax.fori_loop(0, cut, pair, 0)
+    next(moving)
+    lax.fori_loop(cut, pairs, pair, 0)
+    next(moving)
+    for row, s, position in chunks_of(layout):
+        for h in range(heads):
+            low[row : row + part, h * HD : (h + 1) * HD] = attended[
+                s * heads + h, position : position + part
+            ].astype(BF)
+    run(moving)
+
+
+def attend(bounds, qkv, cot, plane, layout):
+    n_seq, n_uly, n_blk, part, heads = layout
+    rows, width = cot.shape
+    pairs, length = n_seq * heads, n_uly * n_blk * part
     return pl.pallas_call(
-        functools.partial(cot_kernel, n_blk),
-        name="cot_gather",
+        functools.partial(attend_kernel, layout),
+        name="attend",
         out_shape=(
-            jax.ShapeDtypeStruct((rows, width), BF),
+            jax.ShapeDtypeStruct((qkv.shape[0], heads * HD), BF),
+            jax.ShapeDtypeStruct((3, pairs, length, HD), BF),
+            jax.ShapeDtypeStruct((pairs, length, HD), F32),
+            jax.ShapeDtypeStruct((pairs, 8, length), F32),
             jax.ShapeDtypeStruct((plane, rows, width), BF),
         ),
-        in_specs=[ANY],
-        out_specs=(ANY, ANY),
+        in_specs=[pl.BlockSpec(memory_space=pltpu.SMEM), VMEM, ANY],
+        out_specs=(VMEM, VMEM, VMEM, VMEM, ANY),
         scratch_shapes=[
             pltpu.SemaphoreType.DMA((SPREAD,)),
             pltpu.SemaphoreType.DMA((SPREAD,)),
             pltpu.SemaphoreType.DMA,
-            pltpu.SemaphoreType.DMA((n_blk - 1,)),
-            pltpu.SemaphoreType.DMA((n_blk - 1,)),
         ],
-        compiler_params=pltpu.CompilerParams(collective_id=2, has_side_effects=True),
-        cost_estimate=pl.CostEstimate(flops=0, bytes_accessed=120 * MIB, transcendentals=0),
-    )(x)
+        compiler_params=pltpu.CompilerParams(
+            collective_id=2, has_side_effects=True, vmem_limit_bytes=40 * MIB
+        ),
+        cost_estimate=pl.CostEstimate(flops=0, bytes_accessed=150 * MIB, transcendentals=0),
+    )(bounds, qkv, cot)
+
+
+def attend_back_kernel(
+    layout, scale, bounds, grad, natural, attended, logs, act, weight, hid, bias, back, out,
+    grads, grads_back, key_grad, value_grad,
+    total, to_twin, from_twin, mine, in_x, in_y, c_send, c_recv,
+):
+    _, near, _, _ = place()
+    rows = total.shape[0]
+    _, _, _, part, heads = layout
+    share = heads * HD
+    meet(near)
+
+    def multiply(block, cols):
+        return product(rows_of(act, block, rows), weight[:, cols])
+
+    moving = collect(multiply, total, to_twin, from_twin, mine, in_x, in_y, c_send, c_recv)
+    next(moving)
+    pairs, length = natural.shape[1:3]
+    for row, s, position in chunks_of(layout):
+        for h in range(heads):
+            grads[s * heads + h, position : position + part] = grad[
+                row : row + part, h * HD : (h + 1) * HD
+            ]
+
+    def pair(p, carry):
+        for start in reversed(range(0, length, BLOCK)):
+            stop = start + BLOCK
+            query, key, value = (
+                natural[0, p, start:stop], natural[1, p, :stop], natural[2, p, :stop]
+            )
+            above = grads[p, start:stop]
+            row = start + lax.broadcasted_iota(jnp.int32, (1, BLOCK), 1)
+            at = lax.broadcasted_iota(jnp.int32, (stop, BLOCK), 0)
+            allowed = (at >= document_start(bounds, p // heads, row)) & (at <= row)
+            scores = jnp.where(allowed, against(key, query), NEGATIVE)
+            chances = jnp.exp(scores - logs[p, 0:1, start:stop])
+            dots = (above.astype(F32) * attended[p, start:stop]).T
+            dots = jnp.sum(dots, axis=0, keepdims=True)
+            by_value = product(chances.astype(BF), above)
+            scored = (chances * (against(value, above) - dots)).astype(BF)
+            by_key = product(scored, query)
+            grads_back[p, start:stop] = (transposed(scored, key) * scale).astype(BF)
+            if stop == length:
+                key_grad[...] = by_key
+                value_grad[...] = by_value
+            else:
+                key_grad[:stop] += by_key
+                value_grad[:stop] += by_value
+        grads_back[pairs + p] = key_grad[...].astype(BF)
+        grads_back[2 * pairs + p] = value_grad[...].astype(BF)
+        return carry
+
+    cut = (pairs + 1) // 2
+    lax.fori_loop(0, cut, pair, 0)
+    next(moving)
+    lax.fori_loop(cut, pairs, pair, 0)
+    for row, s, position in chunks_of(layout):
+        for kind in range(3):
+            for h in range(heads):
+                lane = kind * share + h * HD
+                back[row : row + part, lane : lane + HD] = grads_back[
+                    kind * pairs + s * heads + h, position : position + part
+                ]
+    run(moving)
+
+    def chunk(at):
+        out[at] = (total[at] + hid[at] + bias[...]).astype(BF)
+
+    each_chunk(rows, chunk)
+
+
+def attend_back(bounds, grad, natural, attended, logs, act, weight, hid, bias, layout, scale):
+    rows, width = hid.shape
+    pairs, length = natural.shape[1:3]
+    return pl.pallas_call(
+        functools.partial(attend_back_kernel, layout, scale),
+        name="attend_back",
+        out_shape=(
+            jax.ShapeDtypeStruct((grad.shape[0], 3 * grad.shape[1]), BF),
+            jax.ShapeDtypeStruct((rows, width), BF),
+        ),
+        in_specs=[pl.BlockSpec(memory_space=pltpu.SMEM)] + [VMEM] * 8,
+        out_specs=(VMEM, VMEM),
+        scratch_shapes=[
+            pltpu.VMEM((pairs, length, HD), BF),
+            pltpu.VMEM((3 * pairs, length, HD), BF),
+            pltpu.VMEM((length, HD), F32),
+            pltpu.VMEM((length, HD), F32),
+        ]
+        + collect_scratch(rows, width),
+        compiler_params=pltpu.CompilerParams(
+            collective_id=5, has_side_effects=True, vmem_limit_bytes=60 * MIB
+        ),
+        cost_estimate=pl.CostEstimate(flops=0, bytes_accessed=200 * MIB, transcendentals=0),
+    )(bounds, grad, natural, attended, logs, act, weight, hid, bias)
 
 
 def rows_of(ref, block, rows):
@@ -435,7 +594,7 @@
     def multiply(block, cols):
         return product(rows_of(act, block, rows), weight[:, cols])
 
-    collect(multiply, total, to_twin, from_twin, mine, in_x, in_y, c_send, c_recv)
+    run(collect(multiply, total, to_twin, from_twin, mine, in_x, in_y, c_send, c_recv))
 
     def chunk(at):
         values = total[at] + tok[at].astype(F32) + bias[...]
@@ -444,7 +603,7 @@
         own[at] = reorder(unit * gain[...] + shift[...], *order).astype(BF)
 
     each_chunk(rows, chunk)
-    spread(own, out, send, recv, local)
+    run(spread(own, out, send, recv, local))
 
 
 def hidden_gather(act, weight, tok, bias, gain, shift, plane, order):
@@ -483,7 +642,7 @@
     def multiply(block, cols):
         return against(rows_of(act, block, rows), weight[cols, :])
 
-    collect(multiply, total, to_twin, from_twin, mine, in_x, in_y, c_send, c_recv)
+    run(collect(multiply, total, to_twin, from_twin, mine, in_x, in_y, c_send, c_recv))
     sums[...] = jnp.zeros_like(sums)
     inner, outer, lanes = order[1], order[0], order[2]
 
@@ -501,7 +660,7 @@
         sums[3:4] += row_sum(passed)
 
     each_chunk(rows, chunk)
-    spread(own, out, send, recv, local)
+    run(spread(own, out, send, recv, local))
 
 
 def branch_gather(act, weight, hid, cot, gain, plane, order):
@@ -530,48 +689,6 @@
     )(act, weight, hid, cot, gain)
 
 
-def result_kernel(
-    n_blk, act, weight, hid, bias, out,
-    total, to_twin, from_twin, mine, in_x, in_y, c_send, c_recv, own, send, recv, local,
-):
-    _, near, _, _ = place()
-    rows = total.shape[0]
-    meet(list(near) + blk_peers(n_blk))
-
-    def multiply(block, cols):
-        return product(rows_of(act, block, rows), weight[:, cols])
-
-    collect(multiply, total, to_twin, from_twin, mine, in_x, in_y, c_send, c_recv)
-
-    def chunk(at):
-        own[at] = (total[at] + hid[at] + bias[...]).astype(BF)
-
-    each_chunk(rows, chunk)
-    return_rows(own, out, n_blk, send, recv, local)
-
-
-def result_return(act, weight, hid, bias, n_blk):
-    rows, width = hid.shape
-    return pl.pallas_call(
-        functools.partial(result_kernel, n_blk),
-        name="result_return",
-        out_shape=jax.ShapeDtypeStruct((n_blk, rows // n_blk, width), BF),
-        in_specs=[VMEM] * 4,
-        out_specs=ANY,
-        scratch_shapes=collect_scratch(rows, width)
-        + [
-            pltpu.VMEM((rows, width), BF),
-            pltpu.SemaphoreType.DMA((n_blk - 1,)),
-            pltpu.SemaphoreType.DMA((n_blk - 1,)),
-            pltpu.SemaphoreType.DMA,
-        ],
-        compiler_params=pltpu.CompilerParams(
-            collective_id=5, has_side_effects=True, vmem_limit_bytes=40 * MIB
-        ),
-        cost_estimate=pl.CostEstimate(flops=0, bytes_accessed=180 * MIB, transcendentals=0),
-    )(act, weight, hid, bias)
-
-
 def inputs_kernel(
     n_blk, order, act, weight, tok, grad_hidden, gain, sums, out,
     total, to_twin, from_twin, mine, in_x, in_y, c_send, c_recv, own, send, recv, local,
@@ -583,7 +700,7 @@
     def multiply(block, cols):
         return against(rows_of(act, block, rows), weight[cols, :])
 
-    collect(multiply, total, to_twin, from_twin, mine, in_x, in_y, c_send, c_recv)
+    run(collect(multiply, total, to_twin, from_twin, mine, in_x, in_y, c_send, c_recv))
     sums[...] = jnp.zeros_like(sums)
     inner, outer, lanes = order[1], order[0], order[2]
 
@@ -741,6 +858,9 @@
         block = block.reshape(n_blk // sharing, sharing, held, part, width)
         return block.transpose(0, 2, 1, 3, 4).reshape(seqs, tok, width)
 
+    def over(block):
+        return lax.all_to_all(block, "blk", split_axis=0, concat_axis=0, tiled=True)
+
     vectors = (ln1_gain, ln1_shift, b_query, b_value, b_out, ln2_gain, ln2_shift, b_proj)
     small = jnp.concatenate(
         [v.astype(F32) for v in vectors + (b_fc, doc_lengths.reshape(-1))]
@@ -780,65 +900,61 @@
 
     normed = norm_gather(tokens, gain_one, shift_one, plane, order)
     normed = normed.reshape(plane * n_rows, width)
-    grad_out, grad_all = cot_gather(by_plane(cotangent), plane)
-    grad_all = grad_all.reshape(plane * n_rows, width)
+    grad_out = over(by_plane(cotangent)).reshape(n_rows, width)
 
     made = product(normed, qkv)
-    queries = ((made[:, :share] + bias_q) * scale).astype(BF)
-    keys = made[:, share : 2 * share].astype(BF)
-    values = (made[:, 2 * share :] + bias_v).astype(BF)
+    bias_all = jnp.concatenate([bias_q, jnp.zeros_like(bias_q), bias_v], axis=1)
+    scales = jnp.repeat(jnp.array([[scale, 1.0, 1.0]], F32), share, axis=1)
+    made = ((made + bias_all) * scales).astype(BF)
 
     groups = [
         [g * sharing + i for i in range(sharing)] for g in range(n_blk // sharing)
     ]
     pairs = n_seq * held * heads // sharing
     length = n_blk * n_uly * tok
-
-    def to_heads(matrix):
-        matrix = matrix.reshape(n_seq, n_uly, n_blk, held, part, heads, HD)
-        matrix = matrix.transpose(0, 3, 5, 2, 1, 4, 6)
-        matrix = matrix.reshape(n_seq * held * heads, n_blk, n_uly, 1, part, HD)
+    if sharing == held == 1:
+        layout = (n_seq, n_uly, n_blk, part, heads)
+    else:
+        layout = (pairs, 1, 1, length, 1)
+
+    def to_heads(matrix, kinds):
+        if sharing == held == 1:
+            return matrix
+        matrix = matrix.reshape(n_seq, n_uly, n_blk, held, part, kinds, heads, HD)
+        matrix = matrix.transpose(0, 3, 6, 2, 1, 4, 5, 7)
+        matrix = matrix.reshape(n_seq * held * heads, n_blk, n_uly, 1, part, kinds * HD)
         if sharing > 1:
             matrix = lax.all_to_all(
                 matrix, "blk", split_axis=0, concat_axis=3, axis_index_groups=groups, tiled=True
             )
-        return matrix.reshape(pairs, length, HD)
-
-    def from_heads(matrix):
-        matrix = matrix.reshape(pairs, n_blk, n_uly, sharing, part, HD)
+        return matrix.reshape(pairs * length, kinds * HD)
+
+    def from_heads(matrix, kinds):
+        if sharing == held == 1:
+            return matrix
+        matrix = matrix.reshape(pairs, n_blk, n_uly, sharing, part, kinds * HD)
         if sharing > 1:
             matrix = lax.all_to_all(
                 matrix, "blk", split_axis=3, concat_axis=0, axis_index_groups=groups, tiled=True
             )
-        matrix = matrix.reshape(n_seq, held, heads, n_blk, n_uly, part, HD)
-        return matrix.transpose(0, 4, 3, 1, 5, 2, 6).reshape(plane * n_rows, share)
-
-    hq, hk, hv = to_heads(queries), to_heads(keys), to_heads(values)
+        matrix = matrix.reshape(n_seq, held, heads, n_blk, n_uly, part, kinds, HD)
+        matrix = matrix.transpose(0, 4, 3, 1, 5, 6, 2, 7)
+        return matrix.reshape(plane * n_rows, kinds * share)
+
     turn = here_blk % sharing
-    pair_at = turn * pairs + jnp.arange(pairs)
+    pair_at = turn * pairs + jnp.arange(layout[0]) * layout[4]
     seq_of = pair_at // (held * heads)
     held_of = (pair_at // heads) % held
     which = (here_blk // sharing) * held + held_of
     own_lengths = lengths[seq_of, which]
     first = own_lengths[:, 0:1]
-    second = first + own_lengths[:, 1:2]
-    position = jnp.arange(length, dtype=jnp.int32)[None]
-    doc = (position >= first).astype(jnp.int32) + (position >= second).astype(jnp.int32)
-    allowed = (doc[:, :, None] == doc[:, None, :]) & (
-        position[:, None, :] <= position[:, :, None]
-    )
-
-    def head_forward(args):
-        q, k, v, ok = args
-        scores = jnp.where(ok, against(q, k), NEGATIVE)
-        top = jnp.max(scores, axis=1, keepdims=True)
-        powered = jnp.exp(scores - top)
-        total = jnp.sum(powered, axis=1, keepdims=True)
-        result = product(powered.astype(BF), v) / total
-        return result, top + jnp.log(total)
-
-    attended, log_total = lax.map(head_forward, (hq, hk, hv, allowed))
-    attended_low = from_heads(attended.astype(BF))
+    bounds = jnp.concatenate([first, first + own_lengths[:, 1:2]], axis=1).reshape(-1)
+
+    attended_low, natural, attended, logs, grad_all = attend(
+        bounds, to_heads(made, 3), grad_out, plane, layout
+    )
+    grad_all = grad_all.reshape(plane * n_rows, width)
+    attended_low = from_heads(attended_low, 1)
     hidden, normed_two = hidden_gather(
         attended_low, out_part, tokens, bias_out, gain_two, shift_two, plane, order
     )
@@ -858,28 +974,18 @@
         grad_inner, fc, hidden, grad_out, gain_two, plane, order
     )
     branch_all = branch_all.reshape(plane * n_rows, width)
-    result = result_return(active, proj, hidden, bias_proj, n_blk)
     grad_w_out = transposed(attended_low, branch_all).astype(BF)
     grad_w_out = grad_w_out.reshape(n_blk // n_uly, n_uly, rows, width).transpose(1, 0, 2, 3)
     grad_w_out = lax.all_to_all(grad_w_out, "uly", split_axis=0, concat_axis=0, tiled=True)
     grad_w_out = lax.psum_scatter(
         grad_w_out.reshape(n_blk * rows, width), "blk", scatter_dimension=0, tiled=True
     ).astype(F32)
-    grad_heads = to_heads(against(branch_all, out_part).astype(BF))
-
-    def head_backward(args):
-        q, k, v, ok, grad, kept, logs = args
-        dots = jnp.sum(grad.astype(F32) * kept, axis=1, keepdims=True)
-        scores = jnp.where(ok, against(q, k), NEGATIVE)
-        chances = jnp.exp(scores - logs)
-        grad_v = transposed(chances.astype(BF), grad)
-        grad_scores = (chances * (against(grad, v) - dots)).astype(BF)
-        grad_q = product(grad_scores, k) * scale
-        grad_k = transposed(grad_scores, q)
-        return grad_q.astype(BF), grad_k.astype(BF), grad_v.astype(BF)
-
-    backs = lax.map(head_backward, (hq, hk, hv, allowed, grad_heads, attended, log_total))
-    backs = jnp.concatenate([from_heads(b) for b in backs], axis=1)
+    grad_heads = to_heads(against(branch_all, out_part).astype(BF), 1)
+    backs, result = attend_back(
+        bounds, grad_heads, natural, attended, logs, active, proj, hidden, bias_proj, layout, scale
+    )
+    result = over(result.reshape(n_blk, held * part, width))
+    backs = from_heads(backs, 3)
     grad_bias = jnp.sum(backs.astype(F32), axis=0)
     grad_qkv = lax.psum_scatter(
         transposed(normed, backs).astype(BF), "blk", scatter_dimension=0, tiled=True

time: 891 us -> 795 us (0.89)
  Pallas kernels: 575 us -> 478 us
  waiting for transfers between devices: 13.7 us -> 106 us
  matrix products: 147 us -> 100 us
  local copies, waits for them, and re-layouts: 95.7 us -> 60.2 us
  other arithmetic: 25.7 us -> 7.08 us
  starting transfers between devices: 8.25 us -> 19.9 us
    pallas_call x2, Pallas kernels: 185 us -> 92.4 us  [the longest x1 51.6 us: attend_back(): pl.pallas_call(functools.partial(attend_back_kernel, layout, scale), name...]
    reduce_scatter x1, waiting for transfers between devices: 0.01 us -> 35.5 us  [on_device(): lax.psum_scatter(transposed(normed_two, grad_inner).astype(BF), 'blk', sc...]
    reduce_scatter x1, waiting for transfers between devices: 0.01 us -> 31.3 us  [on_device(): lax.psum_scatter(transposed(active, grad_all).astype(BF), 'blk', scatter_...]
    all_gather x4, waiting for transfers between devices: 0.03 us -> 23.7 us  [over_blk(): return lax.all_gather(matrix, 'blk', axis=0, tiled=True)]
    dot_general x14 -> x2, matrix products: 48.4 us -> 28.6 us  [against(): lax.dot_general(left_side, right_side, (((1,), (1,)), ((), ())), preferre...]
    dot_general x10 -> x2, matrix products: 42.4 us -> 24.5 us  [product(): return jnp.dot(left_side, right_side, preferred_element_type=F32)]
    all_to_all x0 -> x2, starting transfers between devices: none -> 11.4 us  [over(): return lax.all_to_all(block, 'blk', split_axis=0, concat_axis=0, tiled=True)]
    reduce_sum x8 -> x0, other arithmetic: 10.4 us -> none  [the longest x4 6.45 us: head_backward(): dots = jnp.sum(grad.astype(F32) * kept, axis=1, keepdims=True)]
  transfers between devices with their start and end apart: 10 -> 12, of which waited for: 1 -> 5; matrix products, arithmetic and copies ran while one was open for 18% -> 14% of each run, Pallas kernels for 55% -> 49%
where the time goes in v3:
time: 795 us; the launch traced here: 787 us
  Pallas kernels  478 us (60%)
  waiting for transfers between devices  106 us (13%)
  matrix products  100 us (13%)
  local copies, waits for them, and re-layouts  60.2 us (8%)
  starting transfers between devices  19.9 us (3%)
  between operations  15.2 us (2%)
    pallas_call x1, Pallas kernels, inputs_return(): pl.pallas_call(functools.partial(inputs_kernel, n_blk, order), name='inpu...  101 us
    pallas_call x1, Pallas kernels, branch_gather(): pl.pallas_call(functools.partial(branch_kernel, order), name='branch_gath...  91.7 us
    pallas_call x1, Pallas kernels, hidden_gather(): pl.pallas_call(functools.partial(hidden_kernel, order), name='hidden_gath...  84.2 us
    pallas_call x1, Pallas kernels, attend_back(): pl.pallas_call(functools.partial(attend_back_kernel, layout, scale), name...  51.6 us
    dot_general x4, matrix products, transposed(): lax.dot_general(left_side, right_side, (((0,), (0,)), ((), ())), preferre...  47.1 us
    pallas_call x1, Pallas kernels, norm_gather(): pl.pallas_call(functools.partial(norm_kernel, order), name='norm_gather',...  42.9 us
    pallas_call x1, Pallas kernels, enter(): pl.pallas_call(functools.partial(entry_kernel, n_blk), name='enter', out_...  42.2 us
    pallas_call x1, Pallas kernels, attend(): pl.pallas_call(functools.partial(attend_kernel, layout), name='attend', o...  40.8 us
  transfers between devices with their start and end apart: 12, of which 5 were waited for; matrix products, arithmetic and copies ran while one was open for 14% of the time, Pallas kernels for 49%

profile of v3, /device:TPU:8, one launch (start us, length us, event | category | flops | bytes accessed | tf_op | source)
XLA Modules:
  0.0 787.1 jit_solution(17845592338659314217)
XLA Ops:
  9.5 1.0 copy.106
  12.3 1.8 maximum_bitcast_fusion
  14.2 1.7 reshape.227.qkv_ref
  17.0 1.5 reshape.229.fc_ref
  19.4 42.2 %enter.1 = (bf16[4,64,2048]{2,1,0:T(8,128)(2,1)}, bf16[8,64,768]{2,1,0:T(8,128)(2,1)}, bf16[8,64,1024]{2,1,0:T(8,128)(2,1)}, f32[8,4,8,128]{3,2,1,0:T(8,128)}) custom-call(bf16[4,64,2048]{2,1,0:T(8,128)(2,1)} %x_ref.1, bf16[8,64,768]{2,1,0:T(8,128)(2,1)} %reshape.227.qkv_ref, bf16[8,64,1024]{2,1,0:T(8,128)(2,1)} %reshape.229.fc_ref, ...), custom_call_target="tpu_custom_call" | custom-call | bytes 62914560 | tf_op jit(solution)/shard_map/enter/pallas_call | solution.py:338
  63.0 3.8 all-to-all-start
  69.6 1.3 copy-done.1
  70.8 42.9 %norm_gather.1 = bf16[8,256,2048]{2,1,0:T(8,128)(2,1)S(1)} custom-call(bf16[256,2048]{1,0:T(8,128)(2,1)S(1)} %bitcast.81, f32[1,2048]{1,0:T(1,128)S(1)} %reshape.235.gain, f32[1,2048]{1,0:T(1,128)S(1)} %reshape.236.shift), custom_call_target="tpu_custom_call" | custom-call | bytes 104857600 | tf_op jit(solution)/shard_map/norm_gather/pallas_call | solution.py:375
  113.8 3.2 copy-done.6
  117.1 4.5 all-to-all-start.1
  121.6 18.9 %all-gather.5.cloned.1.call-done.weight = bf16[2048,768]{1,0:T(8,128)(2,1)} async-done(((bf16[512,768]{1,0:T(8,128)(2,1)}), bf16[2048,768]{1,0:T(8,128)(2,1)}) %all-gather.5.cloned.1.call-update) | async-done | bytes 3145744 | tf_op jit(solution)/shard_map/all_gather | solution.py:878
  140.5 10.1 %multiply_convert_fusion.1.qkv = bf16[2048,768]{1,0:T(8,128)(2,1)S(1)} fusion(f32[768]{0:T(1024)S(1)} %broadcast_in_dim.15, f32[768]{0:T(1024)S(1)} %fusion.8, bf16[2048,2048]{1,0:T(8,128)(2,1)} %bitcast.84, bf16[2048,768]{1,0:T(8,128)(2,1)} %all-gather.5.cloned.1.call-done.weight), kind=kOutput, calls=%fused_computation.13 | convolution fusion | flops 6447169536 | bytes 14686208 | tf_op jit(solution)/shard_map/dot_general | solution.py:31
  150.6 40.8 %attend.1 = (bf16[2048,256]{1,0:T(8,128)(2,1)S(1)}, bf16[3,4,1024,128]{3,2,1,0:T(8,128)(2,1)S(1)}, f32[4,1024,128]{2,1,0:T(8,128)S(1)}, f32[4,8,1024]{2,1,0:T(8,128)S(1)}, bf16[8,256,2048]{2,1,0:T(8,128)(2,1)}) custom-call(s32[4]{0:T(128)S(1)} %reshape.232.bounds, bf16[2048,768]{1,0:T(8,128)(2,1)S(1)} %multiply_convert_fusion.1.qkv, ...), custom_call_target="tpu_custom_call" | custom-call | bytes 157286400 | tf_op jit(solution)/shard_map/attend/pallas_call | solution.py:462
  191.5 1.7 copy-done.7
  193.1 1.3 copy-done.9
  195.1 84.2 %hidden_gather.1 = (f32[256,2048]{1,0:T(8,128)S(1)}, bf16[8,256,2048]{2,1,0:T(8,128)(2,1)S(1)}) custom-call(bf16[2048,256]{1,0:T(8,128)(2,1)S(1)} %get-tuple-element.42.act, bf16[256,2048]{1,0:T(8,128)(2,1)} %bitcast.11.weight, bf16[256,2048]{1,0:T(8,128)(2,1)S(1)} %bitcast.82, f32[1,2048]{1,0:T(1,128)S(1)} %reshape.244.bias, f32[1,2048]{1,0:T(1,128)S(1)} %reshape.245.gain, ...), custom_call_target="tpu_custom_call" | custom-call | bytes 262144000 | tf_op jit(solution)/shard_map/hidden_gather/pallas_call | solution.py:611
  279.3 1.3 copy-done.4
  280.6 3.3 copy-done.18
  283.9 14.4 %fusion.18 = f32[2048,1024]{1,0:T(8,128)} fusion(bf16[2048,2048]{1,0:T(8,128)(2,1)} %bitcast.89, bf16[2048,1024]{1,0:T(8,128)(2,1)} %all-gather.11.cloned.1.call-done.weight), kind=kOutput, calls=%fused_computation.54 | convolution fusion | flops 8589934592 | bytes 20971520 | tf_op jit(solution)/shard_map/dot_general | solution.py:31
  298.3 4.8 all-gather.7.cloned.1.call-done.weight
  303.1 21.6 %convert_reduce_fusion = (f32[1024]{0:T(1024)S(1)}, bf16[2048,1024]{1,0:T(8,128)(2,1)}, bf16[2048,1024]{1,0:T(8,128)(2,1)}) fusion(f32[2048,1024]{1,0:T(8,128)} %fusion.18, f32[1024]{0:T(1024)S(1)} %bitcast.114, bf16[2048,2048]{1,0:T(8,128)(2,1)} %bitcast.116, bf16[1024,2048]{1,0:T(8,128)(2,1)} %all-gather.7.cloned.1.call-done.weight), kind=kOutput, calls=%fused_computation.10 | convolution fusion | flops 8642362368 | bytes 29368320 | tf_op jit(solution)/shard_map/dot_general | solution.py:41
  324.7 91.7 %branch_gather.1 = (f32[256,2048]{1,0:T(8,128)S(1)}, f32[8,2048]{1,0:T(8,128)S(1)}, bf16[8,256,2048]{2,1,0:T(8,128)(2,1)}) custom-call(bf16[2048,1024]{1,0:T(8,128)(2,1)} %get-tuple-element.66.act, bf16[2048,1024]{1,0:T(8,128)(2,1)} %all-gather.11.cloned.1.call-done.weight, f32[256,2048]{1,0:T(8,128)S(1)} %copy-done.5, bf16[256,2048]{1,0:T(8,128)(2,1)S(1)} %bitcast.80, ...), custom_call_target="tpu_custom_call" | custom-call | bytes 262144000 | tf_op jit(solution)/shard_map/branch_gather/pallas_call | solution.py:668
  416.5 7.5 convolution_convert_fusion.3
  423.9 3.5 all-to-all-start.3
  428.2 13.7 %all-to-all-done.3 = bf16[4,1,64,2048]{3,2,1,0:T(8,128)(2,1)S(1)} async-done(((bf16[4,1,64,2048]{3,2,1,0:T(8,128)(2,1)}), bf16[4,1,64,2048]{3,2,1,0:T(8,128)(2,1)S(1)}, u32[]{:S(2)}, u32[]{:S(2)}) %all-to-all-start.3) | async-done | bytes 1048608 | tf_op jit(solution)/shard_map/all_to_all | solution.py:979
  443.1 7.0 convolution_convert_fusion.4.grad
  450.1 51.6 %attend_back.1 = (bf16[2048,768]{1,0:T(8,128)(2,1)}, bf16[256,2048]{1,0:T(8,128)(2,1)}) custom-call(s32[4]{0:T(128)} %copy-done.17, bf16[2048,256]{1,0:T(8,128)(2,1)} %convolution_convert_fusion.4.grad, bf16[3,4,1024,128]{3,2,1,0:T(8,128)(2,1)} %copy-done.7, f32[4,1024,128]{2,1,0:T(8,128)} %copy-done.9, f32[4,8,1024]{2,1,0:T(8,128)} %copy-done.16, ...), custom_call_target="tpu_custom_call" | custom-call | bytes 209715200 | tf_op jit(solution)/shard_map/attend_back/pallas_call | solution.py:559
  501.7 11.4 %convolution_convert_fusion.2 = bf16[2048,768]{1,0:T(8,128)(2,1)} fusion(bf16[2048,2048]{1,0:T(8,128)(2,1)} %bitcast.85, bf16[2048,768]{1,0:T(8,128)(2,1)} %get-tuple-element.51.act), kind=kOutput, calls=%fused_computation.16 | convolution fusion | flops 6444023808 | bytes 14680064 | tf_op jit(solution)/shard_map/dot_general | solution.py:35
  513.1 14.2 %convolution_convert_fusion.1 = bf16[2048,1024]{1,0:T(8,128)(2,1)} fusion(bf16[2048,2048]{1,0:T(8,128)(2,1)} %bitcast.90, bf16[2048,1024]{1,0:T(8,128)(2,1)} %get-tuple-element.66.act), kind=kOutput, calls=%fused_computation.15 | convolution fusion | flops 8592031744 | bytes 16777216 | tf_op jit(solution)/shard_map/dot_general | solution.py:35
  527.4 14.1 %convolution_convert_fusion = bf16[1024,2048]{1,0:T(8,128)(2,1)} fusion(bf16[2048,1024]{1,0:T(8,128)(2,1)} %get-tuple-element.67.act, bf16[2048,2048]{1,0:T(8,128)(2,1)} %bitcast.117), kind=kOutput, calls=%fused_computation.14 | convolution fusion | flops 8592031744 | bytes 16777216 | tf_op jit(solution)/shard_map/dot_general | solution.py:35
  541.5 7.6 all-to-all-start.2
  549.1 1.2 copy-done.3
  550.3 1.9 copy-done.8
  552.2 1.6 copy-done.11
  553.8 101.0 %inputs_return.1 = (f32[8,2048]{1,0:T(8,128)S(1)}, bf16[4,64,2048]{2,1,0:T(8,128)(2,1)S(1)}) custom-call(bf16[2048,768]{1,0:T(8,128)(2,1)S(1)} %copy-done, bf16[2048,768]{1,0:T(8,128)(2,1)S(1)} %copy-done.8, bf16[256,2048]{1,0:T(8,128)(2,1)S(1)} %bitcast.83, f32[256,2048]{1,0:T(8,128)S(1)} %copy-done.11, f32[1,2048]{1,0:T(1,128)S(1)} %reshape.235.gain), custom_call_target="tpu_custom_call" | custom-call | bytes 188743680 | tf_op jit(solution)/shard_map/inputs_return/pallas_call | solution.py:720
  658.0 1.8 convert_element_type.127
  659.8 35.5 %reduce-scatter.7.cloned.1.call-done = bf16[512,1024]{1,0:T(8,128)(2,1)} async-done(((bf16[2048,1024]{1,0:T(8,128)(2,1)}), bf16[512,1024]{1,0:T(8,128)(2,1)}) %reduce-scatter.7.cloned.1.call-update) | async-done | bytes 1048592 | tf_op jit(solution)/shard_map/reduce_scatter | solution.py:970
  695.3 1.2 copy-done.14
  696.5 1.1 copy-done.15
  697.6 23.9 %finish.1 = (bf16[8,64,768]{2,1,0:T(8,128)(2,1)S(1)}, bf16[8,64,1024]{2,1,0:T(8,128)(2,1)S(1)}, f32[8,128]{1,0:T(8,128)S(1)}) custom-call(bf16[8,64,768]{2,1,0:T(8,128)(2,1)S(1)} %bitcast.87, bf16[8,64,1024]{2,1,0:T(8,128)(2,1)S(1)} %bitcast.86, f32[8,4,8,128]{3,2,1,0:T(8,128)S(1)} %reshape.257.small_ref), custom_call_target="tpu_custom_call" | custom-call | bytes 62914560 | tf_op jit(solution)/shard_map/finish/pallas_call | solution.py:789
  721.6 1.9 reshape.262
  723.5 4.3 copy.103
  727.8 3.3 reshape.260
  731.1 1.8 reshape.261
  732.9 4.6 fusion.14
  742.5 31.3 %reduce-scatter.11.cloned.1.call-done = bf16[256,2048]{1,0:T(8,128)(2,1)} async-done(((bf16[1024,2048]{1,0:T(8,128)(2,1)}), bf16[256,2048]{1,0:T(8,128)(2,1)}) %reduce-scatter.11.cloned.1.call-update) | async-done | bytes 1048592 | tf_op jit(solution)/shard_map/reduce_scatter | solution.py:965
  773.8 2.8 convert_element_type.133
  776.6 2.3 copy.119
  (153 shorter events, 21.8 us)
Async XLA Ops:
  7.2 8.7 %copy-start.20 = (bf16[64,8192]{1,0:T(8,128)(2,1)S(1)}, bf16[64,8192]{1,0:T(8,128)(2,1)}, u32[]{:S(2)}) copy-start(bf16[64,8192]{1,0:T(8,128)(2,1)} %param.32) | copy-start | bytes 3145732
  7.2 11.4 %copy-start.21 = (s32[4,3]{1,0:T(4,128)S(1)}, s32[4,3]{1,0:T(4,128)}, u32[]{:S(2)}) copy-start(s32[4,3]{1,0:T(4,128)} %param.20) | copy-start | bytes 148
  7.2 11.5 %copy-start.22 = (bf16[64]{0:T(256)(128)(2,1)S(1)}, bf16[64]{0:T(256)(128)(2,1)}, u32[]{:S(2)}) copy-start(bf16[64]{0:T(256)(128)(2,1)} %param.21) | copy-start | bytes 388
  7.2 11.5 %copy-start.23 = (bf16[64]{0:T(256)(128)(2,1)S(1)}, bf16[64]{0:T(256)(128)(2,1)}, u32[]{:S(2)}) copy-start(bf16[64]{0:T(256)(128)(2,1)} %param.22) | copy-start | bytes 388
  7.2 11.5 %copy-start.24 = (bf16[64]{0:T(256)(128)(2,1)S(1)}, bf16[64]{0:T(256)(128)(2,1)}, u32[]{:S(2)}) copy-start(bf16[64]{0:T(256)(128)(2,1)} %param.24) | copy-start | bytes 388
  7.2 11.5 %copy-start.25 = (bf16[64]{0:T(256)(128)(2,1)S(1)}, bf16[64]{0:T(256)(128)(2,1)}, u32[]{:S(2)}) copy-start(bf16[64]{0:T(256)(128)(2,1)} %param.27) | copy-start | bytes 388
  7.3 11.5 %copy-start.26 = (bf16[64]{0:T(256)(128)(2,1)S(1)}, bf16[64]{0:T(256)(128)(2,1)}, u32[]{:S(2)}) copy-start(bf16[64]{0:T(256)(128)(2,1)} %param.29) | copy-start | bytes 388
  7.3 11.5 %copy-start.27 = (bf16[64]{0:T(256)(128)(2,1)S(1)}, bf16[64]{0:T(256)(128)(2,1)}, u32[]{:S(2)}) copy-start(bf16[64]{0:T(256)(128)(2,1)} %param.30) | copy-start | bytes 388
  7.3 11.5 %copy-start.28 = (bf16[64]{0:T(256)(128)(2,1)S(1)}, bf16[64]{0:T(256)(128)(2,1)}, u32[]{:S(2)}) copy-start(bf16[64]{0:T(256)(128)(2,1)} %param.31) | copy-start | bytes 388
  7.3 11.5 %copy-start.30 = (bf16[256]{0:T(256)(128)(2,1)S(1)}, bf16[256]{0:T(256)(128)(2,1)}, u32[]{:S(2)}) copy-start(bf16[256]{0:T(256)(128)(2,1)} %param.33) | copy-start | bytes 1540
  7.3 11.5 %copy-start.29 = (bf16[64]{0:T(256)(128)(2,1)S(1)}, bf16[64]{0:T(256)(128)(2,1)}, u32[]{:S(2)}) copy-start(bf16[64]{0:T(256)(128)(2,1)} %param.35) | copy-start | bytes 388
  7.3 109.8 %all-gather.9.cloned.1.call-start = ((), (), s32[]{:S(2)}) async-start(), calls=%async_computation.10 | async-start | bytes 1310720 | tf_op jit(solution)/shard_map/all_gather | solution.py:878
  8.0 132.5 %all-gather.5.cloned.1.call-start = ((), (), s32[]{:S(2)}) async-start(), calls=%async_computation.8 | async-start | bytes 3932160 | tf_op jit(solution)/shard_map/all_gather | solution.py:878
  14.2 54.1 %copy-start.31 = (f32[3]{0:T(128)S(1)}, f32[3]{0:T(128)}, u32[]{:S(2)}) copy-start(f32[3]{0:T(128)} %constant.100) | copy-start | bytes 40
  61.6 222.3 %all-gather.11.cloned.1.call-start = ((), (), s32[]{:S(2)}) async-start(), calls=%async_computation.11 | async-start | bytes 5242880 | tf_op jit(solution)/shard_map/all_gather | solution.py:878
  62.4 240.7 %all-gather.7.cloned.1.call-start = ((), (), s32[]{:S(2)}) async-start(), calls=%async_computation.9 | async-start | bytes 5242880 | tf_op jit(solution)/shard_map/all_gather | solution.py:878
  63.0 54.1 %all-to-all-start = ((bf16[4,64,2048]{2,1,0:T(8,128)(2,1)}), bf16[4,64,2048]{2,1,0:T(8,128)(2,1)S(1)}, u32[]{:S(2)}, u32[]{:S(2)}) async-start(bf16[4,64,2048]{2,1,0:T(8,128)(2,1)} %param.36), calls=%async_computation | async-start | bytes 2097152 | tf_op jit(solution)/shard_map/all_to_all | solution.py:862
  69.3 81.3 %copy-start.17 = (s32[4]{0:T(128)}, s32[4]{0:T(128)S(1)}, u32[]{:S(2)}) copy-start(s32[4]{0:T(128)S(1)} %reshape.232.bounds) | copy-start | bytes 52
  69.6 1.3 copy-start.1
  113.8 3.3 copy-start.6
  117.1 78.0 %all-to-all-start.1 = ((bf16[4,1,64,2048]{3,2,1,0:T(8,128)(2,1)}), bf16[4,1,64,2048]{3,2,1,0:T(8,128)(2,1)}, u32[]{:S(2)}, u32[]{:S(2)}) async-start(bf16[4,1,64,2048]{3,2,1,0:T(8,128)(2,1)} %bitcast.103), calls=%async_computation.1 | async-start | bytes 2097152 | tf_op jit(solution)/shard_map/all_to_all | solution.py:882
  140.5 54.6 %copy-start.2 = (bf16[4,64,2048]{2,1,0:T(8,128)(2,1)S(1)}, bf16[4,64,2048]{2,1,0:T(8,128)(2,1)}, u32[]{:S(2)}) copy-start(bf16[4,64,2048]{2,1,0:T(8,128)(2,1)} %get-tuple-element.39) | copy-start | bytes 3145732
  191.4 1.7 copy-start.7
  193.1 1.3 copy-start.9
  194.4 0.7 copy-start.16
  279.3 1.3 copy-start.4
  280.6 3.3 copy-start.18
  303.1 21.6 %copy-start.5 = (f32[256,2048]{1,0:T(8,128)S(1)}, f32[256,2048]{1,0:T(8,128)}, u32[]{:S(2)}) copy-start(f32[256,2048]{1,0:T(8,128)} %copy-done.4) | copy-start | bytes 6291460
  416.4 7.5 copy-start.10
  423.9 18.0 %all-to-all-start.3 = ((bf16[4,1,64,2048]{3,2,1,0:T(8,128)(2,1)}), bf16[4,1,64,2048]{3,2,1,0:T(8,128)(2,1)S(1)}, u32[]{:S(2)}, u32[]{:S(2)}) async-start(bf16[4,1,64,2048]{3,2,1,0:T(8,128)(2,1)} %bitcast.22), calls=%async_computation.5 | async-start | bytes 2097152 | tf_op jit(solution)/shard_map/all_to_all | solution.py:979
  427.4 230.5 %reduce-scatter.9.cloned.1.call-start = ((), (), s32[]{:S(2)}) async-start(), calls=%async_computation.14 | async-start | bytes 1310720 | tf_op jit(solution)/shard_map/reduce_scatter | solution.py:980
  441.9 1.0 copy-start.19
  442.9 216.9 %reduce-scatter.5.cloned.1.call-start = ((), (), s32[]{:S(2)}) async-start(), calls=%async_computation.12 | async-start | bytes 3932160 | tf_op jit(solution)/shard_map/reduce_scatter | solution.py:990
  513.1 182.2 %reduce-scatter.7.cloned.1.call-start = ((), (), s32[]{:S(2)}) async-start(), calls=%async_computation.13 | async-start | bytes 5242880 | tf_op jit(solution)/shard_map/reduce_scatter | solution.py:970
  527.3 246.4 %reduce-scatter.11.cloned.1.call-start = ((), (), s32[]{:S(2)}) async-start(), calls=%async_computation.15 | async-start | bytes 5242880 | tf_op jit(solution)/shard_map/reduce_scatter | solution.py:965
  541.5 7.6 copy-start
  541.5 116.4 %all-to-all-start.2 = ((bf16[4,64,2048]{2,1,0:T(8,128)(2,1)}), bf16[4,64,2048]{2,1,0:T(8,128)(2,1)}, u32[]{:S(2)}, u32[]{:S(2)}) async-start(bf16[4,64,2048]{2,1,0:T(8,128)(2,1)} %bitcast.105), calls=%async_computation.2 | async-start | bytes 2097152 | tf_op jit(solution)/shard_map/all_to_all | solution.py:862
  549.1 1.2 copy-start.3
  550.3 1.9 copy-start.8
  552.2 1.6 copy-start.11
  654.8 1.0 copy-start.12
  695.3 1.2 copy-start.14
  696.5 1.1 copy-start.15
  731.1 47.8 %copy-start.13 = (bf16[4,64,2048]{2,1,0:T(8,128)(2,1)S(1)}, bf16[4,64,2048]{2,1,0:T(8,128)(2,1)}, u32[]{:S(2)}) copy-start(bf16[4,64,2048]{2,1,0:T(8,128)(2,1)} %copy-done.12) | copy-start | bytes 3145732
Sparse Core Ops, SparseCore 0:
  9.7 45.0 all-gather.8
  61.8 78.6 all-gather.4
  142.1 80.2 all-gather.10
  223.8 79.2 all-gather.6
  443.0 25.0 reduce-scatter.8
  513.2 80.8 reduce-scatter.4
  596.5 98.7 reduce-scatter.6
  697.6 76.1 reduce-scatter.10

commit v4 on v3

--- a/solution.py
+++ b/solution.py
@@ -20,7 +20,7 @@
 VMEM = pl.BlockSpec(memory_space=pltpu.VMEM)
 MIB = 2**20
 CHUNK = 16
-TILE = 512
+TILE = 2048
 
 
 def gelu_tanh(values):
@@ -83,46 +83,82 @@
     return (s, b, u), (beside, across, twin), blocks(c), blocks(1 - c)
 
 
+class Spread:
+    def __init__(self, own, out, send, recv, local):
+        _, self.near_by, self.blocks, self.twins = place()
+        beside, across, twin = self.near_by
+        me = self.blocks[3]
+        half = own.shape[0] // 2
+        self.out, self.parts = out, (pl.ds(0, half), pl.ds(half, half))
+        self.copy = copy = sender(send, recv)
+        p0, p1 = self.parts
+        self.x0 = copy(0, own.at[p0], out.at[me, p0], beside)
+        self.y1 = copy(1, own.at[p1], out.at[me, p1], across)
+        self.x1 = copy(2, own.at[p1], out.at[me, p1], beside)
+        self.y0 = copy(3, own.at[p0], out.at[me, p0], across)
+        self.own_twin = copy(4, own, out.at[me], twin)
+        self.started = [self.x0, self.y1, self.x1, self.y0, self.own_twin]
+        self.kept = pltpu.make_async_copy(own, out.at[me], local)
+        self.kept.start()
+
+    def pass_on(self, i, block, part, device):
+        at = self.out.at[block, self.parts[part]]
+        made = self.copy(i, at, at, device)
+        self.started.append(made)
+        return made
+
+    def own_blocks(self):
+        self.kept.wait()
+        self.own_twin.wait_recv()
+
+    def first_halves(self):
+        beside, across, twin = self.near_by
+        _, on_x, on_y, _ = self.blocks
+        self.x0.wait_recv()
+        self.d0 = self.pass_on(5, on_x, 0, across)
+        self.t0 = self.pass_on(6, on_x, 0, twin)
+        self.y1.wait_recv()
+        self.d1 = self.pass_on(7, on_y, 1, beside)
+        self.t1 = self.pass_on(8, on_y, 1, twin)
+
+    def second_halves(self):
+        _, _, twin = self.near_by
+        _, on_x, on_y, _ = self.blocks
+        self.x1.wait_recv()
+        self.t2 = self.pass_on(9, on_x, 1, twin)
+        self.y0.wait_recv()
+        self.t3 = self.pass_on(10, on_y, 0, twin)
+
+    def twin_sides(self):
+        for made in (self.t0, self.t1, self.t2, self.t3):
+            made.wait_recv()
+
+    def diagonals(self):
+        _, _, twin = self.near_by
+        diag = self.blocks[0]
+        self.d0.wait_recv()
+        t4 = self.pass_on(11, diag, 0, twin)
+        self.d1.wait_recv()
+        t5 = self.pass_on(12, diag, 1, twin)
+        t4.wait_recv()
+        t5.wait_recv()
+
+    def close(self):
+        for made in self.started:
+            made.wait_send()
+
+
 def spread(own, out, send, recv, local):
-    _, (beside, across, twin), (diag, on_x, on_y, me), _ = place()
-    half = own.shape[0] // 2
-    parts = (pl.ds(0, half), pl.ds(half, half))
-    copy = sender(send, recv)
-    x0 = copy(0, own.at[parts[0]], out.at[me, parts[0]], beside)
-    y1 = copy(1, own.at[parts[1]], out.at[me, parts[1]], across)
-    x1 = copy(2, own.at[parts[1]], out.at[me, parts[1]], beside)
-    y0 = copy(3, own.at[parts[0]], out.at[me, parts[0]], across)
-    started = [x0, y1, x1, y0, copy(4, own, out.at[me], twin)]
-    kept = pltpu.make_async_copy(own, out.at[me], local)
-    kept.start()
-
-    def pass_on(i, block, part, device):
-        made = copy(i, out.at[block, parts[part]], out.at[block, parts[part]], device)
-        started.append(made)
-        return made
-
+    moving = Spread(own, out, send, recv, local)
     yield
-    x0.wait_recv()
-    d0 = pass_on(5, on_x, 0, across)
-    pass_on(6, on_x, 0, twin)
-    y1.wait_recv()
-    d1 = pass_on(7, on_y, 1, beside)
-    pass_on(8, on_y, 1, twin)
+    moving.first_halves()
     yield
-    x1.wait_recv()
-    pass_on(9, on_x, 1, twin)
-    y0.wait_recv()
-    pass_on(10, on_y, 0, twin)
+    moving.second_halves()
     yield
-    d0.wait_recv()
-    pass_on(11, diag, 0, twin)
-    d1.wait_recv()
-    pass_on(12, diag, 1, twin)
-    for i in (4, 6, 8, 9, 10, 11, 12):
-        started[i].wait_recv()
-    for made in started:
-        made.wait_send()
-    kept.wait()
+    moving.own_blocks()
+    moving.twin_sides()
+    moving.diagonals()
+    moving.close()
 
 
 def run(steps):
@@ -133,7 +169,9 @@
 SPREAD = 13
 
 
-def collect(multiply, total, to_twin, from_twin, mine, in_x, in_y, send, recv):
+def collect(
+    multiply, total, to_twin, from_twin, mine, in_x, in_y, send, recv, prepare=lambda block: None
+):
     _, (beside, across, twin), here, other = place()
     rows, width = total.shape
     half = rows // 2
@@ -154,10 +192,12 @@
         def term(cols):
             to_twin[k, :, cols] = multiply(other[k], cols).astype(BF)
 
+        prepare(other[k])
         each_tile(term)
         to_twins.append(copy(k, to_twin.at[k], from_twin.at[k], twin))
 
     def for_here(k):
+        prepare(here[k])
         to_twins[k].wait_recv()
 
         def term(cols):
@@ -285,9 +325,7 @@
     rows = pl.ds(pl.multiple_of(b * count, count), count)
     kept = pltpu.make_async_copy(block.at[rows], out.at[b], local)
     kept.start()
-    for made in started:
-        made.wait()
-    kept.wait()
+    return started + [kept]
 
 
 def blk_peers(n_blk):
@@ -295,100 +333,167 @@
     return [(s, (b + j) % n_blk, u) for j in range(1, n_blk)]
 
 
+def exchange_columns(copy, first, whole, cut, p, me, device, sizes, gather):
+    n_seq, _, n_uly, runs = sizes
+    plane = n_seq * n_uly
+    owner = p if gather else me
+    share = whole[0].shape[1] // plane
+    run_share = whole[3].shape[1] // (plane * runs)
+    spans = []
+    for i in range(3):
+        at = pl.ds(pl.multiple_of(owner * share, share), share)
+        spans.append((whole[i], at, cut[0], pl.ds(i * share, share)))
+    for r in range(runs):
+        at = ((owner // n_uly) * runs + r) * n_uly + owner % n_uly
+        at = pl.ds(pl.multiple_of(at * run_share, run_share), run_share)
+        spans.append((whole[3], at, cut[1], pl.ds(r * run_share, run_share)))
+    started = []
+    for i, (matrix, at, part, inside) in enumerate(spans):
+        if gather:
+            source, target = matrix.at[:, at], part.at[me, :, inside]
+        else:
+            source, target = part.at[p, :, inside], matrix.at[:, at]
+        started.append(copy(first + i, source, target, device))
+    return started
+
+
 def entry_kernel(
-    n_blk, x_ref, qkv_ref, fc_ref, small_ref, tok, qkv, fc, small,
-    blk_send, blk_recv, plane_send, plane_recv, local,
+    sizes, x_ref, wq_ref, wk_ref, wv_ref, fc_ref, *refs
 ):
+    vectors, (bias_ref, lengths_ref), refs = refs[:8], refs[8:10], refs[10:]
+    enter_body(sizes, x_ref, wq_ref, wk_ref, wv_ref, fc_ref, vectors, bias_ref, lengths_ref, *refs)
+
+
+def enter_body(
+    sizes, x_ref, wq_ref, wk_ref, wv_ref, fc_ref, short, bias_ref, lengths_ref, tok, qkv, fc, small,
+    small_ref, blk_send, blk_recv, plane_send, plane_recv, local,
+):
+    n_seq, n_blk, n_uly, runs = sizes
     (s, b, u), _, (_, _, _, me), _ = place()
-    plane = qkv_ref.shape[0]
-    n_uly = plane // 2
+    plane = n_seq * n_uly
+    pieces = 3 + runs
+    small_ref[...] = jnp.zeros_like(small_ref)
+    for i, ref in enumerate(short):
+        small_ref[i : i + 1, : ref.shape[1]] = ref[...].astype(F32)
+    lanes = min(128, bias_ref.shape[1])
+    for i in range(bias_ref.shape[1] // lanes):
+        part = bias_ref[:, i * lanes : (i + 1) * lanes].astype(F32)
+        small_ref[8 + i : 9 + i, :lanes] = part
+    small_ref[SMALL - 1 :, : lengths_ref.shape[1]] = lengths_ref[...].astype(F32)
     others = [(me + j) % plane for j in range(1, plane)]
     friends = [(p // n_uly, b, p % n_uly) for p in others]
     column = blk_peers(n_blk)
     meet(friends + column)
     by_blk = sender(blk_send, blk_recv)
     by_plane = sender(plane_send, plane_recv)
-    kept = [
-        pltpu.make_async_copy(small_ref, small.at[me, b], local.at[0]),
-        pltpu.make_async_copy(x_ref.at[b], tok.at[b], local.at[1]),
-        pltpu.make_async_copy(qkv_ref.at[me], qkv.at[me], local.at[2]),
-        pltpu.make_async_copy(fc_ref.at[me], fc.at[me], local.at[3]),
-    ]
-    for made in kept:
+
+    def at_home(i, source, target, _):
+        made = pltpu.make_async_copy(source, target, local.at[i])
         made.start()
+        return made
+
+    sources, targets = (wq_ref, wk_ref, wv_ref, fc_ref), (qkv, fc)
+    first = at_home(0, small_ref, small.at[me, b], None)
     vectors, started = [], []
     for j, peer in enumerate(column):
         vectors.append(by_blk(j, small_ref, small.at[me, b], peer))
     for j, peer in enumerate(column):
         started.append(by_blk(n_blk - 1 + j, x_ref.at[peer[1]], tok.at[b], peer))
     for j, (p, peer) in enumerate(zip(others, friends)):
-        started.append(by_plane(3 * j, qkv_ref.at[p], qkv.at[me], peer))
-        started.append(by_plane(3 * j + 1, fc_ref.at[p], fc.at[me], peer))
-    kept[0].wait()
+        started += exchange_columns(
+            by_plane, pieces * j, sources, targets, p, me, peer, sizes, True
+        )
+    started.append(at_home(1, x_ref.at[b], tok.at[b], None))
+    started += exchange_columns(at_home, 2, sources, targets, me, me, None, sizes, True)
+    first.wait()
     for made in vectors:
         made.wait()
     for j, peer in enumerate(friends):
-        started.append(by_plane(3 * j + 2, small.at[me], small.at[me], peer))
-    for made in kept[1:] + started:
+        at = small.at[me]
+        started.append(by_plane(pieces * (plane - 1) + j, at, at, peer))
+    for made in started:
         made.wait()
 
 
-def enter(x, qkv, fc, small, n_blk):
-    plane = qkv.shape[0]
+SMALL = 16
+
+
+def enter(x, weights, fc, short, sizes):
+    n_seq, n_blk, n_uly, runs = sizes
+    plane = n_seq * n_uly
+    rows, width = weights[0].shape
+    pieces = (4 + runs) * (plane - 1)
     return pl.pallas_call(
-        functools.partial(entry_kernel, n_blk),
+        functools.partial(entry_kernel, sizes),
         name="enter",
         out_shape=(
             jax.ShapeDtypeStruct(x.shape, x.dtype),
-            jax.ShapeDtypeStruct(qkv.shape, qkv.dtype),
-            jax.ShapeDtypeStruct(fc.shape, fc.dtype),
-            jax.ShapeDtypeStruct((plane, n_blk) + small.shape, small.dtype),
-        ),
-        in_specs=[ANY] * 4,
+            jax.ShapeDtypeStruct((plane, rows, 3 * width // plane), BF),
+            jax.ShapeDtypeStruct((plane, rows, fc.shape[1] // plane), BF),
+            jax.ShapeDtypeStruct((plane, n_blk, SMALL, 128), F32),
+        ),
+        in_specs=[ANY] * 5 + [VMEM] * len(short),
         out_specs=(ANY,) * 4,
         scratch_shapes=[
+            pltpu.VMEM((SMALL, 128), F32),
             pltpu.SemaphoreType.DMA((2 * (n_blk - 1),)),
             pltpu.SemaphoreType.DMA((2 * (n_blk - 1),)),
-            pltpu.SemaphoreType.DMA((3 * (plane - 1),)),
-            pltpu.SemaphoreType.DMA((3 * (plane - 1),)),
-            pltpu.SemaphoreType.DMA((4,)),
+            pltpu.SemaphoreType.DMA((pieces,)),
+            pltpu.SemaphoreType.DMA((pieces,)),
+            pltpu.SemaphoreType.DMA((5 + runs,)),
         ],
         compiler_params=pltpu.CompilerParams(collective_id=0, has_side_effects=True),
-        cost_estimate=pl.CostEstimate(flops=0, bytes_accessed=60 * MIB, transcendentals=0),
-    )(x, qkv, fc, small)
-
-
-def norm_kernel(order, tok, gain, shift, out, own, send, recv, local):
-    _, near, _, _ = place()
+        cost_estimate=pl.CostEstimate(flops=0, bytes_accessed=MIB, transcendentals=0),
+    )(x, *weights, fc, *short)
+
+
+def norm_kernel(
+    order, n_blk, tok, gain, shift, cot_ref, out, cot, own, send, recv, local, g_send, g_recv, kept
+):
+    (s, b, u), near, _, _ = place()
+    column = blk_peers(n_blk)
+    meet(list(near) + column)
+    copy = sender(g_send, g_recv)
+    count = cot_ref.shape[1]
+    rows = pl.ds(pl.multiple_of(b * count, count), count)
+    started = [copy(j, cot_ref.at[peer[1]], cot.at[rows], peer) for j, peer in enumerate(column)]
+    started.append(pltpu.make_async_copy(cot_ref.at[b], cot.at[rows], kept))
+    started[-1].start()
 
     def chunk(at):
         unit, _ = norm_parts(tok[at].astype(F32))
         own[at] = reorder(unit * gain[...] + shift[...], *order).astype(BF)
 
     each_chunk(own.shape[0], chunk)
-    meet(near)
     run(spread(own, out, send, recv, local))
-
-
-def norm_gather(tok, gain, shift, plane, order):
+    for made in started:
+        made.wait()
+
+
+def norm_gather(tok, gain, shift, cot, plane, order):
     rows, width = tok.shape
+    n_blk = cot.shape[0]
     return pl.pallas_call(
-        functools.partial(norm_kernel, order),
+        functools.partial(norm_kernel, order, n_blk),
         name="norm_gather",
-        out_shape=jax.ShapeDtypeStruct((plane, rows, width), BF),
-        in_specs=[VMEM] * 3,
-        out_specs=ANY,
-        scratch_shapes=[
-            pltpu.VMEM((rows, width), BF),
-            pltpu.SemaphoreType.DMA((SPREAD,)),
-            pltpu.SemaphoreType.DMA((SPREAD,)),
+        out_shape=(
+            jax.ShapeDtypeStruct((plane, rows, width), BF),
+            jax.ShapeDtypeStruct((rows, width), BF),
+        ),
+        in_specs=[VMEM] * 3 + [ANY],
+        out_specs=(ANY, ANY),
+        scratch_shapes=[pltpu.VMEM((rows, width), BF)]
+        + spread_scratch()
+        + [
+            pltpu.SemaphoreType.DMA((n_blk - 1,)),
+            pltpu.SemaphoreType.DMA((n_blk - 1,)),
             pltpu.SemaphoreType.DMA,
         ],
         compiler_params=pltpu.CompilerParams(
             collective_id=1, has_side_effects=True, vmem_limit_bytes=16 * MIB
         ),
-        cost_estimate=pl.CostEstimate(flops=0, bytes_accessed=100 * MIB, transcendentals=0),
-    )(tok, gain, shift)
+        cost_estimate=pl.CostEstimate(flops=0, bytes_accessed=MIB, transcendentals=0),
+    )(tok, gain, shift, cot)
 
 
 BLOCK = 256
@@ -479,20 +584,26 @@
         compiler_params=pltpu.CompilerParams(
             collective_id=2, has_side_effects=True, vmem_limit_bytes=40 * MIB
         ),
-        cost_estimate=pl.CostEstimate(flops=0, bytes_accessed=150 * MIB, transcendentals=0),
+        cost_estimate=pl.CostEstimate(flops=0, bytes_accessed=MIB, transcendentals=0),
     )(bounds, qkv, cot)
 
 
 def attend_back_kernel(
-    layout, scale, bounds, grad, natural, attended, logs, act, weight, hid, bias, back, out,
-    grads, grads_back, key_grad, value_grad,
-    total, to_twin, from_twin, mine, in_x, in_y, c_send, c_recv,
+    layout, scale, bounds, grad, natural, attended, logs, act, weight, hid, bias, mixed,
+    back, out, mixed_out, grads, grads_back, key_grad, value_grad,
+    total, to_twin, from_twin, mine, in_x, in_y, c_send, c_recv, u_send, u_recv, local,
 ):
-    _, near, _, _ = place()
+    (s, b, u), near, _, _ = place()
     rows = total.shape[0]
     _, _, _, part, heads = layout
     share = heads * HD
-    meet(near)
+    n_uly = mixed.shape[0]
+    in_row = [(s, b, (u + j) % n_uly) for j in range(1, n_uly)]
+    meet([near[1]] + in_row)
+    copy = sender(u_send, u_recv)
+    mixing = [copy(j, mixed.at[to[2]], mixed_out.at[u], to) for j, to in enumerate(in_row)]
+    mixing.append(pltpu.make_async_copy(mixed.at[u], mixed_out.at[u], local))
+    mixing[-1].start()
 
     def multiply(block, cols):
         return product(rows_of(act, block, rows), weight[:, cols])
@@ -551,9 +662,13 @@
         out[at] = (total[at] + hid[at] + bias[...]).astype(BF)
 
     each_chunk(rows, chunk)
-
-
-def attend_back(bounds, grad, natural, attended, logs, act, weight, hid, bias, layout, scale):
+    for made in mixing:
+        made.wait()
+
+
+def attend_back(
+    bounds, grad, natural, attended, logs, act, weight, hid, bias, mixed, layout, scale
+):
     rows, width = hid.shape
     pairs, length = natural.shape[1:3]
     return pl.pallas_call(
@@ -562,21 +677,27 @@
         out_shape=(
             jax.ShapeDtypeStruct((grad.shape[0], 3 * grad.shape[1]), BF),
             jax.ShapeDtypeStruct((rows, width), BF),
-        ),
-        in_specs=[pl.BlockSpec(memory_space=pltpu.SMEM)] + [VMEM] * 8,
-        out_specs=(VMEM, VMEM),
+            jax.ShapeDtypeStruct(mixed.shape, BF),
+        ),
+        in_specs=[pl.BlockSpec(memory_space=pltpu.SMEM)] + [VMEM] * 8 + [ANY],
+        out_specs=(VMEM, VMEM, ANY),
         scratch_shapes=[
             pltpu.VMEM((pairs, length, HD), BF),
             pltpu.VMEM((3 * pairs, length, HD), BF),
             pltpu.VMEM((length, HD), F32),
             pltpu.VMEM((length, HD), F32),
         ]
-        + collect_scratch(rows, width),
+        + collect_scratch(rows, width)
+        + [
+            pltpu.SemaphoreType.DMA((mixed.shape[0] - 1,)),
+            pltpu.SemaphoreType.DMA((mixed.shape[0] - 1,)),
+            pltpu.SemaphoreType.DMA,
+        ],
         compiler_params=pltpu.CompilerParams(
             collective_id=5, has_side_effects=True, vmem_limit_bytes=60 * MIB
         ),
-        cost_estimate=pl.CostEstimate(flops=0, bytes_accessed=200 * MIB, transcendentals=0),
-    )(bounds, grad, natural, attended, logs, act, weight, hid, bias)
+        cost_estimate=pl.CostEstimate(flops=0, bytes_accessed=MIB, transcendentals=0),
+    )(bounds, grad, natural, attended, logs, act, weight, hid, bias, mixed)
 
 
 def rows_of(ref, block, rows):
@@ -584,8 +705,8 @@
 
 
 def hidden_kernel(
-    order, act, weight, tok, bias, gain, shift, hidden, out,
-    total, to_twin, from_twin, mine, in_x, in_y, c_send, c_recv, own, send, recv, local,
+    order, act, weight, tok, bias, gain, shift, hidden, own,
+    total, to_twin, from_twin, mine, in_x, in_y, c_send, c_recv,
 ):
     _, near, _, _ = place()
     rows = total.shape[0]
@@ -603,47 +724,215 @@
         own[at] = reorder(unit * gain[...] + shift[...], *order).astype(BF)
 
     each_chunk(rows, chunk)
-    run(spread(own, out, send, recv, local))
-
-
-def hidden_gather(act, weight, tok, bias, gain, shift, plane, order):
+
+
+def hidden_norm(act, weight, tok, bias, gain, shift, order):
     rows, width = tok.shape
     return pl.pallas_call(
         functools.partial(hidden_kernel, order),
-        name="hidden_gather",
+        name="hidden_norm",
         out_shape=(
             jax.ShapeDtypeStruct((rows, width), F32),
-            jax.ShapeDtypeStruct((plane, rows, width), BF),
+            jax.ShapeDtypeStruct((rows, width), BF),
         ),
         in_specs=[VMEM] * 6,
-        out_specs=(VMEM, ANY),
-        scratch_shapes=collect_scratch(rows, width)
-        + [
-            pltpu.VMEM((rows, width), BF),
-            pltpu.SemaphoreType.DMA((SPREAD,)),
-            pltpu.SemaphoreType.DMA((SPREAD,)),
-            pltpu.SemaphoreType.DMA,
-        ],
+        out_specs=(VMEM, VMEM),
+        scratch_shapes=collect_scratch(rows, width),
         compiler_params=pltpu.CompilerParams(
             collective_id=3, has_side_effects=True, vmem_limit_bytes=40 * MIB
         ),
-        cost_estimate=pl.CostEstimate(flops=0, bytes_accessed=250 * MIB, transcendentals=0),
+        cost_estimate=pl.CostEstimate(flops=0, bytes_accessed=MIB, transcendentals=0),
     )(act, weight, tok, bias, gain, shift)
 
 
-def branch_kernel(
-    order, act, weight, hid, cot, gain, grad_hidden, sums, out,
-    total, to_twin, from_twin, mine, in_x, in_y, c_send, c_recv, own, send, recv, local,
+def spread_scratch():
+    return [
+        pltpu.SemaphoreType.DMA((SPREAD,)),
+        pltpu.SemaphoreType.DMA((SPREAD,)),
+        pltpu.SemaphoreType.DMA,
+    ]
+
+
+def block_rows(block, rows):
+    return pl.ds(pl.multiple_of(block * rows, rows), rows)
+
+
+def fetch(sources, targets, sems):
+    made = [
+        pltpu.make_async_copy(source, target, sems.at[i])
+        for i, (source, target) in enumerate(zip(sources, targets))
+    ]
+    for copy in made:
+        copy.start()
+    return made
+
+
+def pairs_of(moving):
+    diag, on_x, on_y, me = moving.blocks
+    twin_diag, twin_x, twin_y, twin = moving.twins
+    moving.own_blocks()
+    yield me, twin
+    moving.first_halves()
+    moving.second_halves()
+    yield on_x, on_y
+    moving.twin_sides()
+    yield twin_x, twin_y
+    moving.diagonals()
+    yield diag, twin_diag
+    moving.close()
+
+
+FF_TILE = 1024
+FC_TILE = 256
+
+
+def feed_kernel(
+    own, weight_ref, bias, cots, out, active, slope, grad,
+    weight, rows_in, cots_in, low_out, steep_out, acc, w_sem, sems, out_sems, send, recv, local,
 ):
     _, near, _, _ = place()
-    rows = total.shape[0]
+    rows, width = own.shape
+    ff = weight.shape[1]
+    loading = pltpu.make_async_copy(weight_ref, weight, w_sem)
+    loading.start()
+    halves = (pl.ds(0, rows), pl.ds(rows, rows))
     meet(near)
+    moving = Spread(own, out, send, recv, local)
+    diag, on_x, on_y, me = moving.blocks
+    twin_diag, twin_x, twin_y, twin = moving.twins
+    plan = [(me, twin), (on_x, on_y), (twin_x, twin_y), (diag, twin_diag)]
+
+    def cots_of(i):
+        return fetch(
+            [cots.at[p] for p in plan[i]], [cots_in.at[i % 2, h] for h in halves], sems.at[i % 2]
+        )
+
+    arriving = cots_of(0)
+    leaving = {}
+    for i, (left, right) in enumerate(pairs_of(moving)):
+        fetched = fetch([out.at[left], out.at[right]], [rows_in.at[h] for h in halves], sems.at[2])
+        for made in fetched + arriving:
+            made.wait()
+        if i == 0:
+            loading.wait()
+        if i < 3:
+            arriving = cots_of(i + 1)
+        for made in leaving.pop(i - 2, []):
+            made.wait()
+
+        def tile(t, carry, i=i):
+            at = pl.ds(pl.multiple_of(t * FF_TILE, FF_TILE), FF_TILE)
+            inner = product(rows_in[...], weight[:, at]) + bias[:, at]
+            bent = math.sqrt(2 / math.pi) * (inner + 0.044715 * (inner * inner * inner))
+            curve = jnp.tanh(bent)
+            low = (0.5 * inner * (1.0 + curve)).astype(BF)
+            steep = math.sqrt(2 / math.pi) * (1.0 + 3 * 0.044715 * (inner * inner))
+            steep = 0.5 * (1.0 + curve) + 0.5 * inner * (1.0 - curve * curve) * steep
+            low_out[i % 2, :, at] = low
+            steep_out[i % 2, :, at] = steep.astype(BF)
+            for cut in range(0, width, 1024):
+                cols = pl.ds(cut, 1024)
+                term = transposed(low, cots_in[i % 2, :, cols])
+                if i == 0:
+                    acc[at, cols] = term
+                elif i < 3:
+                    acc[at, cols] += term
+                else:
+                    grad[at, cols] = (acc[at, cols] + term).astype(BF)
+            return carry
+
+        lax.fori_loop(0, ff // FF_TILE, tile, 0)
+        places = [block_rows(left, rows), block_rows(right, rows)]
+        leaving[i] = fetch(
+            [held.at[i % 2, h] for held in (low_out, steep_out) for h in halves],
+            [kept.at[p] for kept in (active, slope) for p in places],
+            out_sems.at[i % 2],
+        )
+    for group in leaving.values():
+        for made in group:
+            made.wait()
+
+
+def feed(own, weight, bias, cots):
+    rows, width = own.shape
+    plane, ff = cots.shape[0], weight.shape[1]
+    return pl.pallas_call(
+        feed_kernel,
+        name="feed",
+        out_shape=(
+            jax.ShapeDtypeStruct((plane, rows, width), BF),
+            jax.ShapeDtypeStruct((plane * rows, ff), BF),
+            jax.ShapeDtypeStruct((plane * rows, ff), BF),
+            jax.ShapeDtypeStruct((ff, width), BF),
+        ),
+        in_specs=[VMEM, ANY, VMEM, ANY],
+        out_specs=(ANY, ANY, ANY, VMEM),
+        scratch_shapes=[
+            pltpu.VMEM(weight.shape, BF),
+            pltpu.VMEM((2 * rows, width), BF),
+            pltpu.VMEM((2, 2 * rows, width), BF),
+            pltpu.VMEM((2, 2 * rows, ff), BF),
+            pltpu.VMEM((2, 2 * rows, ff), BF),
+            pltpu.VMEM((ff, width), F32),
+            pltpu.SemaphoreType.DMA,
+            pltpu.SemaphoreType.DMA((3, 2)),
+            pltpu.SemaphoreType.DMA((2, 4)),
+        ]
+        + spread_scratch(),
+        compiler_params=pltpu.CompilerParams(
+            collective_id=8, has_side_effects=True, vmem_limit_bytes=56 * MIB
+        ),
+        cost_estimate=pl.CostEstimate(flops=0, bytes_accessed=MIB, transcendentals=0),
+    )(own, weight, bias, cots)
+
+
+def back_feed_kernel(
+    order, cots, slope, proj, weight, hid, cot, gain, inner_grad, grad_hidden, own, sums, bias,
+    cots_in, slope_in, sems,
+    total, to_twin, from_twin, mine, in_x, in_y, c_send, c_recv,
+):
+    _, near, here, other = place()
+    rows, width = total.shape
+    ff = weight.shape[1]
+    plan = [other[0], other[1], here[0], other[2], here[1], other[3], here[2], here[3]]
+
+    def load(i):
+        at = i % 2
+        return fetch(
+            (cots.at[plan[i]], slope.at[block_rows(plan[i], rows)]),
+            (cots_in.at[at], slope_in.at[at]),
+            sems.at[at],
+        )
+
+    loads = [load(0)]
+    sums[...] = jnp.zeros_like(sums)
+    bias[...] = jnp.zeros_like(bias)
+    meet(near)
+
+    def prepare(block):
+        i = len(loads) - 1
+        for made in loads[i]:
+            made.wait()
+        loads.append(load(i + 1) if i + 1 < len(plan) else [])
+
+        def tile(t, carry):
+            at = pl.ds(pl.multiple_of(t * FF_TILE, FF_TILE), FF_TILE)
+            made = against(cots_in[i % 2], proj[at, :]) * slope_in[i % 2, :, at].astype(F32)
+            low = made.astype(BF)
+            inner_grad[block_rows(block, rows), at] = low
+            bias[0:1, at] += row_sum(low.astype(F32))
+            return carry
+
+        lax.fori_loop(0, ff // FF_TILE, tile, 0)
 
     def multiply(block, cols):
-        return against(rows_of(act, block, rows), weight[cols, :])
-
-    run(collect(multiply, total, to_twin, from_twin, mine, in_x, in_y, c_send, c_recv))
-    sums[...] = jnp.zeros_like(sums)
+        return against(rows_of(inner_grad, block, rows), weight[cols, :])
+
+    run(
+        collect(
+            multiply, total, to_twin, from_twin, mine, in_x, in_y, c_send, c_recv, prepare
+        )
+    )
     inner, outer, lanes = order[1], order[0], order[2]
 
     def chunk(at):
@@ -660,42 +949,116 @@
         sums[3:4] += row_sum(passed)
 
     each_chunk(rows, chunk)
-    run(spread(own, out, send, recv, local))
-
-
-def branch_gather(act, weight, hid, cot, gain, plane, order):
+
+
+def back_feed(cots, slope, proj, weight, hid, cot, gain, order):
     rows, width = cot.shape
+    ff = weight.shape[1]
     return pl.pallas_call(
-        functools.partial(branch_kernel, order),
-        name="branch_gather",
+        functools.partial(back_feed_kernel, order),
+        name="back_feed",
         out_shape=(
+            jax.ShapeDtypeStruct((slope.shape[0], ff), BF),
             jax.ShapeDtypeStruct((rows, width), F32),
+            jax.ShapeDtypeStruct((rows, width), BF),
             jax.ShapeDtypeStruct((8, width), F32),
+            jax.ShapeDtypeStruct((8, ff), F32),
+        ),
+        in_specs=[ANY, ANY] + [VMEM] * 5,
+        out_specs=(VMEM,) * 5,
+        scratch_shapes=[
+            pltpu.VMEM((2, rows, width), BF),
+            pltpu.VMEM((2, rows, ff), BF),
+            pltpu.SemaphoreType.DMA((2, 2)),
+        ]
+        + collect_scratch(rows, width),
+        compiler_params=pltpu.CompilerParams(
+            collective_id=4, has_side_effects=True, vmem_limit_bytes=56 * MIB
+        ),
+        cost_estimate=pl.CostEstimate(flops=0, bytes_accessed=MIB, transcendentals=0),
+    )(cots, slope, proj, weight, hid, cot, gain)
+
+
+def branch_kernel(
+    own, weight, low, normed, inner_grad, out, heads_grad, weight_grad, fc_grad,
+    rows_in, acc, sems, send, recv, local,
+):
+    _, near, _, _ = place()
+    rows, width = own.shape
+    meet(near)
+    moving = Spread(own, out, send, recv, local)
+    tiles = width // FC_TILE
+
+    def fc_tile(t, carry):
+        at = pl.ds(pl.multiple_of(t * FC_TILE, FC_TILE), FC_TILE)
+        fc_grad[at, :] = transposed(normed[:, at], inner_grad[...]).astype(BF)
+        return carry
+
+    done = 0
+    for i, (left, right) in enumerate(pairs_of(moving)):
+        fetched = fetch(
+            (out.at[left], out.at[right]),
+            (rows_in.at[pl.ds(0, rows)], rows_in.at[pl.ds(rows, rows)]),
+            sems,
+        )
+        for made in fetched:
+            made.wait()
+        grads = against(rows_in[...], weight[...]).astype(BF)
+        heads_grad[block_rows(left, rows)] = grads[:rows]
+        heads_grad[block_rows(right, rows)] = grads[rows:]
+        kept = jnp.concatenate(
+            [low[block_rows(left, rows), :], low[block_rows(right, rows), :]], axis=0
+        )
+        for cut in range(0, width, 1024):
+            cols = pl.ds(cut, 1024)
+            term = transposed(kept, rows_in[:, cols])
+            if i == 0:
+                acc[:, cols] = term
+            elif i < 3:
+                acc[:, cols] += term
+            else:
+                weight_grad[:, cols] = (acc[:, cols] + term).astype(BF)
+        more = (3 * tiles // 8, 3 * tiles // 4, tiles, tiles)[i]
+        lax.fori_loop(done, more, fc_tile, 0)
+        done = more
+
+
+def branch_spread(own, weight, low, normed, inner_grad, plane):
+    rows, width = own.shape
+    share, ff = weight.shape[0], inner_grad.shape[1]
+    return pl.pallas_call(
+        branch_kernel,
+        name="branch_spread",
+        out_shape=(
             jax.ShapeDtypeStruct((plane, rows, width), BF),
+            jax.ShapeDtypeStruct((plane * rows, share), BF),
+            jax.ShapeDtypeStruct((share, width), BF),
+            jax.ShapeDtypeStruct((width, ff), BF),
         ),
         in_specs=[VMEM] * 5,
-        out_specs=(VMEM, VMEM, ANY),
-        scratch_shapes=collect_scratch(rows, width)
-        + [
-            pltpu.VMEM((rows, width), BF),
-            pltpu.SemaphoreType.DMA((SPREAD,)),
-            pltpu.SemaphoreType.DMA((SPREAD,)),
-            pltpu.SemaphoreType.DMA,
-        ],
+        out_specs=(ANY, VMEM, VMEM, VMEM),
+        scratch_shapes=[
+            pltpu.VMEM((2 * rows, width), BF),
+            pltpu.VMEM((share, width), F32),
+            pltpu.SemaphoreType.DMA((2,)),
+        ]
+        + spread_scratch(),
         compiler_params=pltpu.CompilerParams(
-            collective_id=4, has_side_effects=True, vmem_limit_bytes=48 * MIB
-        ),
-        cost_estimate=pl.CostEstimate(flops=0, bytes_accessed=250 * MIB, transcendentals=0),
-    )(act, weight, hid, cot, gain)
+            collective_id=9, has_side_effects=True, vmem_limit_bytes=56 * MIB
+        ),
+        cost_estimate=pl.CostEstimate(flops=0, bytes_accessed=MIB, transcendentals=0),
+    )(own, weight, low, normed, inner_grad)
 
 
 def inputs_kernel(
-    n_blk, order, act, weight, tok, grad_hidden, gain, sums, out,
-    total, to_twin, from_twin, mine, in_x, in_y, c_send, c_recv, own, send, recv, local,
+    n_blk, order, act, weight, tok, grad_hidden, gain, result, sums, out, result_out,
+    total, to_twin, from_twin, mine, in_x, in_y, c_send, c_recv, own,
+    send, recv, local, r_send, r_recv, r_local,
 ):
     _, near, _, _ = place()
     rows = total.shape[0]
     meet(list(near) + blk_peers(n_blk))
+    leaving = return_rows(result, result_out, n_blk, r_send, r_recv, r_local)
 
     def multiply(block, cols):
         return against(rows_of(act, block, rows), weight[cols, :])
@@ -712,66 +1075,100 @@
         sums[1:2] += row_sum(grad)
 
     each_chunk(rows, chunk)
-    return_rows(own, out, n_blk, send, recv, local)
-
-
-def inputs_return(act, weight, tok, grad_hidden, gain, n_blk, order):
+    leaving += return_rows(own, out, n_blk, send, recv, local)
+    for made in leaving:
+        made.wait()
+
+
+def inputs_return(act, weight, tok, grad_hidden, gain, result, n_blk, order):
     rows, width = tok.shape
+    back = jax.ShapeDtypeStruct((n_blk, rows // n_blk, width), BF)
+    moves = [
+        pltpu.SemaphoreType.DMA((n_blk - 1,)),
+        pltpu.SemaphoreType.DMA((n_blk - 1,)),
+        pltpu.SemaphoreType.DMA,
+    ]
     return pl.pallas_call(
         functools.partial(inputs_kernel, n_blk, order),
         name="inputs_return",
-        out_shape=(
-            jax.ShapeDtypeStruct((8, width), F32),
-            jax.ShapeDtypeStruct((n_blk, rows // n_blk, width), BF),
-        ),
-        in_specs=[VMEM] * 5,
-        out_specs=(VMEM, ANY),
-        scratch_shapes=collect_scratch(rows, width)
-        + [
-            pltpu.VMEM((rows, width), BF),
-            pltpu.SemaphoreType.DMA((n_blk - 1,)),
-            pltpu.SemaphoreType.DMA((n_blk - 1,)),
-            pltpu.SemaphoreType.DMA,
-        ],
+        out_shape=(jax.ShapeDtypeStruct((8, width), F32), back, back),
+        in_specs=[VMEM] * 5 + [ANY],
+        out_specs=(VMEM, ANY, ANY),
+        scratch_shapes=collect_scratch(rows, width) + [pltpu.VMEM((rows, width), BF)] + moves * 2,
         compiler_params=pltpu.CompilerParams(
             collective_id=6, has_side_effects=True, vmem_limit_bytes=40 * MIB
         ),
-        cost_estimate=pl.CostEstimate(flops=0, bytes_accessed=180 * MIB, transcendentals=0),
-    )(act, weight, tok, grad_hidden, gain)
+        cost_estimate=pl.CostEstimate(flops=0, bytes_accessed=MIB, transcendentals=0),
+    )(act, weight, tok, grad_hidden, gain, result)
+
+
+def weight_kernel(left, right, mixed, out):
+    wide = right.shape[1]
+    share = out.shape[1] - wide
+    pieces = left.shape[1] // share
+    rows = mixed.shape[1]
+
+    def tile(t, carry):
+        at = pl.ds(pl.multiple_of(t * FC_TILE, FC_TILE), FC_TILE)
+        out[at, :wide] = transposed(left[:, at], right[...]).astype(BF)
+        return carry
+
+    lax.fori_loop(0, out.shape[0] // FC_TILE, tile, 0)
+    for b in range(mixed.shape[0]):
+        for j in range(pieces):
+            at = (b * pieces + j) * rows
+            out[at : at + rows, wide:] = mixed[b, :, j * share : (j + 1) * share]
+
+
+def weight_grad(left, right, mixed):
+    width = left.shape[1]
+    return pl.pallas_call(
+        weight_kernel,
+        name="weight_grad",
+        out_shape=jax.ShapeDtypeStruct((width, 4 * right.shape[1] // 3), BF),
+        in_specs=[VMEM] * 3,
+        out_specs=VMEM,
+        compiler_params=pltpu.CompilerParams(vmem_limit_bytes=32 * MIB),
+        cost_estimate=pl.CostEstimate(flops=0, bytes_accessed=MIB, transcendentals=0),
+    )(left, right, mixed)
 
 
 def end_kernel(
-    n_blk, qkv_ref, fc_ref, small_ref, qkv, fc, small, gathered, partial, arrived,
-    blk_send, blk_recv, plane_send, plane_recv, local,
+    sizes, qkv_ref, fc_ref, small_ref, gq, gk, gv, fc, small,
+    gathered, partial, arrived, blk_send, blk_recv, plane_send, plane_recv, local,
 ):
+    n_seq, n_blk, n_uly, runs = sizes
     (s, b, u), _, (_, _, _, me), _ = place()
-    plane = qkv_ref.shape[0]
-    n_uly = plane // 2
+    plane = n_seq * n_uly
+    pieces = 3 + runs
     others = [(me + j) % plane for j in range(1, plane)]
     friends = [(p // n_uly, b, p % n_uly) for p in others]
     column = blk_peers(n_blk)
     meet(friends + column)
     by_blk = sender(blk_send, blk_recv)
     by_plane = sender(plane_send, plane_recv)
-    kept = [
-        pltpu.make_async_copy(small_ref.at[me], gathered.at[me], local.at[0]),
-        pltpu.make_async_copy(qkv_ref.at[me], qkv.at[me], local.at[1]),
-        pltpu.make_async_copy(fc_ref.at[me], fc.at[me], local.at[2]),
-    ]
-    for made in kept:
+
+    def at_home(i, source, target, _):
+        made = pltpu.make_async_copy(source, target, local.at[i])
         made.start()
+        return made
+
+    sources, targets = (qkv_ref, fc_ref), (gq, gk, gv, fc)
+    first = at_home(0, small_ref.at[me], gathered.at[me], None)
     vectors, started = [], []
     for j, (p, peer) in enumerate(zip(others, friends)):
-        vectors.append(by_plane(3 * j, small_ref.at[p], gathered.at[me], peer))
+        slot = pieces * (plane - 1) + j
+        vectors.append(by_plane(slot, small_ref.at[p], gathered.at[me], peer))
     for j, (p, peer) in enumerate(zip(others, friends)):
-        started.append(by_plane(3 * j + 1, qkv_ref.at[p], qkv.at[me], peer))
-        started.append(by_plane(3 * j + 2, fc_ref.at[p], fc.at[me], peer))
-    kept[0].wait()
+        started += exchange_columns(
+            by_plane, pieces * j, targets, sources, p, me, peer, sizes, False
+        )
+    started += exchange_columns(at_home, 2, targets, sources, me, me, None, sizes, False)
+    first.wait()
     for made in vectors:
         made.wait()
     partial[...] = jnp.sum(gathered[...], axis=0)
-    own = pltpu.make_async_copy(partial.at[b], arrived.at[b], local.at[3])
-    own.start()
+    own = at_home(1, partial.at[b], arrived.at[b], None)
     sent = [
         by_blk(j, partial.at[peer[1]], arrived.at[b], peer) for j, peer in enumerate(column)
     ]
@@ -779,37 +1176,43 @@
     for made in sent:
         made.wait()
     small[...] = jnp.sum(arrived[...], axis=0)
-    for made in kept[1:] + started:
+    for made in started:
         made.wait()
 
 
-def finish(qkv, fc, small):
-    plane, n_blk = small.shape[:2]
+def finish(qkv, fc, small, sizes):
+    n_seq, n_blk, n_uly, runs = sizes
+    plane = n_seq * n_uly
+    rows, share = qkv.shape[1], qkv.shape[2] // 4
     tail = small.shape[2:]
+    pieces = (4 + runs) * (plane - 1)
+    whole = jax.ShapeDtypeStruct((rows, plane * share), BF)
     return pl.pallas_call(
-        functools.partial(end_kernel, n_blk),
+        functools.partial(end_kernel, sizes),
         name="finish",
         out_shape=(
-            jax.ShapeDtypeStruct(qkv.shape, qkv.dtype),
-            jax.ShapeDtypeStruct(fc.shape, fc.dtype),
+            whole,
+            whole,
+            whole,
+            jax.ShapeDtypeStruct((rows, plane * fc.shape[2]), BF),
             jax.ShapeDtypeStruct(tail, small.dtype),
         ),
-        in_specs=[ANY, ANY, ANY],
-        out_specs=(ANY, ANY, VMEM),
+        in_specs=[ANY] * 3,
+        out_specs=(ANY, ANY, ANY, ANY, VMEM),
         scratch_shapes=[
             pltpu.VMEM((plane, n_blk) + tail, F32),
             pltpu.VMEM((n_blk,) + tail, F32),
             pltpu.VMEM((n_blk,) + tail, F32),
             pltpu.SemaphoreType.DMA((n_blk - 1,)),
             pltpu.SemaphoreType.DMA((n_blk - 1,)),
-            pltpu.SemaphoreType.DMA((3 * (plane - 1),)),
-            pltpu.SemaphoreType.DMA((3 * (plane - 1),)),
-            pltpu.SemaphoreType.DMA((4,)),
+            pltpu.SemaphoreType.DMA((pieces,)),
+            pltpu.SemaphoreType.DMA((pieces,)),
+            pltpu.SemaphoreType.DMA((5 + runs,)),
         ],
         compiler_params=pltpu.CompilerParams(
             collective_id=7, has_side_effects=True, vmem_limit_bytes=16 * MIB
         ),
-        cost_estimate=pl.CostEstimate(flops=0, bytes_accessed=60 * MIB, transcendentals=0),
+        cost_estimate=pl.CostEstimate(flops=0, bytes_accessed=MIB, transcendentals=0),
     )(qkv, fc, small)
 
 
@@ -858,54 +1261,53 @@
         block = block.reshape(n_blk // sharing, sharing, held, part, width)
         return block.transpose(0, 2, 1, 3, 4).reshape(seqs, tok, width)
 
-    def over(block):
-        return lax.all_to_all(block, "blk", split_axis=0, concat_axis=0, tiled=True)
-
     vectors = (ln1_gain, ln1_shift, b_query, b_value, b_out, ln2_gain, ln2_shift, b_proj)
-    small = jnp.concatenate(
-        [v.astype(F32) for v in vectors + (b_fc, doc_lengths.reshape(-1))]
-    )
-    lanes = -(-small.size // 1024) * 8
-    small = jnp.pad(small, (0, lanes * 128 - small.size)).reshape(lanes, 128)
-    qkv = jnp.stack([w.reshape(rows, plane, share) for w in (w_query, w_key, w_value)], axis=2)
-    qkv = qkv.transpose(1, 0, 2, 3).reshape(plane, rows, 3 * share)
-    fc = w_fc.reshape(rows, n_seq, n_blk, n_uly, hidden_rows).transpose(1, 3, 0, 2, 4)
-    fc = fc.reshape(plane, rows, ff_share)
-    tokens, qkv, fc, small = enter(by_plane(inputs), qkv, fc, small, n_blk)
+    vectors += (b_fc, doc_lengths.reshape(-1))
+    runs = n_blk if hidden_rows % 128 == 0 else 1
+    sizes = (n_seq, n_blk, n_uly, runs)
+    by_block = (rows, n_seq, n_blk, n_uly, hidden_rows)
+    by_device = (rows, n_seq, n_uly, n_blk, hidden_rows)
+    if runs == 1:
+        w_fc = w_fc.reshape(by_block).transpose(0, 1, 3, 2, 4).reshape(rows, -1)
+    tokens, qkv, fc, small = enter(
+        by_plane(inputs), (w_query, w_key, w_value), w_fc, [v.reshape(1, -1) for v in vectors], sizes
+    )
     tokens = tokens.reshape(n_rows, width)
 
     def over_blk(matrix):
         return lax.all_gather(matrix, "blk", axis=0, tiled=True)
 
     qkv = over_blk(qkv.reshape(plane * rows, 3 * share))
-    out_part = over_blk(w_out).reshape(n_uly, n_blk // n_uly, rows, width)
-    out_part = lax.all_to_all(out_part, "uly", split_axis=0, concat_axis=0, tiled=True)
-    out_part = out_part.transpose(1, 0, 2, 3).reshape(share, width)
-    fc = over_blk(fc.reshape(plane * rows, ff_share))
-    proj = over_blk(w_proj)
-
-    small = small.reshape(n_seq, n_uly, n_blk, lanes * 128)
-    flat = small.transpose(0, 2, 1, 3).reshape(n_seq * n_blk * n_uly, lanes * 128)
-    whole = [flat[:, i * rows : (i + 1) * rows].reshape(1, width) for i in range(8)]
-    at = 8 * rows
+    small = small.reshape(n_seq, n_uly, n_blk, SMALL, 128)
+    flat = small[:, :, :, :8, :rows].transpose(3, 0, 2, 1, 4).reshape(8, 1, width)
+    whole = [flat[i] for i in range(8)]
+    lanes = min(128, hidden_rows)
     bias_fc = lax.dynamic_slice(
-        small, (here_seq, here_uly, 0, at), (1, 1, n_blk, hidden_rows)
+        small, (here_seq, here_uly, 0, 8, 0), (1, 1, n_blk, hidden_rows // lanes, lanes)
     ).reshape(1, ff_share)
-    at += hidden_rows
-    lengths = small[:, 0, 0, at : at + doc_lengths.size].astype(jnp.int32)
+    lengths = small[:, 0, 0, SMALL - 1, : doc_lengths.size].astype(jnp.int32)
     lengths = lengths.reshape(n_seq, *doc_lengths.shape)
     gain_one, shift_one, bias_q, bias_v, bias_out, gain_two, shift_two, bias_proj = whole
     mine = lambda v: lax.dynamic_slice(v, (0, here * share), (1, share))
     bias_q, bias_v = mine(bias_q), mine(bias_v)
 
-    normed = norm_gather(tokens, gain_one, shift_one, plane, order)
+    normed, grad_out = norm_gather(
+        tokens, gain_one, shift_one, by_plane(cotangent), plane, order
+    )
+    normed, w_out, fc = lax.optimization_barrier((normed, w_out, fc))
+    out_part = over_blk(w_out)
+    out_part = out_part.reshape(n_uly, n_blk // n_uly, rows, width)
+    out_part = lax.all_to_all(out_part, "uly", split_axis=0, concat_axis=0, tiled=True)
+    out_part = out_part.transpose(1, 0, 2, 3).reshape(share, width)
+    fc = over_blk(fc.reshape(plane * rows, ff_share))
     normed = normed.reshape(plane * n_rows, width)
-    grad_out = over(by_plane(cotangent)).reshape(n_rows, width)
-
     made = product(normed, qkv)
     bias_all = jnp.concatenate([bias_q, jnp.zeros_like(bias_q), bias_v], axis=1)
     scales = jnp.repeat(jnp.array([[scale, 1.0, 1.0]], F32), share, axis=1)
     made = ((made + bias_all) * scales).astype(BF)
+
+    made, w_proj = lax.optimization_barrier((made, w_proj))
+    proj = over_blk(w_proj)
 
     groups = [
         [g * sharing + i for i in range(sharing)] for g in range(n_blk // sharing)
@@ -953,45 +1355,50 @@
     attended_low, natural, attended, logs, grad_all = attend(
         bounds, to_heads(made, 3), grad_out, plane, layout
     )
-    grad_all = grad_all.reshape(plane * n_rows, width)
     attended_low = from_heads(attended_low, 1)
-    hidden, normed_two = hidden_gather(
-        attended_low, out_part, tokens, bias_out, gain_two, shift_two, plane, order
-    )
-    normed_two = normed_two.reshape(plane * n_rows, width)
-    inner = product(normed_two, fc) + bias_fc
-    gelu_value, gelu_back = jax.vjp(gelu_tanh, inner)
-    active = gelu_value.astype(BF)
-    grad_w_proj = lax.psum_scatter(
-        transposed(active, grad_all).astype(BF), "blk", scatter_dimension=0, tiled=True
-    ).astype(F32)
-    grad_inner = gelu_back(against(grad_all, proj))[0].astype(BF)
-    grad_b_fc = jnp.sum(grad_inner.astype(F32), axis=0)
-    grad_fc = lax.psum_scatter(
-        transposed(normed_two, grad_inner).astype(BF), "blk", scatter_dimension=0, tiled=True
-    )
-    grad_hidden, sums_two, branch_all = branch_gather(
-        grad_inner, fc, hidden, grad_out, gain_two, plane, order
-    )
-    branch_all = branch_all.reshape(plane * n_rows, width)
-    grad_w_out = transposed(attended_low, branch_all).astype(BF)
+    hidden, own_two = hidden_norm(
+        attended_low, out_part, tokens, bias_out, gain_two, shift_two, order
+    )
+    normed_two, active, slope, grad_proj = feed(own_two, fc, bias_fc, grad_all)
+
+    def sum_blk(matrix):
+        return lax.psum_scatter(matrix, "blk", scatter_dimension=0, tiled=True)
+
+    grad_w_proj = sum_blk(grad_proj).astype(F32)
+    inner_grad, grad_hidden, branch, sums_two, sums_fc = back_feed(
+        grad_all, slope, proj, fc, hidden, grad_out, gain_two, order
+    )
+    _, grad_heads, grad_w_out, grad_fc = branch_spread(
+        branch, out_part, attended_low, normed_two.reshape(plane * n_rows, width), inner_grad, plane
+    )
+    grad_b_fc = sums_fc[0]
+    grad_fc = sum_blk(grad_fc)
     grad_w_out = grad_w_out.reshape(n_blk // n_uly, n_uly, rows, width).transpose(1, 0, 2, 3)
-    grad_w_out = lax.all_to_all(grad_w_out, "uly", split_axis=0, concat_axis=0, tiled=True)
-    grad_w_out = lax.psum_scatter(
-        grad_w_out.reshape(n_blk * rows, width), "blk", scatter_dimension=0, tiled=True
-    ).astype(F32)
-    grad_heads = to_heads(against(branch_all, out_part).astype(BF), 1)
-    backs, result = attend_back(
-        bounds, grad_heads, natural, attended, logs, active, proj, hidden, bias_proj, layout, scale
-    )
-    result = over(result.reshape(n_blk, held * part, width))
+    grad_w_out = grad_w_out.reshape(n_uly, n_blk // n_uly * rows, width)
+    grad_heads, grad_w_proj = lax.optimization_barrier((grad_heads, grad_w_proj))
+    grad_heads = to_heads(grad_heads, 1)
+    backs, result, grad_w_out = attend_back(
+        bounds,
+        grad_heads,
+        natural,
+        attended,
+        logs,
+        active,
+        proj,
+        hidden,
+        bias_proj,
+        grad_w_out,
+        layout,
+        scale,
+    )
     backs = from_heads(backs, 3)
     grad_bias = jnp.sum(backs.astype(F32), axis=0)
-    grad_qkv = lax.psum_scatter(
-        transposed(normed, backs).astype(BF), "blk", scatter_dimension=0, tiled=True
-    )
-    sums_one, grad_inputs = inputs_return(
-        backs, qkv, tokens, grad_hidden, gain_one, n_blk, order
+    grads = weight_grad(normed, backs, grad_w_out.reshape(n_blk, rows, width))
+    grads = sum_blk(grads).reshape(plane, rows, 4 * share)
+    grad_w_out = grads[:, :, 3 * share :].transpose(1, 0, 2).reshape(rows, width).astype(F32)
+    last, grad_fc = lax.optimization_barrier((backs, grad_fc))
+    sums_one, grad_inputs, result = inputs_return(
+        last, qkv, tokens, grad_hidden, gain_one, result, n_blk, order
     )
 
     def widened(vector):
@@ -1019,15 +1426,18 @@
     end_lanes = -(-used // 1024) * 8
     sums = jnp.pad(sums, ((0, 0),) * 3 + ((0, end_lanes * 128 - used),))
     sums = sums.transpose(0, 2, 1, 3).reshape(plane, n_blk, end_lanes, 128)
-    grad_qkv, grad_fc, sums = finish(
-        grad_qkv.reshape(plane, rows, 3 * share), grad_fc.reshape(plane, rows, ff_share), sums
-    )
+    *grad_qkv, grad_fc, sums = finish(
+        grads,
+        grad_fc.reshape(plane, rows, ff_share),
+        sums,
+        sizes,
+    )
+    grad_qkv = [g.astype(F32) for g in grad_qkv]
+    if runs == 1:
+        grad_fc = grad_fc.reshape(by_device).transpose(0, 1, 3, 2, 4).reshape(rows, -1)
+    grad_fc = grad_fc.astype(F32)
     sums = sums.reshape(-1)
     each = [sums[i * rows : (i + 1) * rows] for i in range(8)]
-    grad_qkv = grad_qkv.reshape(plane, rows, 3, share).transpose(2, 1, 0, 3)
-    grad_qkv = grad_qkv.reshape(3, rows, width).astype(F32)
-    grad_fc = grad_fc.reshape(n_seq, n_uly, rows, n_blk, hidden_rows)
-    grad_fc = grad_fc.transpose(2, 0, 3, 1, 4).reshape(rows, -1).astype(F32)
     return (
         from_plane(result),
         from_plane(grad_inputs),

time: 795 us -> 671 us (0.84)
  matrix products: 100 us -> 11.2 us
  waiting for transfers between devices: 106 us -> 45.7 us
  Pallas kernels: 478 us -> 531 us
  starting transfers between devices: 19.9 us -> 4.19 us
  local copies, waits for them, and re-layouts: 60.2 us -> 49 us
    dot_general x6 -> x0, matrix products: 75.7 us -> none  [the longest x4 47.1 us: transposed(): lax.dot_general(left_side, right_side, (((0,), (0,)), ((), ())), preferre...]
    reduce_scatter x4 -> x3, waiting for transfers between devices: 66.9 us -> 6.93 us  [sum_blk(): return lax.psum_scatter(matrix, 'blk', scatter_dimension=0, tiled=True)]
    pallas_call x5 -> x8, Pallas kernels: 285 us -> 323 us  [the longest x1 58.7 us: back_feed(): pl.pallas_call(functools.partial(back_feed_kernel, order), name='back_fee...]
    all_to_all x3 -> x0, starting transfers between devices: 14.9 us -> none  [the longest x2 11.4 us: over(): return lax.all_to_all(block, 'blk', split_axis=0, concat_axis=0, tiled=True)]
    all_gather x4, waiting for transfers between devices: 23.7 us -> 38 us  [over_blk(): return lax.all_gather(matrix, 'blk', axis=0, tiled=True)]
    all_to_all x3 -> x0, waiting for transfers between devices: 13.7 us -> none  [the longest x1 13.7 us: on_device(): lax.all_to_all(grad_w_out, 'uly', split_axis=0, concat_axis=0, tiled=True)]
    dot_general x2 -> x1, matrix products: 24.5 us -> 11.2 us  [product(): return jnp.dot(left_side, right_side, preferred_element_type=F32)]
    convert_element_type x6 -> x2, local copies, waits for them, and re-layouts: 11.5 us -> 0.93 us  [the longest x1 0.84 us: on_device(): grads[:, :, 3 * share:].transpose(1, 0, 2).reshape(rows, width).astype(F32)]
  transfers between devices with their start and end apart: 12 -> 8, of which waited for: 5 -> 4; matrix products, arithmetic and copies ran while one was open for 14% -> 3% of each run, Pallas kernels for 49% -> 72%
where the time goes in v4:
time: 671 us; the launch traced here: 664 us
  Pallas kernels  531 us (79%)
  local copies, waits for them, and re-layouts  49 us (7%)
  waiting for transfers between devices  45.7 us (7%)
  between operations  14.8 us (2%)
  matrix products  11.2 us (2%)
  other arithmetic  8.42 us (1%)
    pallas_call x1, Pallas kernels, inputs_return(): pl.pallas_call(functools.partial(inputs_kernel, n_blk, order), name='inpu...  103 us
    pallas_call x1, Pallas kernels, attend_back(): pl.pallas_call(functools.partial(attend_back_kernel, layout, scale), name...  59.6 us
    pallas_call x1, Pallas kernels, back_feed(): pl.pallas_call(functools.partial(back_feed_kernel, order), name='back_fee...  58.7 us
    pallas_call x1, Pallas kernels, norm_gather(): pl.pallas_call(functools.partial(norm_kernel, order, n_blk), name='norm_g...  53.3 us
    pallas_call x1, Pallas kernels, feed(): pl.pallas_call(feed_kernel, name='feed', out_shape=(jax.ShapeDtypeStruct(...  51.6 us
    pallas_call x1, Pallas kernels, branch_spread(): pl.pallas_call(branch_kernel, name='branch_spread', out_shape=(jax.ShapeD...  50.5 us
    pallas_call x1, Pallas kernels, hidden_norm(): pl.pallas_call(functools.partial(hidden_kernel, order), name='hidden_norm...  44.8 us
    pallas_call x1, Pallas kernels, attend(): pl.pallas_call(functools.partial(attend_kernel, layout), name='attend', o...  44.7 us
  transfers between devices with their start and end apart: 8, of which 4 were waited for; matrix products, arithmetic and copies ran while one was open for 3% of the time, Pallas kernels for 72%

profile of v4, /device:TPU:8, one launch (start us, length us, event | category | flops | bytes accessed | tf_op | source)
XLA Modules:
  0.0 664.4 jit_solution(17563731493181634052)
XLA Ops:
  7.3 1.3 reshape.207.refs_8_
  8.6 1.3 reshape_reshape.3.refs_9_
  9.8 30.6 %enter.1 = (bf16[4,64,2048]{2,1,0:T(8,128)(2,1)}, bf16[8,64,768]{2,1,0:T(8,128)(2,1)}, bf16[8,64,1024]{2,1,0:T(8,128)(2,1)}, f32[8,4,16,128]{3,2,1,0:T(8,128)}) custom-call(bf16[4,64,2048]{2,1,0:T(8,128)(2,1)} %x_ref.1, bf16[64,2048]{1,0:T(8,128)(2,1)} %wq_ref.1, bf16[64,2048]{1,0:T(8,128)(2,1)} %wk_ref.1, bf16[64,2048]{1,0:T(8,128)(2,1)} %wv_ref.1, ...), custom_call_target="tpu_custom_call" | custom-call | bytes 1048576 | tf_op jit(solution)/shard_map/enter/pallas_call | solution.py:426
  40.5 0.9 slice.139
  41.7 1.2 copy-done.3
  42.9 53.3 %norm_gather.1 = (bf16[8,256,2048]{2,1,0:T(8,128)(2,1)S(1)}, bf16[256,2048]{1,0:T(8,128)(2,1)S(1)}) custom-call(bf16[256,2048]{1,0:T(8,128)(2,1)S(1)} %bitcast.39, f32[1,2048]{1,0:T(1,128)S(1)} %squeeze.25.gain, f32[1,2048]{1,0:T(1,128)S(1)} %squeeze.26.shift, bf16[4,64,2048]{2,1,0:T(8,128)(2,1)S(1)} %copy-done.22), custom_call_target="tpu_custom_call" | custom-call | bytes 1048576 | tf_op jit(solution)/shard_map/norm_gather/pallas_call | solution.py:476
  96.2 3.3 copy-done.7
  100.6 16.6 %all-gather.5.cloned.1.call-done.weight = bf16[2048,768]{1,0:T(8,128)(2,1)} async-done(((bf16[512,768]{1,0:T(8,128)(2,1)}), bf16[2048,768]{1,0:T(8,128)(2,1)}) %all-gather.5.cloned.1.call-update) | async-done | bytes 3145744 | tf_op jit(solution)/shard_map/all_gather | solution.py:1278
  117.2 11.2 %multiply_convert_fusion.qkv = bf16[2048,768]{1,0:T(8,128)(2,1)} fusion(f32[768]{0:T(1024)S(1)} %broadcast_in_dim.15, f32[768]{0:T(1024)S(1)} %fusion.1, bf16[2048,2048]{1,0:T(8,128)(2,1)} %bitcast.44, bf16[2048,768]{1,0:T(8,128)(2,1)} %all-gather.5.cloned.1.call-done.weight), kind=kOutput, calls=%fused_computation.2 | convolution fusion | flops 6447169536 | bytes 14686208 | tf_op jit(solution)/shard_map/dot_general | solution.py:31
  128.4 20.3 %all-gather.7.cloned.1.call-done = bf16[256,2048]{1,0:T(8,128)(2,1)} async-done(((bf16[64,2048]{1,0:T(8,128)(2,1)}), bf16[256,2048]{1,0:T(8,128)(2,1)}) %all-gather.7.cloned.1.call-update) | async-done | bytes 1048592 | tf_op jit(solution)/shard_map/all_gather | solution.py:1278
  148.8 3.5 all-to-all-start
  154.5 1.3 constant_dynamic-slice_fusion
  155.8 2.2 copy-done.14
  158.0 44.7 %attend.1 = (bf16[2048,256]{1,0:T(8,128)(2,1)S(1)}, bf16[3,4,1024,128]{3,2,1,0:T(8,128)(2,1)S(1)}, f32[4,1024,128]{2,1,0:T(8,128)S(1)}, f32[4,8,1024]{2,1,0:T(8,128)S(1)}, bf16[8,256,2048]{2,1,0:T(8,128)(2,1)}) custom-call(s32[4]{0:T(128)S(1)} %reshape.209.bounds, bf16[2048,768]{1,0:T(8,128)(2,1)S(1)} %copy-done.14, bf16[256,2048]{1,0:T(8,128)(2,1)S(1)} %get-tuple-element.69.cot), custom_call_target="tpu_custom_call" | custom-call | bytes 1048576 | tf_op jit(solution)/shard_map/attend/pallas_call | solution.py:567
  202.7 1.0 copy-done.11
  203.6 1.6 copy-done.13
  205.3 1.3 copy-done.16
  207.3 1.6 copy-done.12
  208.9 44.8 %hidden_norm.1 = (f32[256,2048]{1,0:T(8,128)S(1)}, bf16[256,2048]{1,0:T(8,128)(2,1)S(1)}) custom-call(bf16[2048,256]{1,0:T(8,128)(2,1)S(1)} %copy-done.12, bf16[256,2048]{1,0:T(8,128)(2,1)S(1)} %bitcast.42, bf16[256,2048]{1,0:T(8,128)(2,1)S(1)} %bitcast.40, f32[1,2048]{1,0:T(1,128)S(1)} %squeeze.29.bias, f32[1,2048]{1,0:T(1,128)S(1)} %squeeze.30.gain, ...), custom_call_target="tpu_custom_call" | custom-call | bytes 1048576 | tf_op jit(solution)/shard_map/hidden_norm/pallas_call | solution.py:731
  253.7 1.3 copy-done.9
  255.0 1.0 copy-done.21
  256.0 51.6 %feed.1 = (bf16[8,256,2048]{2,1,0:T(8,128)(2,1)}, bf16[2048,1024]{1,0:T(8,128)(2,1)}, bf16[2048,1024]{1,0:T(8,128)(2,1)}, bf16[1024,2048]{1,0:T(8,128)(2,1)}) custom-call(bf16[256,2048]{1,0:T(8,128)(2,1)} %copy-done.21, bf16[2048,1024]{1,0:T(8,128)(2,1)} %all-gather.9.cloned.1.call-done.weight_ref.weight, f32[1,1024]{1,0:T(1,128)} %bitcast.60, ...), custom_call_target="tpu_custom_call" | custom-call | bytes 1048576 | tf_op jit(solution)/shard_map/feed/pallas_call | solution.py:859
  307.7 1.0 all-gather.11.cloned.1.call-done.proj.weight
  308.8 58.7 %back_feed.1 = (bf16[2048,1024]{1,0:T(8,128)(2,1)}, f32[256,2048]{1,0:T(8,128)}, bf16[256,2048]{1,0:T(8,128)(2,1)}, f32[8,2048]{1,0:T(8,128)}, f32[8,1024]{1,0:T(8,128)}) custom-call(bf16[8,256,2048]{2,1,0:T(8,128)(2,1)} %get-tuple-element.70.cots, bf16[2048,1024]{1,0:T(8,128)(2,1)} %get-tuple-element.75.slope, ...), custom_call_target="tpu_custom_call" | custom-call | bytes 1048576 | tf_op jit(solution)/shard_map/back_feed/pallas_call | solution.py:957
  367.5 50.5 %branch_spread.1 = (bf16[8,256,2048]{2,1,0:T(8,128)(2,1)}, bf16[2048,256]{1,0:T(8,128)(2,1)}, bf16[256,2048]{1,0:T(8,128)(2,1)}, bf16[2048,1024]{1,0:T(8,128)(2,1)}) custom-call(bf16[256,2048]{1,0:T(8,128)(2,1)} %get-tuple-element.78.own, bf16[256,2048]{1,0:T(8,128)(2,1)} %bitcast.43, bf16[2048,256]{1,0:T(8,128)(2,1)} %copy-done.11, ...), custom_call_target="tpu_custom_call" | custom-call | bytes 1048576 | tf_op jit(solution)/shard_map/branch_spread/pallas_call | solution.py:1029
  418.9 2.8 convert_element_type.42
  421.6 59.6 %attend_back.1 = (bf16[2048,768]{1,0:T(8,128)(2,1)}, bf16[256,2048]{1,0:T(8,128)(2,1)}, bf16[4,64,2048]{2,1,0:T(8,128)(2,1)}) custom-call(s32[4]{0:T(128)} %copy-done.30, bf16[2048,256]{1,0:T(8,128)(2,1)} %get-tuple-element.83.grad, bf16[3,4,1024,128]{3,2,1,0:T(8,128)(2,1)} %copy-done.13, f32[4,1024,128]{2,1,0:T(8,128)} %copy-done.16, ...), custom_call_target="tpu_custom_call" | custom-call | bytes 1048576 | tf_op jit(solution)/shard_map/attend_back/pallas_call | solution.py:674
  481.3 1.9 copy-done
  483.2 3.5 copy-done.8
  486.7 1.2 copy-done.20
  487.9 8.7 %weight_grad.1 = bf16[2048,1024]{1,0:T(8,128)(2,1)S(1)} custom-call(bf16[2048,2048]{1,0:T(8,128)(2,1)S(1)} %bitcast.45, bf16[2048,768]{1,0:T(8,128)(2,1)S(1)} %copy-done, bf16[4,64,2048]{2,1,0:T(8,128)(2,1)S(1)} %copy-done.20), custom_call_target="tpu_custom_call" | custom-call | bytes 1048576 | tf_op jit(solution)/shard_map/weight_grad/pallas_call | solution.py:1125
  496.6 2.0 copy-done.2
  498.6 0.9 slice_reduce_fusion.6
  501.5 1.2 copy-done.5
  502.7 1.9 copy-done.15
  504.6 2.2 copy-done.17
  506.8 1.2 copy-done.19
  508.0 103.4 %inputs_return.1 = (f32[8,2048]{1,0:T(8,128)S(1)}, bf16[4,64,2048]{2,1,0:T(8,128)(2,1)S(1)}, bf16[4,64,2048]{2,1,0:T(8,128)(2,1)S(1)}) custom-call(bf16[2048,768]{1,0:T(8,128)(2,1)S(1)} %copy-done.1, bf16[2048,768]{1,0:T(8,128)(2,1)S(1)} %copy-done.15, bf16[256,2048]{1,0:T(8,128)(2,1)S(1)} %bitcast.41, f32[256,2048]{1,0:T(8,128)S(1)} %copy-done.17, ...), custom_call_target="tpu_custom_call" | custom-call | bytes 1048576 | tf_op jit(solution)/shard_map/inputs_return/pallas_call | solution.py:1091
  611.4 1.0 copy-done.24
  612.4 1.0 copy-done.26
  613.8 6.9 %reduce-scatter.8.cloned.1.call-done = bf16[512,1024]{1,0:T(8,128)(2,1)} async-done(((bf16[2048,1024]{1,0:T(8,128)(2,1)}), bf16[512,1024]{1,0:T(8,128)(2,1)}) %reduce-scatter.8.cloned.1.call-update) | async-done | bytes 1048592 | tf_op jit(solution)/shard_map/reduce_scatter | solution.py:1365
  620.7 1.0 convert_bitcast_fusion
  621.7 1.2 copy-done.18
  623.0 1.2 copy-done.23
  624.2 25.2 %finish.1 = (bf16[64,2048]{1,0:T(8,128)(2,1)S(1)}, bf16[64,2048]{1,0:T(8,128)(2,1)S(1)}, bf16[64,2048]{1,0:T(8,128)(2,1)S(1)}, bf16[64,8192]{1,0:T(8,128)(2,1)S(1)}, f32[8,128]{1,0:T(8,128)S(1)}) custom-call(bf16[8,64,1024]{2,1,0:T(8,128)(2,1)S(1)} %bitcast.47, bf16[8,64,1024]{2,1,0:T(8,128)(2,1)S(1)} %bitcast.48, f32[8,4,8,128]{3,2,1,0:T(8,128)S(1)} %reshape.221.small_ref), custom_call_target="tpu_custom_call" | custom-call | bytes 1048576 | tf_op jit(solution)/shard_map/finish/pallas_call | solution.py:1190
  649.4 1.5 convert_element_type.50
  655.3 1.0 copy.76
  656.3 1.0 copy.77
  (122 shorter events, 12.2 us)
Async XLA Ops:
  7.2 93.3 %copy-start.32 = (f32[3]{0:T(128)S(1)}, f32[3]{0:T(128)}, u32[]{:S(2)}) copy-start(f32[3]{0:T(128)} %constant.86) | copy-start | bytes 40
  7.2 34.5 %copy-start.22 = (bf16[4,64,2048]{2,1,0:T(8,128)(2,1)S(1)}, bf16[4,64,2048]{2,1,0:T(8,128)(2,1)}, u32[]{:S(2)}) copy-start(bf16[4,64,2048]{2,1,0:T(8,128)(2,1)} %cot_ref.1) | copy-start | bytes 3145732
  7.2 110.0 %all-gather.5.cloned.1.call-start = ((), (), s32[]{:S(2)}) async-start(), calls=%async_computation.4 | async-start | bytes 3932160 | tf_op jit(solution)/shard_map/all_gather | solution.py:1278
  40.4 108.3 %all-gather.7.cloned.1.call-start = ((), (), s32[]{:S(2)}) async-start(), calls=%async_computation.5 | async-start | bytes 1310720 | tf_op jit(solution)/shard_map/all_gather | solution.py:1278
  41.7 1.2 copy-start.3
  96.2 3.3 copy-start.7
  99.5 56.3 %copy-start.10 = (bf16[256,2048]{1,0:T(8,128)(2,1)}, bf16[256,2048]{1,0:T(8,128)(2,1)S(1)}, u32[]{:S(2)}) copy-start(bf16[256,2048]{1,0:T(8,128)(2,1)S(1)} %get-tuple-element.69.cot) | copy-start | bytes 3145732
  99.5 156.5 %all-gather.9.cloned.1.call-start = ((), (), s32[]{:S(2)}) async-start(), calls=%async_computation.6 | async-start | bytes 5242880 | tf_op jit(solution)/shard_map/all_gather | solution.py:1278
  100.3 208.5 %all-gather.11.cloned.1.call-start = ((), (), s32[]{:S(2)}) async-start(), calls=%async_computation.7 | async-start | bytes 5242880 | tf_op jit(solution)/shard_map/all_gather | solution.py:1278
  128.4 78.9 %copy-start.4 = (bf16[4,64,2048]{2,1,0:T(8,128)(2,1)S(1)}, bf16[4,64,2048]{2,1,0:T(8,128)(2,1)}, u32[]{:S(2)}) copy-start(bf16[4,64,2048]{2,1,0:T(8,128)(2,1)} %get-tuple-element.63) | copy-start | bytes 3145732
  148.8 58.5 %all-to-all-start = ((bf16[4,1,64,2048]{3,2,1,0:T(8,128)(2,1)}), bf16[4,1,64,2048]{3,2,1,0:T(8,128)(2,1)S(1)}, u32[]{:S(2)}, u32[]{:S(2)}) async-start(bf16[4,1,64,2048]{3,2,1,0:T(8,128)(2,1)} %bitcast.53), calls=%async_computation | async-start | bytes 2097152 | tf_op jit(solution)/shard_map/all_to_all | solution.py:1300
  152.3 266.6 %reduce-scatter.4.cloned.1.call-start = ((), (), s32[]{:S(2)}) async-start(), calls=%async_computation.8 | async-start | bytes 5242880 | tf_op jit(solution)/shard_map/reduce_scatter | solution.py:1365
  154.2 153.4 %copy-start.30 = (s32[4]{0:T(128)}, s32[4]{0:T(128)S(1)}, u32[]{:S(2)}) copy-start(s32[4]{0:T(128)S(1)} %reshape.209.bounds) | copy-start | bytes 52
  154.3 153.4 %copy-start.29 = (f32[1,2048]{1,0:T(1,128)}, f32[1,2048]{1,0:T(1,128)S(1)}, u32[]{:S(2)}) copy-start(f32[1,2048]{1,0:T(1,128)S(1)} %squeeze.30.gain) | copy-start | bytes 24580
  155.8 2.2 copy-start.14
  202.6 1.0 copy-start.11
  203.6 1.6 copy-start.13
  205.3 1.3 copy-start.16
  206.6 0.7 copy-start.28
  207.3 100.4 %copy-start.6 = (bf16[4,1,64,2048]{3,2,1,0:T(8,128)(2,1)}, bf16[4,1,64,2048]{3,2,1,0:T(8,128)(2,1)S(1)}, u32[]{:S(2)}) copy-start(bf16[4,1,64,2048]{3,2,1,0:T(8,128)(2,1)S(1)} %all-to-all-done) | copy-start | bytes 3145732
  207.3 1.6 copy-start.12
  253.7 1.3 copy-start.9
  255.0 1.0 copy-start.21
  307.7 193.8 %reduce-scatter.6.cloned.1.call-start = ((), (), s32[]{:S(2)}) async-start(), calls=%async_computation.9 | async-start | bytes 5242880 | tf_op jit(solution)/shard_map/reduce_scatter | solution.py:1365
  418.0 202.8 %reduce-scatter.8.cloned.1.call-start = ((), (), s32[]{:S(2)}) async-start(), calls=%async_computation.10 | async-start | bytes 5242880 | tf_op jit(solution)/shard_map/reduce_scatter | solution.py:1365
  481.3 1.9 copy-start
  483.2 3.5 copy-start.8
  486.7 1.2 copy-start.20
  496.6 2.0 copy-start.2
  498.6 1.0 copy-start.31
  498.6 1.9 copy-start.1
  501.5 1.2 copy-start.5
  502.7 1.9 copy-start.15
  504.6 2.2 copy-start.17
  506.8 1.2 copy-start.19
  611.4 1.0 copy-start.24
  612.4 1.0 copy-start.26
  621.7 1.2 copy-start.18
  623.0 1.2 copy-start.23
  624.2 31.1 %copy-start.27 = (bf16[4,64,2048]{2,1,0:T(8,128)(2,1)S(1)}, bf16[4,64,2048]{2,1,0:T(8,128)(2,1)}, u32[]{:S(2)}) copy-start(bf16[4,64,2048]{2,1,0:T(8,128)(2,1)} %copy-done.26) | copy-start | bytes 3145732
  649.4 6.9 %copy-start.25 = (bf16[4,64,2048]{2,1,0:T(8,128)(2,1)S(1)}, bf16[4,64,2048]{2,1,0:T(8,128)(2,1)}, u32[]{:S(2)}) copy-start(bf16[4,64,2048]{2,1,0:T(8,128)(2,1)} %copy-done.24) | copy-start | bytes 3145732
Sparse Core Ops, SparseCore 0:
  40.5 76.6 all-gather.4
  118.8 29.9 all-gather.6
  150.3 77.6 all-gather.8
  229.4 79.2 all-gather.10
  310.9 77.9 reduce-scatter.3
  418.1 78.0 reduce-scatter.5
  498.7 121.9 reduce-scatter.7

commit v5 on v4

--- a/solution.py
+++ b/solution.py
@@ -19,6 +19,7 @@
 ANY = pl.BlockSpec(memory_space=pl.ANY)
 VMEM = pl.BlockSpec(memory_space=pltpu.VMEM)
 MIB = 2**20
+GRANT = 60 * MIB
 CHUNK = 16
 TILE = 2048
 
@@ -169,106 +170,154 @@
 SPREAD = 13
 
 
-def collect(
-    multiply, total, to_twin, from_twin, mine, in_x, in_y, send, recv, prepare=lambda block: None
-):
-    _, (beside, across, twin), here, other = place()
-    rows, width = total.shape
-    half = rows // 2
-    parts = (pl.ds(0, half), pl.ds(half, half))
-    copy = sender(send, recv)
-    tiles = width // TILE
-
-    def each_tile(body):
+class ChipSums:
+    def __init__(self, multiply, total, to_twin, from_twin, mine, send, recv, prepare=None):
+        _, (_, _, self.twin), self.here, self.other = place()
+        self.multiply, self.prepare = multiply, prepare or (lambda block: None)
+        self.total, self.mine = total, mine
+        self.to_twin, self.from_twin = to_twin, from_twin
+        self.copy = sender(send, recv)
+        self.sent = []
+
+    def each_tile(self, body):
         def step(t, carry):
             body(pl.ds(pl.multiple_of(t * TILE, TILE), TILE))
             return carry
 
-        lax.fori_loop(0, tiles, step, 0)
-
-    to_twins = []
-
-    def for_twin(k):
+        lax.fori_loop(0, self.total.shape[1] // TILE, step, 0)
+
+    def for_twin(self, k):
         def term(cols):
-            to_twin[k, :, cols] = multiply(other[k], cols).astype(BF)
-
-        prepare(other[k])
-        each_tile(term)
-        to_twins.append(copy(k, to_twin.at[k], from_twin.at[k], twin))
-
-    def for_here(k):
-        prepare(here[k])
-        to_twins[k].wait_recv()
-
+            self.to_twin[k, :, cols] = self.multiply(self.other[k], cols).astype(BF)
+
+        self.prepare(self.other[k])
+        self.each_tile(term)
+        self.sent.append(self.copy(k, self.to_twin.at[k], self.from_twin.at[k], self.twin))
+
+    def for_here(self, k):
         def term(cols):
-            both = multiply(here[k], cols) + from_twin[k, :, cols].astype(F32)
+            both = self.multiply(self.here[k], cols) + self.from_twin[k, :, cols].astype(F32)
             if k < 3:
-                mine[k, :, cols] = both.astype(BF)
+                self.mine[k, :, cols] = both.astype(BF)
             else:
-                total[:, cols] = both
-
-        each_tile(term)
-
-    started = []
-    for_twin(0)
-    for_twin(1)
-    for_here(0)
-    dx = copy(4, mine.at[0, parts[0]], in_x.at[0], beside)
-    dy = copy(5, mine.at[0, parts[1]], in_y.at[0], across)
-    for_twin(2)
-    for_here(1)
-    started.append(copy(6, mine.at[1, parts[0]], in_x.at[1], beside))
-    for_twin(3)
-    for_here(2)
-    started.append(copy(7, mine.at[2, parts[1]], in_y.at[1], across))
-    for_here(3)
-    yield
-
-    def add(k, part, arrived):
+                self.total[:, cols] = both
+
+        self.prepare(self.here[k])
+        self.sent[k].wait_recv()
+        self.each_tile(term)
+
+    def close(self):
+        for made in self.sent:
+            made.wait_send()
+
+
+class Cross:
+    def __init__(self, total, mine, in_x, in_y, send, recv, cut=None):
+        _, (self.beside, self.across, _), _, _ = place()
+        self.total, self.mine, self.in_x, self.in_y = total, mine, in_x, in_y
+        rows = total.shape[0]
+        self.cut = cut or rows // 2
+        self.rest = rows - self.cut
+        self.parts = (pl.ds(0, self.cut), pl.ds(self.cut, self.rest))
+        self.copy = sender(send, recv)
+        self.started = []
+
+    def to_x(self, i, k, part, slot):
+        rows = (self.cut, self.rest)[part]
+        target = self.in_x.at[slot, pl.ds(0, rows)]
+        return self.copy(i, self.mine.at[k, self.parts[part]], target, self.beside)
+
+    def to_y(self, i, k, part, slot):
+        rows = (self.cut, self.rest)[part]
+        target = self.in_y.at[slot, pl.ds(0, rows)]
+        return self.copy(i, self.mine.at[k, self.parts[part]], target, self.across)
+
+    def begin(self, k):
+        if k == 0:
+            self.dx = self.to_x(4, 0, 0, 0)
+            self.dy = self.to_y(5, 0, 1, 0)
+        elif k == 1:
+            self.started.append(self.to_x(6, 1, 0, 1))
+        else:
+            self.started.append(self.to_y(7, 2, 1, 1))
+
+    def add(self, k, first, rows, arrived):
         def step(t, carry):
             at = pl.ds(pl.multiple_of(t * CHUNK, CHUNK), CHUNK)
-            to = pl.ds(pl.multiple_of(part * half + t * CHUNK, CHUNK), CHUNK)
-            mine[k, to] = (mine[k, to].astype(F32) + arrived[0, at].astype(F32)).astype(BF)
+            to = pl.ds(pl.multiple_of(first + t * CHUNK, CHUNK), CHUNK)
+            both = self.mine[k, to].astype(F32) + arrived[0, at].astype(F32)
+            self.mine[k, to] = both.astype(BF)
             return carry
 
-        lax.fori_loop(0, half // CHUNK, step, 0)
-
-    dy.wait_recv()
-    add(1, 1, in_y)
-    started.append(copy(8, mine.at[1, parts[1]], in_x.at[2], beside))
-    dx.wait_recv()
-    add(2, 0, in_x)
-    started.append(copy(9, mine.at[2, parts[0]], in_y.at[2], across))
+        lax.fori_loop(0, rows // CHUNK, step, 0)
+
+    def diagonals(self):
+        self.dy.wait_recv()
+        self.add(1, self.cut, self.rest, self.in_y)
+        self.started.append(self.to_x(8, 1, 1, 2))
+        self.dx.wait_recv()
+        self.add(2, 0, self.cut, self.in_x)
+        self.started.append(self.to_y(9, 2, 0, 2))
+
+    def finish(self):
+        total, in_x, in_y = self.total, self.in_x, self.in_y
+        for made in self.started:
+            made.wait_recv()
+
+        def add(first, rows, x_slot, y_slot):
+            def step(t, carry):
+                at = pl.ds(pl.multiple_of(t * CHUNK, CHUNK), CHUNK)
+                to = pl.ds(pl.multiple_of(first + t * CHUNK, CHUNK), CHUNK)
+                total[to] += in_x[x_slot, at].astype(F32) + in_y[y_slot, at].astype(F32)
+                return carry
+
+            lax.fori_loop(0, rows // CHUNK, step, 0)
+
+        add(0, self.cut, 1, 2)
+        add(self.cut, self.rest, 2, 1)
+        for made in self.started + [self.dx, self.dy]:
+            made.wait_send()
+
+
+def collect(
+    multiply, total, to_twin, from_twin, mine, in_x, in_y, send, recv, prepare=None
+):
+    chip = ChipSums(multiply, total, to_twin, from_twin, mine, send, recv, prepare)
+    cross = Cross(total, mine, in_x, in_y, send, recv)
+    chip.for_twin(0)
+    for k in range(4):
+        if k < 3:
+            chip.for_twin(k + 1)
+        chip.for_here(k)
+        if k < 3:
+            cross.begin(k)
     yield
-    for made in started:
-        made.wait_recv()
-
-    def finish(t, carry):
-        at = pl.ds(pl.multiple_of(t * CHUNK, CHUNK), CHUNK)
-        low = pl.ds(pl.multiple_of(half + t * CHUNK, CHUNK), CHUNK)
-        total[at] += in_x[1, at].astype(F32) + in_y[2, at].astype(F32)
-        total[low] += in_x[2, at].astype(F32) + in_y[1, at].astype(F32)
-        return carry
-
-    lax.fori_loop(0, half // CHUNK, finish, 0)
-    for made in to_twins + started + [dx, dy]:
-        made.wait_send()
+    cross.diagonals()
+    yield
+    cross.finish()
+    chip.close()
 
 
 COLLECT = 10
 
 
-def collect_scratch(rows, width):
+def chip_scratch(rows, width):
+    return [pltpu.VMEM((4, rows, width), BF)] * 2
+
+
+def cross_scratch(rows, width, cut=None):
+    cut = cut or rows // 2
     return [
-        pltpu.VMEM((rows, width), F32),
-        pltpu.VMEM((4, rows, width), BF),
-        pltpu.VMEM((4, rows, width), BF),
         pltpu.VMEM((3, rows, width), BF),
-        pltpu.VMEM((3, rows // 2, width), BF),
-        pltpu.VMEM((3, rows // 2, width), BF),
+        pltpu.VMEM((3, rows - cut, width), BF),
+        pltpu.VMEM((3, rows - cut, width), BF),
         pltpu.SemaphoreType.DMA((COLLECT,)),
         pltpu.SemaphoreType.DMA((COLLECT,)),
     ]
+
+
+def collect_scratch(rows, width):
+    return [pltpu.VMEM((rows, width), F32)] + chip_scratch(rows, width) + cross_scratch(rows, width)
 
 
 def reorder(values, outer, inner, lanes):
@@ -333,39 +382,64 @@
     return [(s, (b + j) % n_blk, u) for j in range(1, n_blk)]
 
 
-def exchange_columns(copy, first, whole, cut, p, me, device, sizes, gather):
+def projection_spans(whole, cut, owner, sizes):
+    plane = sizes[0] * sizes[2]
+    share = whole[0].shape[1] // plane
+    at = pl.ds(pl.multiple_of(owner * share, share), share)
+    return [(matrix, at, cut, pl.ds(i * share, share)) for i, matrix in enumerate(whole)]
+
+
+def feed_spans(matrix, cut, owner, sizes):
     n_seq, _, n_uly, runs = sizes
-    plane = n_seq * n_uly
-    owner = p if gather else me
-    share = whole[0].shape[1] // plane
-    run_share = whole[3].shape[1] // (plane * runs)
+    share = matrix.shape[1] // (n_seq * n_uly * runs)
     spans = []
-    for i in range(3):
-        at = pl.ds(pl.multiple_of(owner * share, share), share)
-        spans.append((whole[i], at, cut[0], pl.ds(i * share, share)))
     for r in range(runs):
         at = ((owner // n_uly) * runs + r) * n_uly + owner % n_uly
-        at = pl.ds(pl.multiple_of(at * run_share, run_share), run_share)
-        spans.append((whole[3], at, cut[1], pl.ds(r * run_share, run_share)))
-    started = []
-    for i, (matrix, at, part, inside) in enumerate(spans):
-        if gather:
-            source, target = matrix.at[:, at], part.at[me, :, inside]
-        else:
-            source, target = part.at[p, :, inside], matrix.at[:, at]
-        started.append(copy(first + i, source, target, device))
-    return started
+        at = pl.ds(pl.multiple_of(at * share, share), share)
+        spans.append((matrix, at, cut, pl.ds(r * share, share)))
+    return spans
+
+
+def gather_columns(copy, first, spans, me, device):
+    return [
+        copy(first + i, matrix.at[:, at], cut.at[me, :, inside], device)
+        for i, (matrix, at, cut, inside) in enumerate(spans)
+    ]
+
+
+def return_columns(copy, first, spans, p, device):
+    return [
+        copy(first + i, cut.at[p, :, inside], matrix.at[:, at], device)
+        for i, (matrix, at, cut, inside) in enumerate(spans)
+    ]
+
+
+def plane_peers(plane):
+    (s, b, u), _, (_, _, _, me), _ = place()
+    n_uly = plane // 2
+    others = [(me + j) % plane for j in range(1, plane)]
+    return me, [(p, (p // n_uly, b, p % n_uly)) for p in others]
+
+
+def home(local):
+    def copy(i, source, target, _):
+        made = pltpu.make_async_copy(source, target, local.at[i])
+        made.start()
+        return made
+
+    return copy
 
 
 def entry_kernel(
     sizes, x_ref, wq_ref, wk_ref, wv_ref, fc_ref, *refs
 ):
     vectors, (bias_ref, lengths_ref), refs = refs[:8], refs[8:10], refs[10:]
-    enter_body(sizes, x_ref, wq_ref, wk_ref, wv_ref, fc_ref, vectors, bias_ref, lengths_ref, *refs)
+    matrices = (wq_ref, wk_ref, wv_ref)
+    enter_body(sizes, x_ref, matrices, fc_ref, vectors, bias_ref, lengths_ref, *refs)
 
 
 def enter_body(
-    sizes, x_ref, wq_ref, wk_ref, wv_ref, fc_ref, short, bias_ref, lengths_ref, tok, qkv, fc, small,
+    sizes, x_ref, matrices, fc_ref, short, bias_ref, lengths_ref, tok, qkv, fc, small,
     small_ref, blk_send, blk_recv, plane_send, plane_recv, local,
 ):
     n_seq, n_blk, n_uly, runs = sizes
@@ -380,35 +454,30 @@
         part = bias_ref[:, i * lanes : (i + 1) * lanes].astype(F32)
         small_ref[8 + i : 9 + i, :lanes] = part
     small_ref[SMALL - 1 :, : lengths_ref.shape[1]] = lengths_ref[...].astype(F32)
-    others = [(me + j) % plane for j in range(1, plane)]
-    friends = [(p // n_uly, b, p % n_uly) for p in others]
+    me, friends = plane_peers(plane)
     column = blk_peers(n_blk)
-    meet(friends + column)
+    meet([peer for _, peer in friends] + column)
     by_blk = sender(blk_send, blk_recv)
     by_plane = sender(plane_send, plane_recv)
-
-    def at_home(i, source, target, _):
-        made = pltpu.make_async_copy(source, target, local.at[i])
-        made.start()
-        return made
-
-    sources, targets = (wq_ref, wk_ref, wv_ref, fc_ref), (qkv, fc)
+    at_home = home(local)
+
+    def spans(owner):
+        return projection_spans(matrices, qkv, owner, sizes) + feed_spans(fc_ref, fc, owner, sizes)
+
     first = at_home(0, small_ref, small.at[me, b], None)
     vectors, started = [], []
     for j, peer in enumerate(column):
         vectors.append(by_blk(j, small_ref, small.at[me, b], peer))
     for j, peer in enumerate(column):
         started.append(by_blk(n_blk - 1 + j, x_ref.at[peer[1]], tok.at[b], peer))
-    for j, (p, peer) in enumerate(zip(others, friends)):
-        started += exchange_columns(
-            by_plane, pieces * j, sources, targets, p, me, peer, sizes, True
-        )
+    for j, (p, peer) in enumerate(friends):
+        started += gather_columns(by_plane, pieces * j, spans(p), me, peer)
     started.append(at_home(1, x_ref.at[b], tok.at[b], None))
-    started += exchange_columns(at_home, 2, sources, targets, me, me, None, sizes, True)
+    started += gather_columns(at_home, 2, spans(me), me, None)
     first.wait()
     for made in vectors:
         made.wait()
-    for j, peer in enumerate(friends):
+    for j, (_, peer) in enumerate(friends):
         at = small.at[me]
         started.append(by_plane(pieces * (plane - 1) + j, at, at, peer))
     for made in started:
@@ -442,13 +511,16 @@
             pltpu.SemaphoreType.DMA((pieces,)),
             pltpu.SemaphoreType.DMA((5 + runs,)),
         ],
-        compiler_params=pltpu.CompilerParams(collective_id=0, has_side_effects=True),
+        compiler_params=pltpu.CompilerParams(
+            collective_id=0, has_side_effects=True, vmem_limit_bytes=GRANT
+        ),
         cost_estimate=pl.CostEstimate(flops=0, bytes_accessed=MIB, transcendentals=0),
     )(x, *weights, fc, *short)
 
 
 def norm_kernel(
-    order, n_blk, tok, gain, shift, cot_ref, out, cot, own, send, recv, local, g_send, g_recv, kept
+    order, n_blk, tok, gain, shift, cot_ref, out, cot, cots,
+    own, send, recv, local, c_send, c_recv, c_local, g_send, g_recv, kept,
 ):
     (s, b, u), near, _, _ = place()
     column = blk_peers(n_blk)
@@ -456,9 +528,8 @@
     copy = sender(g_send, g_recv)
     count = cot_ref.shape[1]
     rows = pl.ds(pl.multiple_of(b * count, count), count)
-    started = [copy(j, cot_ref.at[peer[1]], cot.at[rows], peer) for j, peer in enumerate(column)]
-    started.append(pltpu.make_async_copy(cot_ref.at[b], cot.at[rows], kept))
-    started[-1].start()
+    exchanged = [copy(j, cot_ref.at[peer[1]], cot.at[rows], peer) for j, peer in enumerate(column)]
+    exchanged.append(home(kept)(0, cot_ref.at[b], cot.at[rows], None))
 
     def chunk(at):
         unit, _ = norm_parts(tok[at].astype(F32))
@@ -466,8 +537,9 @@
 
     each_chunk(own.shape[0], chunk)
     run(spread(own, out, send, recv, local))
-    for made in started:
+    for made in exchanged:
         made.wait()
+    run(spread(cot, cots, c_send, c_recv, c_local))
 
 
 def norm_gather(tok, gain, shift, cot, plane, order):
@@ -479,18 +551,19 @@
         out_shape=(
             jax.ShapeDtypeStruct((plane, rows, width), BF),
             jax.ShapeDtypeStruct((rows, width), BF),
+            jax.ShapeDtypeStruct((plane, rows, width), BF),
         ),
         in_specs=[VMEM] * 3 + [ANY],
-        out_specs=(ANY, ANY),
+        out_specs=(ANY, ANY, ANY),
         scratch_shapes=[pltpu.VMEM((rows, width), BF)]
-        + spread_scratch()
+        + spread_scratch() * 2
         + [
             pltpu.SemaphoreType.DMA((n_blk - 1,)),
             pltpu.SemaphoreType.DMA((n_blk - 1,)),
-            pltpu.SemaphoreType.DMA,
+            pltpu.SemaphoreType.DMA((1,)),
         ],
         compiler_params=pltpu.CompilerParams(
-            collective_id=1, has_side_effects=True, vmem_limit_bytes=16 * MIB
+            collective_id=1, has_side_effects=True, vmem_limit_bytes=GRANT
         ),
         cost_estimate=pl.CostEstimate(flops=0, bytes_accessed=MIB, transcendentals=0),
     )(tok, gain, shift, cot)
@@ -513,13 +586,11 @@
 
 
 def attend_kernel(
-    layout, bounds, qkv, cot, low, natural, attended, logs, out, send, recv, local,
+    layout, bounds, qkv, mixed, low, natural, attended, logs, mixed_out, u_send, u_recv, u_local
 ):
-    _, near, _, _ = place()
     _, _, _, part, heads = layout
-    meet(near)
-    moving = spread(cot, out, send, recv, local)
-    next(moving)
+    meet(row_peers(mixed.shape[0]))
+    mixing = mix_row(mixed, mixed_out, u_send, u_recv, u_local)
     share = heads * HD
     pairs, length = natural.shape[1:3]
     for row, s, position in chunks_of(layout):
@@ -547,22 +618,18 @@
             logs[p, :, start:stop] = log_total.T[:8]
         return carry
 
-    cut = (pairs + 1) // 2
-    lax.fori_loop(0, cut, pair, 0)
-    next(moving)
-    lax.fori_loop(cut, pairs, pair, 0)
-    next(moving)
+    lax.fori_loop(0, pairs, pair, 0)
     for row, s, position in chunks_of(layout):
         for h in range(heads):
             low[row : row + part, h * HD : (h + 1) * HD] = attended[
                 s * heads + h, position : position + part
             ].astype(BF)
-    run(moving)
-
-
-def attend(bounds, qkv, cot, plane, layout):
+    for made in mixing:
+        made.wait()
+
+
+def attend(bounds, qkv, mixed, layout):
     n_seq, n_uly, n_blk, part, heads = layout
-    rows, width = cot.shape
     pairs, length = n_seq * heads, n_uly * n_blk * part
     return pl.pallas_call(
         functools.partial(attend_kernel, layout),
@@ -572,48 +639,47 @@
             jax.ShapeDtypeStruct((3, pairs, length, HD), BF),
             jax.ShapeDtypeStruct((pairs, length, HD), F32),
             jax.ShapeDtypeStruct((pairs, 8, length), F32),
-            jax.ShapeDtypeStruct((plane, rows, width), BF),
+            jax.ShapeDtypeStruct(mixed.shape, BF),
         ),
         in_specs=[pl.BlockSpec(memory_space=pltpu.SMEM), VMEM, ANY],
         out_specs=(VMEM, VMEM, VMEM, VMEM, ANY),
-        scratch_shapes=[
-            pltpu.SemaphoreType.DMA((SPREAD,)),
-            pltpu.SemaphoreType.DMA((SPREAD,)),
-            pltpu.SemaphoreType.DMA,
-        ],
+        scratch_shapes=mix_scratch(mixed.shape[0]),
         compiler_params=pltpu.CompilerParams(
-            collective_id=2, has_side_effects=True, vmem_limit_bytes=40 * MIB
+            collective_id=2, has_side_effects=True, vmem_limit_bytes=GRANT
         ),
         cost_estimate=pl.CostEstimate(flops=0, bytes_accessed=MIB, transcendentals=0),
-    )(bounds, qkv, cot)
+    )(bounds, qkv, mixed)
 
 
 def attend_back_kernel(
-    layout, scale, bounds, grad, natural, attended, logs, act, weight, hid, bias, mixed,
-    back, out, mixed_out, grads, grads_back, key_grad, value_grad,
-    total, to_twin, from_twin, mine, in_x, in_y, c_send, c_recv, u_send, u_recv, local,
+    layout, scale, fused, bounds, grad, natural, attended, logs, mine_ref, own_ref, hid, bias,
+    mixed, normed_ref, back, out, mixed_out, *refs
 ):
+    weights, refs = (refs[0], refs[1:]) if fused else (None, refs)
+    (
+        grads, grads_back, key_grad, value_grad, mixed_in, normed, n_sems,
+        total, mine, in_x, in_y, c_send, c_recv, u_send, u_recv, u_local,
+    ) = refs
     (s, b, u), near, _, _ = place()
     rows = total.shape[0]
     _, _, _, part, heads = layout
     share = heads * HD
-    n_uly = mixed.shape[0]
-    in_row = [(s, b, (u + j) % n_uly) for j in range(1, n_uly)]
-    meet([near[1]] + in_row)
-    copy = sender(u_send, u_recv)
-    mixing = [copy(j, mixed.at[to[2]], mixed_out.at[u], to) for j, to in enumerate(in_row)]
-    mixing.append(pltpu.make_async_copy(mixed.at[u], mixed_out.at[u], local))
-    mixing[-1].start()
-
-    def multiply(block, cols):
-        return product(rows_of(act, block, rows), weight[:, cols])
-
-    moving = collect(multiply, total, to_twin, from_twin, mine, in_x, in_y, c_send, c_recv)
-    next(moving)
+    first = fetch((mine_ref.at[0], mine_ref.at[1], mine_ref.at[2], own_ref),
+                  (mine.at[0], mine.at[1], mine.at[2], total), n_sems)
+    if fused:
+        loading = pltpu.make_async_copy(normed_ref, normed, n_sems.at[4])
+        loading.start()
+    meet([near[1]] + row_peers(mixed.shape[0]))
+    cross = Cross(total, mine, in_x, in_y, c_send, c_recv, rows // 4)
+    for k in range(3):
+        first[k].wait()
+        cross.begin(k)
+    target = mixed_in if fused else mixed_out
+    mixing = mix_row(mixed, target, u_send, u_recv, u_local)
     pairs, length = natural.shape[1:3]
-    for row, s, position in chunks_of(layout):
+    for row, s_at, position in chunks_of(layout):
         for h in range(heads):
-            grads[s * heads + h, position : position + part] = grad[
+            grads[s_at * heads + h, position : position + part] = grad[
                 row : row + part, h * HD : (h + 1) * HD
             ]
 
@@ -647,57 +713,98 @@
 
     cut = (pairs + 1) // 2
     lax.fori_loop(0, cut, pair, 0)
-    next(moving)
+    cross.diagonals()
     lax.fori_loop(cut, pairs, pair, 0)
-    for row, s, position in chunks_of(layout):
+    for row, s_at, position in chunks_of(layout):
         for kind in range(3):
             for h in range(heads):
                 lane = kind * share + h * HD
                 back[row : row + part, lane : lane + HD] = grads_back[
-                    kind * pairs + s * heads + h, position : position + part
+                    kind * pairs + s_at * heads + h, position : position + part
                 ]
-    run(moving)
+    for made in mixing:
+        made.wait()
+    if fused:
+        loading.wait()
+        weight_terms(normed, back, mixed_in, weights)
+        mixed_out[...] = jnp.zeros_like(mixed_out)
+    first[3].wait()
+    cross.finish()
 
     def chunk(at):
         out[at] = (total[at] + hid[at] + bias[...]).astype(BF)
 
     each_chunk(rows, chunk)
-    for made in mixing:
-        made.wait()
 
 
 def attend_back(
-    bounds, grad, natural, attended, logs, act, weight, hid, bias, mixed, layout, scale
+    bounds, grad, natural, attended, logs, mine, own, hid, bias, mixed, normed, layout, scale,
+    fused,
 ):
     rows, width = hid.shape
     pairs, length = natural.shape[1:3]
+    wide = 3 * grad.shape[1]
+    out_shape = (
+        jax.ShapeDtypeStruct((grad.shape[0], wide), BF),
+        jax.ShapeDtypeStruct((rows, width), BF),
+        jax.ShapeDtypeStruct((16, 128) if fused else mixed.shape, BF),
+    )
+    out_specs = (VMEM, VMEM, VMEM if fused else ANY)
+    if fused:
+        out_shape += (jax.ShapeDtypeStruct((normed.shape[1], 4 * grad.shape[1]), BF),)
+        out_specs += (VMEM,)
     return pl.pallas_call(
-        functools.partial(attend_back_kernel, layout, scale),
+        functools.partial(attend_back_kernel, layout, scale, fused),
         name="attend_back",
-        out_shape=(
-            jax.ShapeDtypeStruct((grad.shape[0], 3 * grad.shape[1]), BF),
-            jax.ShapeDtypeStruct((rows, width), BF),
-            jax.ShapeDtypeStruct(mixed.shape, BF),
-        ),
-        in_specs=[pl.BlockSpec(memory_space=pltpu.SMEM)] + [VMEM] * 8 + [ANY],
-        out_specs=(VMEM, VMEM, ANY),
+        out_shape=out_shape,
+        in_specs=[pl.BlockSpec(memory_space=pltpu.SMEM)]
+        + [VMEM] * 4
+        + [ANY] * 2
+        + [VMEM] * 2
+        + [ANY] * 2,
+        out_specs=out_specs,
         scratch_shapes=[
             pltpu.VMEM((pairs, length, HD), BF),
             pltpu.VMEM((3 * pairs, length, HD), BF),
             pltpu.VMEM((length, HD), F32),
             pltpu.VMEM((length, HD), F32),
+            pltpu.VMEM(mixed.shape if fused else (16, 128), BF),
+            pltpu.VMEM(normed.shape if fused else (16, 128), BF),
+            pltpu.SemaphoreType.DMA((5,)),
+            pltpu.VMEM((rows, width), F32),
         ]
-        + collect_scratch(rows, width)
-        + [
-            pltpu.SemaphoreType.DMA((mixed.shape[0] - 1,)),
-            pltpu.SemaphoreType.DMA((mixed.shape[0] - 1,)),
-            pltpu.SemaphoreType.DMA,
-        ],
+        + cross_scratch(rows, width, rows // 4)
+        + mix_scratch(mixed.shape[0]),
         compiler_params=pltpu.CompilerParams(
-            collective_id=5, has_side_effects=True, vmem_limit_bytes=60 * MIB
+            collective_id=5, has_side_effects=True, vmem_limit_bytes=GRANT
         ),
         cost_estimate=pl.CostEstimate(flops=0, bytes_accessed=MIB, transcendentals=0),
-    )(bounds, grad, natural, attended, logs, act, weight, hid, bias, mixed)
+    )(bounds, grad, natural, attended, logs, mine, own, hid, bias, mixed, normed)
+
+
+def mix_row(source, target, send, recv, local):
+    (s, b, u), _, _, _ = place()
+    copy = sender(send, recv)
+    made = [
+        copy(j, source.at[to[2]], target.at[u], to)
+        for j, to in enumerate(row_peers(source.shape[0]))
+    ]
+    kept = pltpu.make_async_copy(source.at[u], target.at[u], local)
+    kept.start()
+    return made + [kept]
+
+
+def row_peers(n_uly):
+    (s, b, u), _, _, _ = place()
+    return [(s, b, (u + j) % n_uly) for j in range(1, n_uly)]
+
+
+def mix_scratch(n_uly):
+    return [
+        pltpu.SemaphoreType.DMA((n_uly - 1,)),
+        pltpu.SemaphoreType.DMA((n_uly - 1,)),
+        pltpu.SemaphoreType.DMA,
+    ]
 
 
 def rows_of(ref, block, rows):
@@ -739,7 +846,7 @@
         out_specs=(VMEM, VMEM),
         scratch_shapes=collect_scratch(rows, width),
         compiler_params=pltpu.CompilerParams(
-            collective_id=3, has_side_effects=True, vmem_limit_bytes=40 * MIB
+            collective_id=3, has_side_effects=True, vmem_limit_bytes=GRANT
         ),
         cost_estimate=pl.CostEstimate(flops=0, bytes_accessed=MIB, transcendentals=0),
     )(act, weight, tok, bias, gain, shift)
@@ -880,15 +987,16 @@
         ]
         + spread_scratch(),
         compiler_params=pltpu.CompilerParams(
-            collective_id=8, has_side_effects=True, vmem_limit_bytes=56 * MIB
+            collective_id=8, has_side_effects=True, vmem_limit_bytes=GRANT
         ),
         cost_estimate=pl.CostEstimate(flops=0, bytes_accessed=MIB, transcendentals=0),
     )(own, weight, bias, cots)
 
 
 def back_feed_kernel(
-    order, cots, slope, proj, weight, hid, cot, gain, inner_grad, grad_hidden, own, sums, bias,
-    cots_in, slope_in, sems,
+    order, cots, slope, normed_ref, proj, weight, hid, cot, gain,
+    fc_grad, grad_hidden, own, sums, bias,
+    inner_grad, normed, cots_in, slope_in, sems, n_sem,
     total, to_twin, from_twin, mine, in_x, in_y, c_send, c_recv,
 ):
     _, near, here, other = place()
@@ -905,6 +1013,8 @@
         )
 
     loads = [load(0)]
+    normed_load = pltpu.make_async_copy(normed_ref, normed, n_sem)
+    normed_load.start()
     sums[...] = jnp.zeros_like(sums)
     bias[...] = jnp.zeros_like(bias)
     meet(near)
@@ -928,11 +1038,19 @@
     def multiply(block, cols):
         return against(rows_of(inner_grad, block, rows), weight[cols, :])
 
-    run(
-        collect(
-            multiply, total, to_twin, from_twin, mine, in_x, in_y, c_send, c_recv, prepare
-        )
-    )
+    def fc_tile(t, carry):
+        at = pl.ds(pl.multiple_of(t * FC_TILE, FC_TILE), FC_TILE)
+        fc_grad[at, :] = transposed(normed[:, at], inner_grad[...]).astype(BF)
+        return carry
+
+    moving = collect(
+        multiply, total, to_twin, from_twin, mine, in_x, in_y, c_send, c_recv, prepare
+    )
+    next(moving)
+    next(moving)
+    normed_load.wait()
+    lax.fori_loop(0, width // FC_TILE, fc_tile, 0)
+    run(moving)
     inner, outer, lanes = order[1], order[0], order[2]
 
     def chunk(at):
@@ -951,50 +1069,51 @@
     each_chunk(rows, chunk)
 
 
-def back_feed(cots, slope, proj, weight, hid, cot, gain, order):
+def back_feed(cots, slope, normed, proj, weight, hid, cot, gain, order):
     rows, width = cot.shape
     ff = weight.shape[1]
     return pl.pallas_call(
         functools.partial(back_feed_kernel, order),
         name="back_feed",
         out_shape=(
-            jax.ShapeDtypeStruct((slope.shape[0], ff), BF),
+            jax.ShapeDtypeStruct((width, ff), BF),
             jax.ShapeDtypeStruct((rows, width), F32),
             jax.ShapeDtypeStruct((rows, width), BF),
             jax.ShapeDtypeStruct((8, width), F32),
             jax.ShapeDtypeStruct((8, ff), F32),
         ),
-        in_specs=[ANY, ANY] + [VMEM] * 5,
+        in_specs=[ANY] * 3 + [VMEM] * 5,
         out_specs=(VMEM,) * 5,
         scratch_shapes=[
+            pltpu.VMEM((slope.shape[0], ff), BF),
+            pltpu.VMEM(normed.shape, BF),
             pltpu.VMEM((2, rows, width), BF),
             pltpu.VMEM((2, rows, ff), BF),
             pltpu.SemaphoreType.DMA((2, 2)),
+            pltpu.SemaphoreType.DMA,
         ]
         + collect_scratch(rows, width),
         compiler_params=pltpu.CompilerParams(
-            collective_id=4, has_side_effects=True, vmem_limit_bytes=56 * MIB
+            collective_id=4, has_side_effects=True, vmem_limit_bytes=GRANT
         ),
         cost_estimate=pl.CostEstimate(flops=0, bytes_accessed=MIB, transcendentals=0),
-    )(cots, slope, proj, weight, hid, cot, gain)
+    )(cots, slope, normed, proj, weight, hid, cot, gain)
 
 
 def branch_kernel(
-    own, weight, low, normed, inner_grad, out, heads_grad, weight_grad, fc_grad,
-    rows_in, acc, sems, send, recv, local,
+    own, weight, low, act_ref, proj_ref, out, heads_grad, weight_grad, mine, total,
+    act, proj, rows_in, acc, sems, to_twin, from_twin, c_send, c_recv, a_sems, send, recv, local,
 ):
     _, near, _, _ = place()
     rows, width = own.shape
+    loading = fetch((act_ref, proj_ref), (act, proj), a_sems)
     meet(near)
     moving = Spread(own, out, send, recv, local)
-    tiles = width // FC_TILE
-
-    def fc_tile(t, carry):
-        at = pl.ds(pl.multiple_of(t * FC_TILE, FC_TILE), FC_TILE)
-        fc_grad[at, :] = transposed(normed[:, at], inner_grad[...]).astype(BF)
-        return carry
-
-    done = 0
+
+    def multiply(block, cols):
+        return product(rows_of(act, block, rows), proj[:, cols])
+
+    chip = ChipSums(multiply, total, to_twin, from_twin, mine, c_send, c_recv)
     for i, (left, right) in enumerate(pairs_of(moving)):
         fetched = fetch(
             (out.at[left], out.at[right]),
@@ -1018,14 +1137,20 @@
                 acc[:, cols] += term
             else:
                 weight_grad[:, cols] = (acc[:, cols] + term).astype(BF)
-        more = (3 * tiles // 8, 3 * tiles // 4, tiles, tiles)[i]
-        lax.fori_loop(done, more, fc_tile, 0)
-        done = more
-
-
-def branch_spread(own, weight, low, normed, inner_grad, plane):
+        if i == 0:
+            for made in loading:
+                made.wait()
+            for k in range(4):
+                chip.for_twin(k)
+        elif i == 1:
+            for k in range(4):
+                chip.for_here(k)
+    chip.close()
+
+
+def branch_spread(own, weight, low, act, proj, plane):
     rows, width = own.shape
-    share, ff = weight.shape[0], inner_grad.shape[1]
+    share = weight.shape[0]
     return pl.pallas_call(
         branch_kernel,
         name="branch_spread",
@@ -1033,37 +1158,47 @@
             jax.ShapeDtypeStruct((plane, rows, width), BF),
             jax.ShapeDtypeStruct((plane * rows, share), BF),
             jax.ShapeDtypeStruct((share, width), BF),
-            jax.ShapeDtypeStruct((width, ff), BF),
-        ),
-        in_specs=[VMEM] * 5,
-        out_specs=(ANY, VMEM, VMEM, VMEM),
+            jax.ShapeDtypeStruct((3, rows, width), BF),
+            jax.ShapeDtypeStruct((rows, width), F32),
+        ),
+        in_specs=[VMEM] * 3 + [ANY] * 2,
+        out_specs=(ANY, VMEM, VMEM, VMEM, VMEM),
         scratch_shapes=[
+            pltpu.VMEM(act.shape, BF),
+            pltpu.VMEM(proj.shape, BF),
             pltpu.VMEM((2 * rows, width), BF),
             pltpu.VMEM((share, width), F32),
             pltpu.SemaphoreType.DMA((2,)),
         ]
+        + chip_scratch(rows, width)
+        + [pltpu.SemaphoreType.DMA((4,))] * 2
+        + [pltpu.SemaphoreType.DMA((2,))]
         + spread_scratch(),
         compiler_params=pltpu.CompilerParams(
-            collective_id=9, has_side_effects=True, vmem_limit_bytes=56 * MIB
+            collective_id=9, has_side_effects=True, vmem_limit_bytes=GRANT
         ),
         cost_estimate=pl.CostEstimate(flops=0, bytes_accessed=MIB, transcendentals=0),
-    )(own, weight, low, normed, inner_grad)
+    )(own, weight, low, act, proj)
 
 
 def inputs_kernel(
-    n_blk, order, act, weight, tok, grad_hidden, gain, result, sums, out, result_out,
+    sizes, order, act, weight, tok, grad_hidden, gain, fc_ref, sums, out, fc,
     total, to_twin, from_twin, mine, in_x, in_y, c_send, c_recv, own,
-    send, recv, local, r_send, r_recv, r_local,
+    send, recv, local, f_send, f_recv, f_local,
 ):
-    _, near, _, _ = place()
+    n_seq, n_blk, n_uly, runs = sizes
     rows = total.shape[0]
-    meet(list(near) + blk_peers(n_blk))
-    leaving = return_rows(result, result_out, n_blk, r_send, r_recv, r_local)
+    me, friends = plane_peers(n_seq * n_uly)
+    meet([peer for _, peer in friends] + blk_peers(n_blk))
 
     def multiply(block, cols):
         return against(rows_of(act, block, rows), weight[cols, :])
 
     run(collect(multiply, total, to_twin, from_twin, mine, in_x, in_y, c_send, c_recv))
+    spans = feed_spans(fc, fc_ref, me, sizes)
+    leaving = return_columns(home(f_local), 0, spans, me, None)
+    for j, (p, peer) in enumerate(friends):
+        leaving += return_columns(sender(f_send, f_recv), runs * j, spans, p, peer)
     sums[...] = jnp.zeros_like(sums)
     inner, outer, lanes = order[1], order[0], order[2]
 
@@ -1080,29 +1215,34 @@
         made.wait()
 
 
-def inputs_return(act, weight, tok, grad_hidden, gain, result, n_blk, order):
+def inputs_return(act, weight, tok, grad_hidden, gain, fc, sizes, order):
     rows, width = tok.shape
-    back = jax.ShapeDtypeStruct((n_blk, rows // n_blk, width), BF)
-    moves = [
-        pltpu.SemaphoreType.DMA((n_blk - 1,)),
-        pltpu.SemaphoreType.DMA((n_blk - 1,)),
-        pltpu.SemaphoreType.DMA,
-    ]
+    n_blk, runs = sizes[1], sizes[3]
+    plane = fc.shape[0]
     return pl.pallas_call(
-        functools.partial(inputs_kernel, n_blk, order),
+        functools.partial(inputs_kernel, sizes, order),
         name="inputs_return",
-        out_shape=(jax.ShapeDtypeStruct((8, width), F32), back, back),
+        out_shape=(
+            jax.ShapeDtypeStruct((8, width), F32),
+            jax.ShapeDtypeStruct((n_blk, rows // n_blk, width), BF),
+            jax.ShapeDtypeStruct((fc.shape[1], plane * fc.shape[2]), BF),
+        ),
         in_specs=[VMEM] * 5 + [ANY],
         out_specs=(VMEM, ANY, ANY),
-        scratch_shapes=collect_scratch(rows, width) + [pltpu.VMEM((rows, width), BF)] + moves * 2,
+        scratch_shapes=collect_scratch(rows, width)
+        + [pltpu.VMEM((rows, width), BF)]
+        + [pltpu.SemaphoreType.DMA((n_blk - 1,))] * 2
+        + [pltpu.SemaphoreType.DMA]
+        + [pltpu.SemaphoreType.DMA((runs * (plane - 1),))] * 2
+        + [pltpu.SemaphoreType.DMA((runs,))],
         compiler_params=pltpu.CompilerParams(
-            collective_id=6, has_side_effects=True, vmem_limit_bytes=40 * MIB
+            collective_id=6, has_side_effects=True, vmem_limit_bytes=GRANT
         ),
         cost_estimate=pl.CostEstimate(flops=0, bytes_accessed=MIB, transcendentals=0),
-    )(act, weight, tok, grad_hidden, gain, result)
-
-
-def weight_kernel(left, right, mixed, out):
+    )(act, weight, tok, grad_hidden, gain, fc)
+
+
+def weight_terms(left, right, mixed, out):
     wide = right.shape[1]
     share = out.shape[1] - wide
     pieces = left.shape[1] // share
@@ -1114,65 +1254,58 @@
         return carry
 
     lax.fori_loop(0, out.shape[0] // FC_TILE, tile, 0)
-    for b in range(mixed.shape[0]):
+    for at in range(0, mixed.shape[0] * rows, rows):
+        b, first = at // rows, at * pieces
         for j in range(pieces):
-            at = (b * pieces + j) * rows
-            out[at : at + rows, wide:] = mixed[b, :, j * share : (j + 1) * share]
+            to = first + j * rows
+            out[to : to + rows, wide:] = mixed[b, :, j * share : (j + 1) * share]
 
 
 def weight_grad(left, right, mixed):
     width = left.shape[1]
     return pl.pallas_call(
-        weight_kernel,
+        weight_terms,
         name="weight_grad",
         out_shape=jax.ShapeDtypeStruct((width, 4 * right.shape[1] // 3), BF),
         in_specs=[VMEM] * 3,
         out_specs=VMEM,
-        compiler_params=pltpu.CompilerParams(vmem_limit_bytes=32 * MIB),
+        compiler_params=pltpu.CompilerParams(vmem_limit_bytes=GRANT),
         cost_estimate=pl.CostEstimate(flops=0, bytes_accessed=MIB, transcendentals=0),
     )(left, right, mixed)
 
 
 def end_kernel(
-    sizes, qkv_ref, fc_ref, small_ref, gq, gk, gv, fc, small,
-    gathered, partial, arrived, blk_send, blk_recv, plane_send, plane_recv, local,
+    sizes, qkv_ref, small_ref, result_ref, gq, gk, gv, small, result,
+    gathered, partial, arrived,
+    blk_send, blk_recv, plane_send, plane_recv, local, r_send, r_recv, r_local,
 ):
-    n_seq, n_blk, n_uly, runs = sizes
-    (s, b, u), _, (_, _, _, me), _ = place()
+    n_seq, n_blk, n_uly, _ = sizes
+    (s, b, u), _, _, _ = place()
     plane = n_seq * n_uly
-    pieces = 3 + runs
-    others = [(me + j) % plane for j in range(1, plane)]
-    friends = [(p // n_uly, b, p % n_uly) for p in others]
+    me, friends = plane_peers(plane)
     column = blk_peers(n_blk)
-    meet(friends + column)
+    meet([peer for _, peer in friends] + column)
     by_blk = sender(blk_send, blk_recv)
     by_plane = sender(plane_send, plane_recv)
-
-    def at_home(i, source, target, _):
-        made = pltpu.make_async_copy(source, target, local.at[i])
-        made.start()
-        return made
-
-    sources, targets = (qkv_ref, fc_ref), (gq, gk, gv, fc)
+    at_home = home(local)
+    spans = projection_spans((gq, gk, gv), qkv_ref, me, sizes)
     first = at_home(0, small_ref.at[me], gathered.at[me], None)
-    vectors, started = [], []
-    for j, (p, peer) in enumerate(zip(others, friends)):
-        slot = pieces * (plane - 1) + j
-        vectors.append(by_plane(slot, small_ref.at[p], gathered.at[me], peer))
-    for j, (p, peer) in enumerate(zip(others, friends)):
-        started += exchange_columns(
-            by_plane, pieces * j, targets, sources, p, me, peer, sizes, False
-        )
-    started += exchange_columns(at_home, 2, targets, sources, me, me, None, sizes, False)
+    vectors = [
+        by_plane(3 * (plane - 1) + j, small_ref.at[p], gathered.at[me], peer)
+        for j, (p, peer) in enumerate(friends)
+    ]
+    started = return_rows(result_ref, result, n_blk, r_send, r_recv, r_local)
+    for j, (p, peer) in enumerate(friends):
+        started += return_columns(by_plane, 3 * j, spans, p, peer)
+    started += return_columns(at_home, 2, spans, me, None)
     first.wait()
     for made in vectors:
         made.wait()
     partial[...] = jnp.sum(gathered[...], axis=0)
-    own = at_home(1, partial.at[b], arrived.at[b], None)
-    sent = [
+    sent = [at_home(1, partial.at[b], arrived.at[b], None)]
+    sent += [
         by_blk(j, partial.at[peer[1]], arrived.at[b], peer) for j, peer in enumerate(column)
     ]
-    own.wait()
     for made in sent:
         made.wait()
     small[...] = jnp.sum(arrived[...], axis=0)
@@ -1180,40 +1313,35 @@
         made.wait()
 
 
-def finish(qkv, fc, small, sizes):
-    n_seq, n_blk, n_uly, runs = sizes
+def finish(qkv, small, result, sizes):
+    n_seq, n_blk, n_uly, _ = sizes
     plane = n_seq * n_uly
     rows, share = qkv.shape[1], qkv.shape[2] // 4
     tail = small.shape[2:]
-    pieces = (4 + runs) * (plane - 1)
     whole = jax.ShapeDtypeStruct((rows, plane * share), BF)
+    back = jax.ShapeDtypeStruct((n_blk, result.shape[0] // n_blk, result.shape[1]), BF)
+    blk_sems = [pltpu.SemaphoreType.DMA((n_blk - 1,))] * 2
     return pl.pallas_call(
         functools.partial(end_kernel, sizes),
         name="finish",
-        out_shape=(
-            whole,
-            whole,
-            whole,
-            jax.ShapeDtypeStruct((rows, plane * fc.shape[2]), BF),
-            jax.ShapeDtypeStruct(tail, small.dtype),
-        ),
+        out_shape=(whole, whole, whole, jax.ShapeDtypeStruct(tail, small.dtype), back),
         in_specs=[ANY] * 3,
-        out_specs=(ANY, ANY, ANY, ANY, VMEM),
+        out_specs=(ANY, ANY, ANY, VMEM, ANY),
         scratch_shapes=[
             pltpu.VMEM((plane, n_blk) + tail, F32),
             pltpu.VMEM((n_blk,) + tail, F32),
             pltpu.VMEM((n_blk,) + tail, F32),
-            pltpu.SemaphoreType.DMA((n_blk - 1,)),
-            pltpu.SemaphoreType.DMA((n_blk - 1,)),
-            pltpu.SemaphoreType.DMA((pieces,)),
-            pltpu.SemaphoreType.DMA((pieces,)),
-            pltpu.SemaphoreType.DMA((5 + runs,)),
-        ],
+        ]
+        + blk_sems
+        + [pltpu.SemaphoreType.DMA((4 * (plane - 1),))] * 2
+        + [pltpu.SemaphoreType.DMA((5,))]
+        + blk_sems
+        + [pltpu.SemaphoreType.DMA],
         compiler_params=pltpu.CompilerParams(
             collective_id=7, has_side_effects=True, vmem_limit_bytes=16 * MIB
         ),
         cost_estimate=pl.CostEstimate(flops=0, bytes_accessed=MIB, transcendentals=0),
-    )(qkv, fc, small)
+    )(qkv, small, result)
 
 
 def on_device(
@@ -1277,6 +1405,8 @@
     def over_blk(matrix):
         return lax.all_gather(matrix, "blk", axis=0, tiled=True)
 
+    out_part = over_blk(w_out)
+    tokens, out_part = lax.optimization_barrier((tokens, out_part))
     qkv = over_blk(qkv.reshape(plane * rows, 3 * share))
     small = small.reshape(n_seq, n_uly, n_blk, SMALL, 128)
     flat = small[:, :, :, :8, :rows].transpose(3, 0, 2, 1, 4).reshape(8, 1, width)
@@ -1291,14 +1421,9 @@
     mine = lambda v: lax.dynamic_slice(v, (0, here * share), (1, share))
     bias_q, bias_v = mine(bias_q), mine(bias_v)
 
-    normed, grad_out = norm_gather(
+    normed, grad_out, grad_all = norm_gather(
         tokens, gain_one, shift_one, by_plane(cotangent), plane, order
     )
-    normed, w_out, fc = lax.optimization_barrier((normed, w_out, fc))
-    out_part = over_blk(w_out)
-    out_part = out_part.reshape(n_uly, n_blk // n_uly, rows, width)
-    out_part = lax.all_to_all(out_part, "uly", split_axis=0, concat_axis=0, tiled=True)
-    out_part = out_part.transpose(1, 0, 2, 3).reshape(share, width)
     fc = over_blk(fc.reshape(plane * rows, ff_share))
     normed = normed.reshape(plane * n_rows, width)
     made = product(normed, qkv)
@@ -1352,9 +1477,12 @@
     first = own_lengths[:, 0:1]
     bounds = jnp.concatenate([first, first + own_lengths[:, 1:2]], axis=1).reshape(-1)
 
-    attended_low, natural, attended, logs, grad_all = attend(
-        bounds, to_heads(made, 3), grad_out, plane, layout
-    )
+    out_part = out_part.reshape(n_uly, n_blk // n_uly * rows, width)
+    attended_low, natural, attended, logs, out_part = attend(
+        bounds, to_heads(made, 3), out_part, layout
+    )
+    out_part = out_part.reshape(n_uly, n_blk // n_uly, rows, width)
+    out_part = out_part.transpose(1, 0, 2, 3).reshape(share, width)
     attended_low = from_heads(attended_low, 1)
     hidden, own_two = hidden_norm(
         attended_low, out_part, tokens, bias_out, gain_two, shift_two, order
@@ -1364,12 +1492,12 @@
     def sum_blk(matrix):
         return lax.psum_scatter(matrix, "blk", scatter_dimension=0, tiled=True)
 
-    grad_w_proj = sum_blk(grad_proj).astype(F32)
-    inner_grad, grad_hidden, branch, sums_two, sums_fc = back_feed(
-        grad_all, slope, proj, fc, hidden, grad_out, gain_two, order
-    )
-    _, grad_heads, grad_w_out, grad_fc = branch_spread(
-        branch, out_part, attended_low, normed_two.reshape(plane * n_rows, width), inner_grad, plane
+    grad_w_proj = sum_blk(grad_proj)
+    grad_fc, grad_hidden, branch, sums_two, sums_fc = back_feed(
+        grad_all, slope, normed_two.reshape(plane * n_rows, width), proj, fc, hidden, grad_out, gain_two, order
+    )
+    _, grad_heads, grad_w_out, chip_sums, own_sum = branch_spread(
+        branch, out_part, attended_low, active, proj, plane
     )
     grad_b_fc = sums_fc[0]
     grad_fc = sum_blk(grad_fc)
@@ -1377,28 +1505,41 @@
     grad_w_out = grad_w_out.reshape(n_uly, n_blk // n_uly * rows, width)
     grad_heads, grad_w_proj = lax.optimization_barrier((grad_heads, grad_w_proj))
     grad_heads = to_heads(grad_heads, 1)
-    backs, result, grad_w_out = attend_back(
+    fused = sharing == held == 1
+    backs, result, grad_w_out, *grads = attend_back(
         bounds,
         grad_heads,
         natural,
         attended,
         logs,
-        active,
-        proj,
+        chip_sums,
+        own_sum,
         hidden,
         bias_proj,
         grad_w_out,
+        normed,
         layout,
         scale,
+        fused,
     )
     backs = from_heads(backs, 3)
+    if fused:
+        grads = grads[0]
+    else:
+        grads = weight_grad(normed, backs, grad_w_out.reshape(n_blk, rows, width))
     grad_bias = jnp.sum(backs.astype(F32), axis=0)
-    grads = weight_grad(normed, backs, grad_w_out.reshape(n_blk, rows, width))
     grads = sum_blk(grads).reshape(plane, rows, 4 * share)
     grad_w_out = grads[:, :, 3 * share :].transpose(1, 0, 2).reshape(rows, width).astype(F32)
     last, grad_fc = lax.optimization_barrier((backs, grad_fc))
-    sums_one, grad_inputs, result = inputs_return(
-        last, qkv, tokens, grad_hidden, gain_one, result, n_blk, order
+    sums_one, grad_inputs, grad_fc = inputs_return(
+        last,
+        qkv,
+        tokens,
+        grad_hidden,
+        gain_one,
+        grad_fc.reshape(plane, rows, ff_share),
+        sizes,
+        order,
     )
 
     def widened(vector):
@@ -1426,16 +1567,12 @@
     end_lanes = -(-used // 1024) * 8
     sums = jnp.pad(sums, ((0, 0),) * 3 + ((0, end_lanes * 128 - used),))
     sums = sums.transpose(0, 2, 1, 3).reshape(plane, n_blk, end_lanes, 128)
-    *grad_qkv, grad_fc, sums = finish(
-        grads,
-        grad_fc.reshape(plane, rows, ff_share),
-        sums,
-        sizes,
-    )
+    *grad_qkv, sums, result = finish(grads, sums, result, sizes)
     grad_qkv = [g.astype(F32) for g in grad_qkv]
     if runs == 1:
         grad_fc = grad_fc.reshape(by_device).transpose(0, 1, 3, 2, 4).reshape(rows, -1)
     grad_fc = grad_fc.astype(F32)
+    grad_w_proj = grad_w_proj.astype(F32)
     sums = sums.reshape(-1)
     each = [sums[i * rows : (i + 1) * rows] for i in range(8)]
     return (

time: 671 us -> 618 us (0.921)
  waiting for transfers between devices: 45.7 us -> 2.18 us
  local copies, waits for them, and re-layouts: 49 us -> 20.2 us
  Pallas kernels: 531 us -> 548 us
    all_gather x4, waiting for transfers between devices: 38 us -> 0.71 us  [over_blk(): return lax.all_gather(matrix, 'blk', axis=0, tiled=True)]
    pallas_call x1, Pallas kernels: 53.3 us -> 90.4 us  [norm_gather(): pl.pallas_call(functools.partial(norm_kernel, order, n_blk), name='norm_g...]
    unnamed x69 -> x15, local copies, waits for them, and re-layouts: 37.1 us -> 3.74 us
    pallas_call x1, Pallas kernels: 44.7 us -> 17.4 us  [attend(): pl.pallas_call(functools.partial(attend_kernel, layout), name='attend', o...]
    pallas_call x3 -> x2, Pallas kernels: 172 us -> 145 us  [the longest x1 93.7 us: inputs_return(): pl.pallas_call(functools.partial(inputs_kernel, sizes, order), name='inpu...]
    pallas_call x1, Pallas kernels: 30.6 us -> 47.4 us  [enter(): pl.pallas_call(functools.partial(entry_kernel, sizes), name='enter', out_...]
    pallas_call x1, Pallas kernels: 51.6 us -> 63.5 us  [feed(): pl.pallas_call(feed_kernel, name='feed', out_shape=(jax.ShapeDtypeStruct(...]
    reduce_scatter x3, waiting for transfers between devices: 6.93 us -> 0.02 us  [sum_blk(): return lax.psum_scatter(matrix, 'blk', scatter_dimension=0, tiled=True)]
  transfers between devices with their start and end apart: 8 -> 7, of which waited for: 4 -> 1; matrix products, arithmetic and copies ran while one was open for 3% -> 5% of each run, Pallas kernels for 72% -> 86%
where the time goes in v5:
time: 618 us; the launch traced here: 607 us
  Pallas kernels  548 us (89%)
  local copies, waits for them, and re-layouts  20.2 us (3%)
  between operations  14.7 us (2%)
  matrix products  11.2 us (2%)
  other arithmetic  9.64 us (2%)
    pallas_call x1, Pallas kernels, inputs_return(): pl.pallas_call(functools.partial(inputs_kernel, sizes, order), name='inpu...  93.7 us
    pallas_call x1, Pallas kernels, norm_gather(): pl.pallas_call(functools.partial(norm_kernel, order, n_blk), name='norm_g...  90.4 us
    pallas_call x1, Pallas kernels, feed(): pl.pallas_call(feed_kernel, name='feed', out_shape=(jax.ShapeDtypeStruct(...  63.5 us
    pallas_call x1, Pallas kernels, back_feed(): pl.pallas_call(functools.partial(back_feed_kernel, order), name='back_fee...  60.9 us
    pallas_call x1, Pallas kernels, attend_back(): pl.pallas_call(functools.partial(attend_back_kernel, layout, scale, fused...  51.2 us
    pallas_call x1, Pallas kernels, branch_spread(): pl.pallas_call(branch_kernel, name='branch_spread', out_shape=(jax.ShapeD...  49.5 us
    pallas_call x1, Pallas kernels, hidden_norm(): pl.pallas_call(functools.partial(hidden_kernel, order), name='hidden_norm...  48 us
    pallas_call x1, Pallas kernels, enter(): pl.pallas_call(functools.partial(entry_kernel, sizes), name='enter', out_...  47.4 us
  transfers between devices with their start and end apart: 7, of which 1 were waited for; matrix products, arithmetic and copies ran while one was open for 5% of the time, Pallas kernels for 86%

profile of v5, /device:TPU:8, one launch (start us, length us, event | category | flops | bytes accessed | tf_op | source)
XLA Modules:
  0.0 606.6 jit_solution(6902891743160250313)
XLA Ops:
  7.2 0.7 all-gather.5.cloned.1.call-update
  8.0 1.2 reshape.207.refs_8_
  9.2 1.3 reshape_reshape.3.refs_9_
  10.5 47.4 %enter.1 = (bf16[4,64,2048]{2,1,0:T(8,128)(2,1)}, bf16[8,64,768]{2,1,0:T(8,128)(2,1)}, bf16[8,64,1024]{2,1,0:T(8,128)(2,1)}, f32[8,4,16,128]{3,2,1,0:T(8,128)}) custom-call(bf16[4,64,2048]{2,1,0:T(8,128)(2,1)} %x_ref.1, bf16[64,2048]{1,0:T(8,128)(2,1)} %wq_ref.1, bf16[64,2048]{1,0:T(8,128)(2,1)} %wk_ref.1, bf16[64,2048]{1,0:T(8,128)(2,1)} %wv_ref.1, ...), custom_call_target="tpu_custom_call" | custom-call | bytes 1048576 | tf_op jit(solution)/shard_map/enter/pallas_call | solution.py:495
  58.0 0.7 all-gather.9.cloned.1.call-update
  58.7 0.9 slice.139
  59.6 0.1 copy.59
  59.7 0.1 squeeze.27
  59.9 0.7 squeeze.25.gain
  60.6 0.7 squeeze.26.shift
  61.4 90.4 %norm_gather.1 = (bf16[8,256,2048]{2,1,0:T(8,128)(2,1)}, bf16[256,2048]{1,0:T(8,128)(2,1)}, bf16[8,256,2048]{2,1,0:T(8,128)(2,1)}) custom-call(bf16[256,2048]{1,0:T(8,128)(2,1)} %bitcast.42, f32[1,2048]{1,0:T(1,128)} %squeeze.25.gain, f32[1,2048]{1,0:T(1,128)} %squeeze.26.shift, bf16[4,64,2048]{2,1,0:T(8,128)(2,1)} %cot_ref.1), custom_call_target="tpu_custom_call" | custom-call | bytes 1048576 | tf_op jit(solution)/shard_map/norm_gather/pallas_call | solution.py:548
  151.9 11.2 %multiply_convert_fusion.qkv = bf16[2048,768]{1,0:T(8,128)(2,1)} fusion(f32[768]{0:T(1024)S(1)} %broadcast_in_dim.15, f32[768]{0:T(1024)S(1)} %fusion.1, bf16[2048,2048]{1,0:T(8,128)(2,1)} %bitcast.46, bf16[2048,768]{1,0:T(8,128)(2,1)} %all-gather.7.cloned.1.call-done.weight), kind=kOutput, calls=%fused_computation.2 | convolution fusion | flops 6447169536 | bytes 14686208 | tf_op jit(solution)/shard_map/dot_general | solution.py:32
  163.2 0.7 slice.138
  164.0 0.6 gather_fusion
  164.7 0.6 reshape.209.bounds
  165.3 0.7 squeeze.30.gain
  166.0 0.7 squeeze.29.bias
  166.7 0.7 squeeze.31.shift
  167.4 1.3 constant_dynamic-slice_fusion
  168.7 17.4 %attend.1 = (bf16[2048,256]{1,0:T(8,128)(2,1)}, bf16[3,4,1024,128]{3,2,1,0:T(8,128)(2,1)}, f32[4,1024,128]{2,1,0:T(8,128)}, f32[4,8,1024]{2,1,0:T(8,128)}, bf16[4,64,2048]{2,1,0:T(8,128)(2,1)}) custom-call(s32[4]{0:T(128)} %reshape.209.bounds, bf16[2048,768]{1,0:T(8,128)(2,1)} %multiply_convert_fusion.qkv, bf16[4,64,2048]{2,1,0:T(8,128)(2,1)} %bitcast.50), custom_call_target="tpu_custom_call" | custom-call | bytes 1048576 | tf_op jit(solution)/shard_map/attend/pallas_call | solution.py:634
  186.1 48.0 %hidden_norm.1 = (f32[256,2048]{1,0:T(8,128)}, bf16[256,2048]{1,0:T(8,128)(2,1)}) custom-call(bf16[2048,256]{1,0:T(8,128)(2,1)} %get-tuple-element.71.act.low, bf16[256,2048]{1,0:T(8,128)(2,1)} %bitcast.48, bf16[256,2048]{1,0:T(8,128)(2,1)} %bitcast.43, f32[1,2048]{1,0:T(1,128)} %squeeze.29.bias, f32[1,2048]{1,0:T(1,128)} %squeeze.30.gain, ...), custom_call_target="tpu_custom_call" | custom-call | bytes 1048576 | tf_op jit(solution)/shard_map/hidden_norm/pallas_call | solution.py:838
  234.1 63.5 %feed.1 = (bf16[8,256,2048]{2,1,0:T(8,128)(2,1)}, bf16[2048,1024]{1,0:T(8,128)(2,1)}, bf16[2048,1024]{1,0:T(8,128)(2,1)}, bf16[1024,2048]{1,0:T(8,128)(2,1)}) custom-call(bf16[256,2048]{1,0:T(8,128)(2,1)} %get-tuple-element.73.own, bf16[2048,1024]{1,0:T(8,128)(2,1)} %all-gather.9.cloned.1.call-done.weight_ref.weight, f32[1,1024]{1,0:T(1,128)} %bitcast.60, ...), custom_call_target="tpu_custom_call" | custom-call | bytes 1048576 | tf_op jit(solution)/shard_map/feed/pallas_call | solution.py:966
  297.6 0.6 all-gather.11.cloned.1.call-done.proj.proj_ref
  298.3 60.9 %back_feed.1 = (bf16[2048,1024]{1,0:T(8,128)(2,1)}, f32[256,2048]{1,0:T(8,128)}, bf16[256,2048]{1,0:T(8,128)(2,1)}, f32[8,2048]{1,0:T(8,128)}, f32[8,1024]{1,0:T(8,128)}) custom-call(bf16[8,256,2048]{2,1,0:T(8,128)(2,1)} %get-tuple-element.66.cots, bf16[2048,1024]{1,0:T(8,128)(2,1)} %get-tuple-element.75.slope, bf16[2048,2048]{1,0:T(8,128)(2,1)} %bitcast.45, ...), custom_call_target="tpu_custom_call" | custom-call | bytes 1048576 | tf_op jit(solution)/shard_map/back_feed/pallas_call | solution.py:1075
  359.3 0.7 squeeze.32.bias
  360.0 49.5 %branch_spread.1 = (bf16[8,256,2048]{2,1,0:T(8,128)(2,1)}, bf16[2048,256]{1,0:T(8,128)(2,1)}, bf16[256,2048]{1,0:T(8,128)(2,1)}, bf16[3,256,2048]{2,1,0:T(8,128)(2,1)}, f32[256,2048]{1,0:T(8,128)}) custom-call(bf16[256,2048]{1,0:T(8,128)(2,1)} %get-tuple-element.80.own, bf16[256,2048]{1,0:T(8,128)(2,1)} %bitcast.49, ...), custom_call_target="tpu_custom_call" | custom-call | bytes 1048576 | tf_op jit(solution)/shard_map/branch_spread/pallas_call | solution.py:1154
  409.5 51.2 %attend_back.1 = (bf16[2048,768]{1,0:T(8,128)(2,1)}, bf16[256,2048]{1,0:T(8,128)(2,1)}, bf16[16,128]{1,0:T(8,128)(2,1)}, bf16[2048,1024]{1,0:T(8,128)(2,1)}) custom-call(s32[4]{0:T(128)} %reshape.209.bounds, bf16[2048,256]{1,0:T(8,128)(2,1)} %get-tuple-element.84.grad, bf16[3,4,1024,128]{3,2,1,0:T(8,128)(2,1)} %get-tuple-element.85.natural, ...), custom_call_target="tpu_custom_call" | custom-call | bytes 1048576 | tf_op jit(solution)/shard_map/attend_back/pallas_call | solution.py:756
  460.7 0.9 slice_reduce_fusion.6
  462.2 0.5 copy-done.2
  462.6 0.5 convert_reduce_fusion
  463.2 0.1 slice_dynamic-update-slice_fusion.1
  463.4 0.3 slice_dynamic-update-slice_fusion
  463.8 2.8 convert_element_type.50
  466.6 93.7 %inputs_return.1 = (f32[8,2048]{1,0:T(8,128)}, bf16[4,64,2048]{2,1,0:T(8,128)(2,1)}, bf16[64,8192]{1,0:T(8,128)(2,1)}) custom-call(bf16[2048,768]{1,0:T(8,128)(2,1)} %get-tuple-element.94.act, bf16[2048,768]{1,0:T(8,128)(2,1)} %all-gather.7.cloned.1.call-done.weight, bf16[256,2048]{1,0:T(8,128)(2,1)} %bitcast.44, f32[256,2048]{1,0:T(8,128)} %get-tuple-element.95.grad_hidden, ...), custom_call_target="tpu_custom_call" | custom-call | bytes 1048576 | tf_op jit(solution)/shard_map/inputs_return/pallas_call | solution.py:1222
  560.3 1.0 slice_reduce_fusion.4
  561.4 0.1 concatenate.15
  561.7 2.7 convert_element_type.49
  564.3 1.0 convert_bitcast_fusion
  565.4 1.2 copy-done
  566.6 26.5 %finish.1 = (bf16[64,2048]{1,0:T(8,128)(2,1)S(1)}, bf16[64,2048]{1,0:T(8,128)(2,1)S(1)}, bf16[64,2048]{1,0:T(8,128)(2,1)S(1)}, f32[8,128]{1,0:T(8,128)S(1)}, bf16[4,64,2048]{2,1,0:T(8,128)(2,1)S(1)}) custom-call(bf16[8,64,1024]{2,1,0:T(8,128)(2,1)S(1)} %bitcast.40, f32[8,4,8,128]{3,2,1,0:T(8,128)S(1)} %reshape.221.small_ref, bf16[256,2048]{1,0:T(8,128)(2,1)S(1)} %copy-done.1), custom_call_target="tpu_custom_call" | custom-call | bytes 1048576 | tf_op jit(solution)/shard_map/finish/pallas_call | solution.py:1324
  593.1 0.8 convert_element_type.43
  593.9 0.8 convert_element_type.44
  594.8 0.8 convert_element_type.45
  595.6 0.6 slice_bitcast_fusion
  596.1 0.6 fusion.7
  596.7 0.8 copy.57
  597.6 1.0 copy.65
  598.6 1.0 copy.66
  (65 shorter events, 1.8 us)
Async XLA Ops:
  7.2 54.1 %copy-start.5 = (f32[3]{0:T(128)S(1)}, f32[3]{0:T(128)}, u32[]{:S(2)}) copy-start(f32[3]{0:T(128)} %constant.86) | copy-start | bytes 40
  7.2 54.2 %all-gather.5.cloned.1.call-start = ((), (), s32[]{:S(2)}) async-start(), calls=%async_computation.3 | async-start | bytes 1310720 | tf_op jit(solution)/shard_map/all_gather | solution.py:1406
  7.9 144.0 %all-gather.7.cloned.1.call-start = ((), (), s32[]{:S(2)}) async-start(), calls=%async_computation.4 | async-start | bytes 3932160 | tf_op jit(solution)/shard_map/all_gather | solution.py:1406
  57.9 176.2 %all-gather.9.cloned.1.call-start = ((), (), s32[]{:S(2)}) async-start(), calls=%async_computation.5 | async-start | bytes 5242880 | tf_op jit(solution)/shard_map/all_gather | solution.py:1406
  58.6 239.6 %all-gather.11.cloned.1.call-start = ((), (), s32[]{:S(2)}) async-start(), calls=%async_computation.6 | async-start | bytes 5242880 | tf_op jit(solution)/shard_map/all_gather | solution.py:1406
  163.1 246.4 %reduce-scatter.4.cloned.1.call-start = ((), (), s32[]{:S(2)}) async-start(), calls=%async_computation.7 | async-start | bytes 5242880 | tf_op jit(solution)/shard_map/reduce_scatter | solution.py:1493
  297.6 169.0 %reduce-scatter.8.cloned.1.call-start = ((), (), s32[]{:S(2)}) async-start(), calls=%async_computation.9 | async-start | bytes 5242880 | tf_op jit(solution)/shard_map/reduce_scatter | solution.py:1493
  359.2 205.1 %reduce-scatter.6.cloned.1.call-start = ((), (), s32[]{:S(2)}) async-start(), calls=%async_computation.8 | async-start | bytes 5242880 | tf_op jit(solution)/shard_map/reduce_scatter | solution.py:1493
  460.7 1.0 copy-start.4
  460.7 1.9 copy-start.2
  560.2 5.1 copy-start.1
  565.3 1.2 copy-start
  566.6 32.0 %copy-start.3 = (bf16[4,64,2048]{2,1,0:T(8,128)(2,1)S(1)}, bf16[4,64,2048]{2,1,0:T(8,128)(2,1)}, u32[]{:S(2)}) copy-start(bf16[4,64,2048]{2,1,0:T(8,128)(2,1)} %get-tuple-element.153) | copy-start | bytes 3145732
Sparse Core Ops, SparseCore 0:
  9.6 45.6 all-gather.4
  58.0 78.9 all-gather.6
  138.6 78.8 all-gather.8
  218.9 79.2 all-gather.10
  300.4 77.9 reduce-scatter.3
  380.7 77.2 reduce-scatter.7
  460.9 95.0 reduce-scatter.5

commit v6 on v5

--- a/solution.py
+++ b/solution.py
@@ -1182,7 +1182,9 @@
 
 
 def inputs_kernel(
-    sizes, order, act, weight, tok, grad_hidden, gain, fc_ref, sums, out, fc,
+    sizes, order, act, weight, tok, grad_hidden, gain, fc_ref, sums_two, sums_fc, sums_qkv,
+    small, out, fc, sums, stacked, parts, gathered, partial, arrived,
+    s_send, s_recv, b_send, b_recv, s_local,
     total, to_twin, from_twin, mine, in_x, in_y, c_send, c_recv, own,
     send, recv, local, f_send, f_recv, f_local,
 ):
@@ -1211,11 +1213,53 @@
 
     each_chunk(rows, chunk)
     leaving += return_rows(own, out, n_blk, send, recv, local)
+    width = total.shape[1]
+    share = sums_qkv.shape[1] // 3
+    mine_at = pl.ds(pl.multiple_of(me * share, share), share)
+    stacked[0:2] = sums[0:2]
+    stacked[2:4] = jnp.zeros((2, width), F32)
+    stacked[2:3, mine_at] = sums_qkv[:, :share]
+    stacked[3:4, mine_at] = sums_qkv[:, 2 * share :]
+    stacked[4:5] = sums_two[2:3]
+    stacked[5:7] = sums_two[0:2]
+    stacked[7:8] = sums_two[3:4]
+    parts[...] = jnp.zeros_like(parts)
+    lanes = width // (n_seq * n_blk * n_uly)
+    for s in range(n_seq):
+        for b in range(n_blk):
+            for u in range(n_uly):
+                at = ((s * n_blk + b) * n_uly + u) * lanes
+                parts[s * n_uly + u, b, 0:8, 0:lanes] = stacked[:, at : at + lanes]
+    hidden_rows = sums_fc.shape[1] // n_blk
+    lanes = min(128, hidden_rows)
+    for b in range(n_blk):
+        for i in range(hidden_rows // lanes):
+            at = b * hidden_rows + i * lanes
+            parts[me, b, 8 + i : 9 + i, 0:lanes] = sums_fc[0:1, at : at + lanes]
+    here_blk = lax.axis_index("blk")
+    at_home, to_plane, to_blk = home(s_local), sender(s_send, s_recv), sender(b_send, b_recv)
+    moved = [at_home(0, parts.at[me], gathered.at[me], None)]
+    moved += [
+        to_plane(j, parts.at[p], gathered.at[me], peer) for j, (p, peer) in enumerate(friends)
+    ]
+    for made in moved:
+        made.wait()
+    partial[...] = jnp.sum(gathered[...], axis=0)
+    moved = [at_home(1, partial.at[here_blk], arrived.at[here_blk], None)]
+    moved += [
+        to_blk(j, partial.at[peer[1]], arrived.at[here_blk], peer)
+        for j, peer in enumerate(blk_peers(n_blk))
+    ]
+    for made in moved:
+        made.wait()
+    small[...] = jnp.sum(arrived[...], axis=0)
     for made in leaving:
         made.wait()
 
 
-def inputs_return(act, weight, tok, grad_hidden, gain, fc, sizes, order):
+def inputs_return(
+    act, weight, tok, grad_hidden, gain, fc, sums_two, sums_fc, sums_qkv, sizes, order
+):
     rows, width = tok.shape
     n_blk, runs = sizes[1], sizes[3]
     plane = fc.shape[0]
@@ -1223,13 +1267,24 @@
         functools.partial(inputs_kernel, sizes, order),
         name="inputs_return",
         out_shape=(
-            jax.ShapeDtypeStruct((8, width), F32),
+            jax.ShapeDtypeStruct((SMALL, 128), F32),
             jax.ShapeDtypeStruct((n_blk, rows // n_blk, width), BF),
             jax.ShapeDtypeStruct((fc.shape[1], plane * fc.shape[2]), BF),
         ),
-        in_specs=[VMEM] * 5 + [ANY],
+        in_specs=[VMEM] * 5 + [ANY] + [VMEM] * 3,
         out_specs=(VMEM, ANY, ANY),
-        scratch_shapes=collect_scratch(rows, width)
+        scratch_shapes=[
+            pltpu.VMEM((8, width), F32),
+            pltpu.VMEM((8, width), F32),
+            pltpu.VMEM((plane, n_blk, SMALL, 128), F32),
+            pltpu.VMEM((plane, n_blk, SMALL, 128), F32),
+            pltpu.VMEM((n_blk, SMALL, 128), F32),
+            pltpu.VMEM((n_blk, SMALL, 128), F32),
+        ]
+        + [pltpu.SemaphoreType.DMA((plane - 1,))] * 2
+        + [pltpu.SemaphoreType.DMA((n_blk - 1,))] * 2
+        + [pltpu.SemaphoreType.DMA((2,))]
+        + collect_scratch(rows, width)
         + [pltpu.VMEM((rows, width), BF)]
         + [pltpu.SemaphoreType.DMA((n_blk - 1,))] * 2
         + [pltpu.SemaphoreType.DMA]
@@ -1239,7 +1294,7 @@
             collective_id=6, has_side_effects=True, vmem_limit_bytes=GRANT
         ),
         cost_estimate=pl.CostEstimate(flops=0, bytes_accessed=MIB, transcendentals=0),
-    )(act, weight, tok, grad_hidden, gain, fc)
+    )(act, weight, tok, grad_hidden, gain, fc, sums_two, sums_fc, sums_qkv)
 
 
 def weight_terms(left, right, mixed, out):
@@ -1275,73 +1330,42 @@
 
 
 def end_kernel(
-    sizes, qkv_ref, small_ref, result_ref, gq, gk, gv, small, result,
-    gathered, partial, arrived,
-    blk_send, blk_recv, plane_send, plane_recv, local, r_send, r_recv, r_local,
+    sizes, qkv_ref, result_ref, gq, gk, gv, result,
+    plane_send, plane_recv, local, r_send, r_recv, r_local,
 ):
     n_seq, n_blk, n_uly, _ = sizes
-    (s, b, u), _, _, _ = place()
-    plane = n_seq * n_uly
-    me, friends = plane_peers(plane)
-    column = blk_peers(n_blk)
-    meet([peer for _, peer in friends] + column)
-    by_blk = sender(blk_send, blk_recv)
-    by_plane = sender(plane_send, plane_recv)
-    at_home = home(local)
+    me, friends = plane_peers(n_seq * n_uly)
+    meet([peer for _, peer in friends] + blk_peers(n_blk))
     spans = projection_spans((gq, gk, gv), qkv_ref, me, sizes)
-    first = at_home(0, small_ref.at[me], gathered.at[me], None)
-    vectors = [
-        by_plane(3 * (plane - 1) + j, small_ref.at[p], gathered.at[me], peer)
-        for j, (p, peer) in enumerate(friends)
-    ]
     started = return_rows(result_ref, result, n_blk, r_send, r_recv, r_local)
     for j, (p, peer) in enumerate(friends):
-        started += return_columns(by_plane, 3 * j, spans, p, peer)
-    started += return_columns(at_home, 2, spans, me, None)
-    first.wait()
-    for made in vectors:
-        made.wait()
-    partial[...] = jnp.sum(gathered[...], axis=0)
-    sent = [at_home(1, partial.at[b], arrived.at[b], None)]
-    sent += [
-        by_blk(j, partial.at[peer[1]], arrived.at[b], peer) for j, peer in enumerate(column)
-    ]
-    for made in sent:
-        made.wait()
-    small[...] = jnp.sum(arrived[...], axis=0)
+        started += return_columns(sender(plane_send, plane_recv), 3 * j, spans, p, peer)
+    started += return_columns(home(local), 0, spans, me, None)
     for made in started:
         made.wait()
 
 
-def finish(qkv, small, result, sizes):
+def finish(qkv, result, sizes):
     n_seq, n_blk, n_uly, _ = sizes
     plane = n_seq * n_uly
     rows, share = qkv.shape[1], qkv.shape[2] // 4
-    tail = small.shape[2:]
     whole = jax.ShapeDtypeStruct((rows, plane * share), BF)
     back = jax.ShapeDtypeStruct((n_blk, result.shape[0] // n_blk, result.shape[1]), BF)
-    blk_sems = [pltpu.SemaphoreType.DMA((n_blk - 1,))] * 2
     return pl.pallas_call(
         functools.partial(end_kernel, sizes),
         name="finish",
-        out_shape=(whole, whole, whole, jax.ShapeDtypeStruct(tail, small.dtype), back),
-        in_specs=[ANY] * 3,
-        out_specs=(ANY, ANY, ANY, VMEM, ANY),
-        scratch_shapes=[
-            pltpu.VMEM((plane, n_blk) + tail, F32),
-            pltpu.VMEM((n_blk,) + tail, F32),
-            pltpu.VMEM((n_blk,) + tail, F32),
-        ]
-        + blk_sems
-        + [pltpu.SemaphoreType.DMA((4 * (plane - 1),))] * 2
-        + [pltpu.SemaphoreType.DMA((5,))]
-        + blk_sems
+        out_shape=(whole, whole, whole, back),
+        in_specs=[ANY] * 2,
+        out_specs=(ANY,) * 4,
+        scratch_shapes=[pltpu.SemaphoreType.DMA((3 * (plane - 1),))] * 2
+        + [pltpu.SemaphoreType.DMA((3,))]
+        + [pltpu.SemaphoreType.DMA((n_blk - 1,))] * 2
         + [pltpu.SemaphoreType.DMA],
         compiler_params=pltpu.CompilerParams(
             collective_id=7, has_side_effects=True, vmem_limit_bytes=16 * MIB
         ),
         cost_estimate=pl.CostEstimate(flops=0, bytes_accessed=MIB, transcendentals=0),
-    )(qkv, small, result)
+    )(qkv, result)
 
 
 def on_device(
@@ -1499,7 +1523,6 @@
     _, grad_heads, grad_w_out, chip_sums, own_sum = branch_spread(
         branch, out_part, attended_low, active, proj, plane
     )
-    grad_b_fc = sums_fc[0]
     grad_fc = sum_blk(grad_fc)
     grad_w_out = grad_w_out.reshape(n_blk // n_uly, n_uly, rows, width).transpose(1, 0, 2, 3)
     grad_w_out = grad_w_out.reshape(n_uly, n_blk // n_uly * rows, width)
@@ -1527,54 +1550,36 @@
         grads = grads[0]
     else:
         grads = weight_grad(normed, backs, grad_w_out.reshape(n_blk, rows, width))
-    grad_bias = jnp.sum(backs.astype(F32), axis=0)
+    sums_qkv = jnp.sum(backs.astype(F32), axis=0, keepdims=True)
     grads = sum_blk(grads).reshape(plane, rows, 4 * share)
-    grad_w_out = grads[:, :, 3 * share :].transpose(1, 0, 2).reshape(rows, width).astype(F32)
+    grad_w_out = grads[:, :, 3 * share :].transpose(1, 0, 2).reshape(rows, width)
     last, grad_fc = lax.optimization_barrier((backs, grad_fc))
-    sums_one, grad_inputs, grad_fc = inputs_return(
+    sums, grad_inputs, grad_fc = inputs_return(
         last,
         qkv,
         tokens,
         grad_hidden,
         gain_one,
         grad_fc.reshape(plane, rows, ff_share),
+        sums_two,
+        sums_fc,
+        sums_qkv,
         sizes,
         order,
     )
-
-    def widened(vector):
-        return lax.dynamic_update_slice(jnp.zeros((width,), F32), vector, (here * share,))
-
-    parts = (
-        sums_one[0],
-        sums_one[1],
-        widened(grad_bias[:share]),
-        widened(grad_bias[2 * share :]),
-        sums_two[2],
-        sums_two[0],
-        sums_two[1],
-        sums_two[3],
+    *grad_qkv, result = finish(grads, result, sizes)
+    grad_w_proj, grad_fc, grad_w_out, result = lax.optimization_barrier(
+        (grad_w_proj, grad_fc, grad_w_out, result)
     )
-    wide_fc = lax.dynamic_update_slice(
-        jnp.zeros((n_seq, n_blk, n_uly, hidden_rows), F32),
-        grad_b_fc.reshape(1, n_blk, 1, hidden_rows),
-        (here_seq, 0, here_uly, 0),
-    )
-    sums = jnp.concatenate(
-        [p.reshape(n_seq, n_blk, n_uly, rows) for p in parts] + [wide_fc], axis=3
-    )
-    used = sums.shape[3]
-    end_lanes = -(-used // 1024) * 8
-    sums = jnp.pad(sums, ((0, 0),) * 3 + ((0, end_lanes * 128 - used),))
-    sums = sums.transpose(0, 2, 1, 3).reshape(plane, n_blk, end_lanes, 128)
-    *grad_qkv, sums, result = finish(grads, sums, result, sizes)
+    grad_w_out = grad_w_out.astype(F32)
     grad_qkv = [g.astype(F32) for g in grad_qkv]
     if runs == 1:
         grad_fc = grad_fc.reshape(by_device).transpose(0, 1, 3, 2, 4).reshape(rows, -1)
     grad_fc = grad_fc.astype(F32)
     grad_w_proj = grad_w_proj.astype(F32)
-    sums = sums.reshape(-1)
-    each = [sums[i * rows : (i + 1) * rows] for i in range(8)]
+    each = [sums[i, :rows] for i in range(8)]
+    lanes = min(128, hidden_rows)
+    grad_b_fc = sums[8 : 8 + hidden_rows // lanes, :lanes].reshape(-1)
     return (
         from_plane(result),
         from_plane(grad_inputs),
@@ -1590,7 +1595,7 @@
         each[5],
         each[6],
         grad_fc,
-        sums[8 * rows : used],
+        grad_b_fc,
         grad_w_proj,
         each[7],
     )

time: 618 us -> 617 us (level)
  transfers between devices with their start and end apart: 7 -> 7, of which waited for: 1 -> 1; matrix products, arithmetic and copies ran while one was open for 5% -> 4% of each run, Pallas kernels for 86% -> 86%
where the time goes in v6:
time: 617 us; the launch traced here: 608 us
  Pallas kernels  552 us (89%)
  local copies, waits for them, and re-layouts  20.5 us (3%)
  between operations  14.6 us (2%)
  matrix products  11.2 us (2%)
  other arithmetic  7.04 us (1%)
    pallas_call x1, Pallas kernels, inputs_return(): pl.pallas_call(functools.partial(inputs_kernel, sizes, order), name='inpu...  97.5 us
    pallas_call x1, Pallas kernels, norm_gather(): pl.pallas_call(functools.partial(norm_kernel, order, n_blk), name='norm_g...  90.4 us
    pallas_call x1, Pallas kernels, feed(): pl.pallas_call(feed_kernel, name='feed', out_shape=(jax.ShapeDtypeStruct(...  63.5 us
    pallas_call x1, Pallas kernels, back_feed(): pl.pallas_call(functools.partial(back_feed_kernel, order), name='back_fee...  61 us
    pallas_call x1, Pallas kernels, attend_back(): pl.pallas_call(functools.partial(attend_back_kernel, layout, scale, fused...  51.1 us
    pallas_call x1, Pallas kernels, branch_spread(): pl.pallas_call(branch_kernel, name='branch_spread', out_shape=(jax.ShapeD...  49.4 us
    pallas_call x1, Pallas kernels, hidden_norm(): pl.pallas_call(functools.partial(hidden_kernel, order), name='hidden_norm...  47.9 us
    pallas_call x1, Pallas kernels, enter(): pl.pallas_call(functools.partial(entry_kernel, sizes), name='enter', out_...  47.4 us
  transfers between devices with their start and end apart: 7, of which 1 were waited for; matrix products, arithmetic and copies ran while one was open for 4% of the time, Pallas kernels for 86%

profile of v6, /device:TPU:8, one launch (start us, length us, event | category | flops | bytes accessed | tf_op | source)
XLA Modules:
  0.0 608.2 jit_solution(3378854181541094603)
XLA Ops:
  7.2 0.7 all-gather.5.cloned.1.call-update
  8.0 1.3 reshape_reshape.3.refs_9_
  9.3 1.2 reshape.197.refs_8_
  10.5 47.4 %enter.1 = (bf16[4,64,2048]{2,1,0:T(8,128)(2,1)}, bf16[8,64,768]{2,1,0:T(8,128)(2,1)}, bf16[8,64,1024]{2,1,0:T(8,128)(2,1)}, f32[8,4,16,128]{3,2,1,0:T(8,128)}) custom-call(bf16[4,64,2048]{2,1,0:T(8,128)(2,1)} %x_ref.1, bf16[64,2048]{1,0:T(8,128)(2,1)} %wq_ref.1, bf16[64,2048]{1,0:T(8,128)(2,1)} %wk_ref.1, bf16[64,2048]{1,0:T(8,128)(2,1)} %wv_ref.1, ...), custom_call_target="tpu_custom_call" | custom-call | bytes 1048576 | tf_op jit(solution)/shard_map/enter/pallas_call | solution.py:495
  58.0 0.7 all-gather.9.cloned.1.call-update
  58.8 0.9 slice.98
  59.7 0.1 copy.45
  59.8 0.7 squeeze.49.gain
  60.5 0.1 squeeze.52
  60.6 0.1 squeeze.51
  60.7 0.7 squeeze.50.shift
  61.4 90.4 %norm_gather.1 = (bf16[8,256,2048]{2,1,0:T(8,128)(2,1)}, bf16[256,2048]{1,0:T(8,128)(2,1)}, bf16[8,256,2048]{2,1,0:T(8,128)(2,1)}) custom-call(bf16[256,2048]{1,0:T(8,128)(2,1)} %bitcast.54, f32[1,2048]{1,0:T(1,128)} %squeeze.49.gain, f32[1,2048]{1,0:T(1,128)} %squeeze.50.shift, bf16[4,64,2048]{2,1,0:T(8,128)(2,1)} %cot_ref.1), custom_call_target="tpu_custom_call" | custom-call | bytes 1048576 | tf_op jit(solution)/shard_map/norm_gather/pallas_call | solution.py:548
  151.9 11.2 %multiply_convert_fusion.qkv = bf16[2048,768]{1,0:T(8,128)(2,1)} fusion(f32[768]{0:T(1024)S(1)} %broadcast_in_dim.15, f32[768]{0:T(1024)S(1)} %fusion.1, bf16[2048,2048]{1,0:T(8,128)(2,1)} %bitcast.58, bf16[2048,768]{1,0:T(8,128)(2,1)} %all-gather.7.cloned.1.call-done.weight), kind=kOutput, calls=%fused_computation.2 | convolution fusion | flops 6447169536 | bytes 14686208 | tf_op jit(solution)/shard_map/dot_general | solution.py:32
  163.2 0.7 slice.101
  163.9 0.1 convert_element_type.32
  164.0 0.6 gather_fusion
  164.6 0.1 fusion.7
  164.6 0.1 pad_add_fusion
  164.7 0.6 reshape.200.bounds
  165.3 0.7 squeeze.54.gain
  166.0 0.7 squeeze.55.shift
  166.7 0.7 squeeze.53.bias
  167.4 1.3 constant_dynamic-slice_fusion
  168.7 17.4 %attend.1 = (bf16[2048,256]{1,0:T(8,128)(2,1)}, bf16[3,4,1024,128]{3,2,1,0:T(8,128)(2,1)}, f32[4,1024,128]{2,1,0:T(8,128)}, f32[4,8,1024]{2,1,0:T(8,128)}, bf16[4,64,2048]{2,1,0:T(8,128)(2,1)}) custom-call(s32[4]{0:T(128)} %reshape.200.bounds, bf16[2048,768]{1,0:T(8,128)(2,1)} %multiply_convert_fusion.qkv, bf16[4,64,2048]{2,1,0:T(8,128)(2,1)} %bitcast.62), custom_call_target="tpu_custom_call" | custom-call | bytes 1048576 | tf_op jit(solution)/shard_map/attend/pallas_call | solution.py:634
  186.1 47.9 %hidden_norm.1 = (f32[256,2048]{1,0:T(8,128)}, bf16[256,2048]{1,0:T(8,128)(2,1)}) custom-call(bf16[2048,256]{1,0:T(8,128)(2,1)} %get-tuple-element.74.act.low, bf16[256,2048]{1,0:T(8,128)(2,1)} %bitcast.60, bf16[256,2048]{1,0:T(8,128)(2,1)} %bitcast.55, f32[1,2048]{1,0:T(1,128)} %squeeze.53.bias, f32[1,2048]{1,0:T(1,128)} %squeeze.54.gain, ...), custom_call_target="tpu_custom_call" | custom-call | bytes 1048576 | tf_op jit(solution)/shard_map/hidden_norm/pallas_call | solution.py:838
  234.0 63.5 %feed.1 = (bf16[8,256,2048]{2,1,0:T(8,128)(2,1)}, bf16[2048,1024]{1,0:T(8,128)(2,1)}, bf16[2048,1024]{1,0:T(8,128)(2,1)}, bf16[1024,2048]{1,0:T(8,128)(2,1)}) custom-call(bf16[256,2048]{1,0:T(8,128)(2,1)} %get-tuple-element.76.own, bf16[2048,1024]{1,0:T(8,128)(2,1)} %all-gather.9.cloned.1.call-done.weight_ref.weight, f32[1,1024]{1,0:T(1,128)} %bitcast.72, ...), custom_call_target="tpu_custom_call" | custom-call | bytes 1048576 | tf_op jit(solution)/shard_map/feed/pallas_call | solution.py:966
  297.5 0.7 all-gather.11.cloned.1.call-done.proj.proj_ref
  298.2 61.0 %back_feed.1 = (bf16[2048,1024]{1,0:T(8,128)(2,1)}, f32[256,2048]{1,0:T(8,128)}, bf16[256,2048]{1,0:T(8,128)(2,1)}, f32[8,2048]{1,0:T(8,128)}, f32[8,1024]{1,0:T(8,128)}) custom-call(bf16[8,256,2048]{2,1,0:T(8,128)(2,1)} %get-tuple-element.69.cots, bf16[2048,1024]{1,0:T(8,128)(2,1)} %get-tuple-element.78.slope, bf16[2048,2048]{1,0:T(8,128)(2,1)} %bitcast.57, ...), custom_call_target="tpu_custom_call" | custom-call | bytes 1048576 | tf_op jit(solution)/shard_map/back_feed/pallas_call | solution.py:1075
  359.3 0.7 squeeze.56.bias
  360.0 49.4 %branch_spread.1 = (bf16[8,256,2048]{2,1,0:T(8,128)(2,1)}, bf16[2048,256]{1,0:T(8,128)(2,1)}, bf16[256,2048]{1,0:T(8,128)(2,1)}, bf16[3,256,2048]{2,1,0:T(8,128)(2,1)}, f32[256,2048]{1,0:T(8,128)}) custom-call(bf16[256,2048]{1,0:T(8,128)(2,1)} %get-tuple-element.83.own, bf16[256,2048]{1,0:T(8,128)(2,1)} %bitcast.61, ...), custom_call_target="tpu_custom_call" | custom-call | bytes 1048576 | tf_op jit(solution)/shard_map/branch_spread/pallas_call | solution.py:1154
  409.4 51.1 %attend_back.1 = (bf16[2048,768]{1,0:T(8,128)(2,1)}, bf16[256,2048]{1,0:T(8,128)(2,1)}, bf16[16,128]{1,0:T(8,128)(2,1)}, bf16[2048,1024]{1,0:T(8,128)(2,1)}) custom-call(s32[4]{0:T(128)} %reshape.200.bounds, bf16[2048,256]{1,0:T(8,128)(2,1)} %get-tuple-element.88.grad, bf16[3,4,1024,128]{3,2,1,0:T(8,128)(2,1)} %get-tuple-element.89.natural, ...), custom_call_target="tpu_custom_call" | custom-call | bytes 1048576 | tf_op jit(solution)/shard_map/attend_back/pallas_call | solution.py:756
  460.6 1.9 copy-done.2
  462.5 0.5 convert_reduce_fusion
  463.0 0.6 broadcast_in_dim.16.sums_qkv
  463.6 97.5 %inputs_return.1 = (f32[16,128]{1,0:T(8,128)}, bf16[4,64,2048]{2,1,0:T(8,128)(2,1)}, bf16[64,8192]{1,0:T(8,128)(2,1)}) custom-call(bf16[2048,768]{1,0:T(8,128)(2,1)} %get-tuple-element.97.act, bf16[2048,768]{1,0:T(8,128)(2,1)} %all-gather.7.cloned.1.call-done.weight, bf16[256,2048]{1,0:T(8,128)(2,1)} %bitcast.56, f32[256,2048]{1,0:T(8,128)} %get-tuple-element.98.grad_hidden, ...), custom_call_target="tpu_custom_call" | custom-call | bytes 1048576 | tf_op jit(solution)/shard_map/inputs_return/pallas_call | solution.py:1266
  561.0 1.2 slice_bitcast_fusion.1
  562.3 1.5 slice_bitcast_fusion.2
  563.8 1.0 slice_bitcast_fusion
  564.8 1.2 copy-done
  566.0 26.8 %finish.1 = (bf16[64,2048]{1,0:T(8,128)(2,1)S(1)}, bf16[64,2048]{1,0:T(8,128)(2,1)S(1)}, bf16[64,2048]{1,0:T(8,128)(2,1)S(1)}, bf16[4,64,2048]{2,1,0:T(8,128)(2,1)S(1)}) custom-call(bf16[8,64,1024]{2,1,0:T(8,128)(2,1)S(1)} %bitcast.53, bf16[256,2048]{1,0:T(8,128)(2,1)S(1)} %copy-done.1), custom_call_target="tpu_custom_call" | custom-call | bytes 1048576 | tf_op jit(solution)/shard_map/finish/pallas_call | solution.py:1354
  592.9 0.8 convert_element_type.38
  593.7 0.8 convert_element_type.35
  594.5 0.8 convert_element_type.36
  595.3 0.8 convert_element_type.37
  596.2 1.5 convert_element_type.39
  597.6 1.6 convert_element_type.40
  599.2 1.0 copy.48
  600.2 1.0 copy.49
  (40 shorter events, 0.7 us)
Async XLA Ops:
  7.2 51.5 %copy-start.6 = (f32[3]{0:T(128)S(1)}, f32[3]{0:T(128)}, u32[]{:S(2)}) copy-start(f32[3]{0:T(128)} %constant.81) | copy-start | bytes 40
  7.2 54.2 %all-gather.5.cloned.1.call-start = ((), (), s32[]{:S(2)}) async-start(), calls=%async_computation.3 | async-start | bytes 1310720 | tf_op jit(solution)/shard_map/all_gather | solution.py:1430
  7.9 144.0 %all-gather.7.cloned.1.call-start = ((), (), s32[]{:S(2)}) async-start(), calls=%async_computation.4 | async-start | bytes 3932160 | tf_op jit(solution)/shard_map/all_gather | solution.py:1430
  57.9 176.0 %all-gather.9.cloned.1.call-start = ((), (), s32[]{:S(2)}) async-start(), calls=%async_computation.5 | async-start | bytes 5242880 | tf_op jit(solution)/shard_map/all_gather | solution.py:1430
  58.6 239.6 %all-gather.11.cloned.1.call-start = ((), (), s32[]{:S(2)}) async-start(), calls=%async_computation.6 | async-start | bytes 5242880 | tf_op jit(solution)/shard_map/all_gather | solution.py:1430
  163.1 246.3 %reduce-scatter.4.cloned.1.call-start = ((), (), s32[]{:S(2)}) async-start(), calls=%async_computation.7 | async-start | bytes 5242880 | tf_op jit(solution)/shard_map/reduce_scatter | solution.py:1517
  297.5 166.1 %reduce-scatter.6.cloned.1.call-start = ((), (), s32[]{:S(2)}) async-start(), calls=%async_computation.8 | async-start | bytes 5242880 | tf_op jit(solution)/shard_map/reduce_scatter | solution.py:1517
  359.2 204.6 %reduce-scatter.8.cloned.1.call-start = ((), (), s32[]{:S(2)}) async-start(), calls=%async_computation.9 | async-start | bytes 5242880 | tf_op jit(solution)/shard_map/reduce_scatter | solution.py:1517
  460.6 1.9 copy-start.2
  463.6 101.2 %copy-start.1 = (bf16[256,2048]{1,0:T(8,128)(2,1)S(1)}, bf16[256,2048]{1,0:T(8,128)(2,1)}, u32[]{:S(2)}) copy-start(bf16[256,2048]{1,0:T(8,128)(2,1)} %get-tuple-element.104.result_ref) | copy-start | bytes 3145732
  564.8 1.2 copy-start
  566.0 30.1 %copy-start.4 = (bf16[64,8192]{1,0:T(8,128)(2,1)S(1)}, bf16[64,8192]{1,0:T(8,128)(2,1)}, u32[]{:S(2)}) copy-start(bf16[64,8192]{1,0:T(8,128)(2,1)} %get-tuple-element.113) | copy-start | bytes 3145732
  566.0 31.6 %copy-start.3 = (bf16[256,2048]{1,0:T(8,128)(2,1)S(1)}, bf16[256,2048]{1,0:T(8,128)(2,1)}, u32[]{:S(2)}) copy-start(bf16[256,2048]{1,0:T(8,128)(2,1)} %reduce-scatter.4.cloned.1.call-done) | copy-start | bytes 3145732
  596.2 4.0 copy-start.5
Sparse Core Ops, SparseCore 0:
  9.6 45.6 all-gather.4
  58.0 78.9 all-gather.6
  138.6 78.8 all-gather.8
  218.9 79.2 all-gather.10
  300.4 77.9 reduce-scatter.3
  380.7 77.2 reduce-scatter.5
  460.7 97.0 reduce-scatter.7
